TPU v7x, 32 devices: a whole 2x2x4 slice. The times are simulated.
32 devices in a mesh: dp: 4 (over x, core), ctx: 8 (over z, y).
Axes of the slice: x: 2, y: 2, z: 4, core: 2. Of those that a mesh axis runs over, the one named last changes fastest.
Arguments:
- queries: bfloat16 [4, 256, 2048], P('dp', 'ctx'), may hold values from -8 to 8
- keys: bfloat16 [4, 256, 512], P('dp', 'ctx'), may hold values from -8 to 8
- values: bfloat16 [4, 256, 512], P('dp', 'ctx'), may hold values from -6 to 6
- out_grad: bfloat16 [4, 256, 2048], P('dp', 'ctx'), may hold values from -6 to 6
- routed_inputs: bfloat16 [4, 256, 4096], P('dp', 'ctx'), may hold values from -6 to 6
- router_weight: float32 [4096], replicated, may hold values from -0.09375 to 0.09375
- positions: int32 [4, 256], P('dp', 'ctx'), may hold values from 0 to 2047, as said below
Outputs:
- query_grad: bfloat16 [4, 256, 2048], P('dp', 'ctx')
- key_grad: bfloat16 [4, 256, 512], P('dp', 'ctx')
- value_grad: bfloat16 [4, 256, 512], P('dp', 'ctx')
- router_grad: float32 [4096], replicated
Inputs may be any that keep to these rules, and one draw needn't show every extreme that they name: `positions`: within each sequence strictly increasing, the first 0 and the last 2047.
All inputs are finite; a program needn't handle non-finite values.
Results may differ from a plain program's by a relative error of at most 0.039.
Values may be sent and summed in bfloat16 or wider, within the bound.
No kernel may reach another device: no remote copies, remote signals or barrier semaphores. Data moves between devices by JAX's collectives and lax.ppermute only.
A program may use at most 128 MiB of HBM per device.

v0:
```python
import math

import jax
import jax.numpy as jnp
from jax import lax
from jax.sharding import PartitionSpec as P

HQ = 16
KVH = 4
HD = 128


ROPE_BASE = 500000.0
NEG_LARGE = -1e30


def rope_tables(pair_count):
    frequency = [ROPE_BASE ** (-number / pair_count) for number in range(pair_count)]
    coarse = [256.0 * factor % (2.0 * math.pi) for factor in frequency]
    return (jnp.asarray(frequency, jnp.float32), jnp.asarray(coarse, jnp.float32))


def rotation(positions, head_dim):
    frequency, coarse = rope_tables(head_dim // 2)
    upper_part = (positions // 256).astype(jnp.float32)
    lower_part = (positions % 256).astype(jnp.float32)
    angles = upper_part[:, None] * coarse[None, :] + lower_part[:, None] * frequency[None, :]
    return (jnp.cos(angles)[:, None, :], jnp.sin(angles)[:, None, :])


def turn_forward(vectors, cosine, sine):
    width_half = vectors.shape[-1] // 2
    first_half = vectors[..., :width_half]
    second_half = vectors[..., width_half:]
    return jnp.concatenate(
        [first_half * cosine - second_half * sine, second_half * cosine + first_half * sine],
        axis=-1,
    )


def turn_back(vectors, cosine, sine):
    width_half = vectors.shape[-1] // 2
    first_half = vectors[..., :width_half]
    second_half = vectors[..., width_half:]
    return jnp.concatenate(
        [first_half * cosine + second_half * sine, second_half * cosine - first_half * sine],
        axis=-1,
    )


def unchanged(state):
    return state


def shards(queries, keys, values, out_grad, routed_inputs, router_weight, positions):
    slots = queries.shape[1]
    half_rows = slots // 2
    group_size = HQ // KVH
    score_scale = 1.0 / math.sqrt(HD)
    own_places = positions[0]
    cosine, sine = rotation(own_places, HD)
    key_rot = turn_forward(keys[0].astype(jnp.float32).reshape(slots, KVH, HD), cosine, sine)
    key_rot = key_rot.astype(jnp.bfloat16).reshape(slots, KVH * HD)
    key_all, value_all, place_all = (
        lax.all_gather(key_rot, "ctx", axis=0, tiled=True),
        lax.all_gather(values[0], "ctx", axis=0, tiled=True),
        lax.all_gather(own_places, "ctx", axis=0, tiled=True),
    )
    input_wide = routed_inputs[0].astype(jnp.float32)
    own_gate = jax.nn.sigmoid(jnp.dot(input_wide, router_weight, precision=lax.Precision.HIGHEST))
    query_rows = queries[0]
    upstream_rows = out_grad[0]
    held_cos, held_sin = rotation(own_places, HD)
    query_rot = turn_forward(
        query_rows.astype(jnp.float32).reshape(slots, HQ, HD), held_cos, held_sin
    )
    query_rot = query_rot.astype(jnp.bfloat16).reshape(2, half_rows, KVH, group_size, HD)
    upstream = upstream_rows.astype(jnp.float32).reshape(2, half_rows, KVH, group_size, HD)
    scaled_grad = (own_gate.reshape(2, half_rows)[:, :, None, None, None] * upstream).astype(
        jnp.bfloat16
    )
    place_half = own_places.reshape(2, half_rows)
    query_top = jnp.max(place_half, axis=1)
    total_keys = key_all.shape[0]

    def key_block(start, count):
        key_tile = lax.dynamic_slice_in_dim(key_all, start, count, 0).reshape(count, KVH, HD)
        value_tile = lax.dynamic_slice_in_dim(value_all, start, count, 0).reshape(count, KVH, HD)
        place_tile = lax.dynamic_slice_in_dim(place_all, start, count, 0)
        return (key_tile, value_tile, place_tile)

    def tile_scores(which, key_tile, place_tile):
        scores = (
            jnp.einsum(
                "tkgd,ukd->kgtu", query_rot[which], key_tile, preferred_element_type=jnp.float32
            )
            * score_scale
        )
        allowed = place_half[which][:, None] >= place_tile[None, :]
        return jnp.where(allowed[None, None], scores, -jnp.inf)

    block_rows = math.gcd(total_keys, 512)
    block_count = total_keys // block_rows

    def stats_step(number, carry):
        top_all, mass_all = carry
        key_tile, value_tile, place_tile = key_block(number * block_rows, block_rows)
        new_top = []
        new_mass = []
        for which in range(2):

            def stats_live(state, which=which):
                top_old, mass_old = state
                scores = tile_scores(which, key_tile, place_tile)
                top_new = jnp.maximum(top_old, jnp.max(scores, axis=-1))
                mass_new = mass_old * jnp.exp(top_old - top_new) + jnp.sum(
                    jnp.exp(scores - top_new[..., None]), axis=-1
                )
                return (top_new, mass_new)

            top_one, mass_one = lax.cond(
                place_tile[0] <= query_top[which],
                stats_live,
                unchanged,
                (top_all[which], mass_all[which]),
            )
            new_top.append(top_one)
            new_mass.append(mass_one)
        return (jnp.stack(new_top), jnp.stack(new_mass))

    stat_shape = (2, KVH, group_size, half_rows)
    top_all, mass_all = lax.fori_loop(
        0,
        block_count,
        stats_step,
        (jnp.full(stat_shape, NEG_LARGE, jnp.float32), jnp.zeros(stat_shape, jnp.float32)),
    )
    lse = top_all + jnp.log(mass_all)

    def output_step(number, totals):
        key_tile, value_tile, place_tile = key_block(number * block_rows, block_rows)
        parts = []
        for which in range(2):

            def output_live(total, which=which):
                scores = tile_scores(which, key_tile, place_tile)
                probs = jnp.exp(scores - lse[which][..., None]).astype(jnp.bfloat16)
                return total + jnp.einsum(
                    "kgtu,ukd->tkgd", probs, value_tile, preferred_element_type=jnp.float32
                )

            parts.append(
                lax.cond(place_tile[0] <= query_top[which], output_live, unchanged, totals[which])
            )
        return jnp.stack(parts)

    row_shape = (2, half_rows, KVH, group_size, HD)
    attn = lax.fori_loop(0, block_count, output_step, jnp.zeros(row_shape, jnp.float32))
    router_term = jnp.sum(upstream * attn, axis=(2, 3, 4)).reshape(slots)
    logit_grad = own_gate * (1.0 - own_gate) * router_term
    delta = jnp.transpose(jnp.sum(scaled_grad.astype(jnp.float32) * attn, axis=-1), (0, 2, 3, 1))

    def tile_grads(which, key_tile, value_tile, place_tile):
        scores = tile_scores(which, key_tile, place_tile)
        weights = jnp.exp(scores - lse[which][..., None])
        prob_grad = jnp.einsum(
            "tkgd,ukd->kgtu", scaled_grad[which], value_tile, preferred_element_type=jnp.float32
        )
        score_grad = (weights * (prob_grad - delta[which][..., None]) * score_scale).astype(
            jnp.bfloat16
        )
        return (weights, score_grad)

    def query_step(number, totals):
        key_tile, value_tile, place_tile = key_block(number * block_rows, block_rows)
        parts = []
        for which in range(2):

            def query_live(total, which=which):
                weights, score_grad = tile_grads(which, key_tile, value_tile, place_tile)
                return total + jnp.einsum(
                    "kgtu,ukd->tkgd", score_grad, key_tile, preferred_element_type=jnp.float32
                )

            parts.append(
                lax.cond(place_tile[0] <= query_top[which], query_live, unchanged, totals[which])
            )
        return jnp.stack(parts)

    query_acc = lax.fori_loop(0, block_count, query_step, jnp.zeros(row_shape, jnp.float32))
    query_acc = query_acc.reshape(slots, HQ, HD)
    query_done = (
        turn_back(query_acc, held_cos, held_sin).astype(jnp.bfloat16).reshape(slots, HQ * HD)
    )
    tile_rows = math.gcd(lax.axis_size("ctx") * slots, 512)

    def term_step(number, terms):
        key_tile, value_tile, place_tile = key_block(number * tile_rows, tile_rows)
        key_acc = jnp.zeros((tile_rows, KVH, HD), jnp.float32)
        value_acc = jnp.zeros((tile_rows, KVH, HD), jnp.float32)
        for which in range(2):

            def term_live(state, which=which):
                key_old, value_old = state
                weights, score_grad = tile_grads(which, key_tile, value_tile, place_tile)
                probs = weights.astype(jnp.bfloat16)
                key_new = key_old + jnp.einsum(
                    "kgtu,tkgd->ukd",
                    score_grad,
                    query_rot[which],
                    preferred_element_type=jnp.float32,
                )
                value_new = value_old + jnp.einsum(
                    "kgtu,tkgd->ukd", probs, scaled_grad[which], preferred_element_type=jnp.float32
                )
                return (key_new, value_new)

            key_acc, value_acc = lax.cond(
                place_tile[0] <= query_top[which], term_live, unchanged, (key_acc, value_acc)
            )
        piece = jnp.stack(
            [key_acc.reshape(tile_rows, KVH * HD), value_acc.reshape(tile_rows, KVH * HD)], axis=1
        )
        return lax.dynamic_update_slice_in_dim(terms, piece, number * tile_rows, 0)

    key_sums = lax.psum_scatter(
        lax.fori_loop(
            0,
            lax.axis_size("ctx") * slots // tile_rows,
            term_step,
            jnp.zeros((lax.axis_size("ctx") * slots, 2, KVH * HD), jnp.float32),
        ),
        "ctx",
        scatter_dimension=0,
        tiled=True,
    )
    key_grad = (
        turn_back(key_sums[:, 0].reshape(slots, KVH, HD), cosine, sine)
        .astype(jnp.bfloat16)
        .reshape(slots, KVH * HD)
    )
    value_grad = key_sums[:, 1].astype(jnp.bfloat16)
    router_part = jnp.dot(logit_grad, input_wide, precision=lax.Precision.HIGHEST)
    router_total = lax.psum(router_part, ("dp", "ctx"))
    router_grad = router_total / math.sqrt(lax.axis_size("dp") * lax.axis_size("ctx") * slots)
    return (query_done[None], key_grad[None], value_grad[None], router_grad)


def solution(mesh):
    in_specs = (
        P("dp", "ctx", None),
        P("dp", "ctx", None),
        P("dp", "ctx", None),
        P("dp", "ctx", None),
        P("dp", "ctx", None),
        P(),
        P("dp", "ctx"),
    )
    out_specs = (P("dp", "ctx", None), P("dp", "ctx", None), P("dp", "ctx", None), P())
    return jax.shard_map(shards, mesh=mesh, in_specs=in_specs, out_specs=out_specs, check_vma=False)
```

profile of v0, /device:TPU:0, one launch (start us, length us, event | category | flops | bytes accessed | tf_op | source)
XLA Modules:
  0.0 183.6 jit_solution(4861422479824273964)
XLA Ops:
  7.3 0.5 broadcast.453
  7.8 1.3 reduce.4
  9.3 0.6 fusion.124
  9.9 0.6 dynamic-slice
  11.1 0.7 fusion.118
  11.9 13.1 %all-reduce = s32[256]{0:T(256)S(1)} all-reduce(s32[256]{0:T(256)S(1)} %get-tuple-element.913), channel_id=2, replica_groups=mesh['dp'=4,'ctx'=8] {'ctx'}, use_global_device_ids=true, to_apply=%add | all-reduce | flops 256 | bytes 2048 | tf_op jit(solution)/shard_map/all_gather | solution.py:67
  24.9 0.5 slice.210
  28.1 0.6 copy-done.11
  29.1 30.8 %all_gather.10 = bf16[256,512]{1,0:T(8,128)(2,1)S(1)} all-gather(bf16[32,512]{1,0:T(8,128)(2,1)S(1)} %bitcast.468), channel_id=1, replica_groups=mesh['dp'=4,'ctx'=8] {'ctx'}, dimensions={0}, use_global_device_ids=true | all-gather | bytes 294912 | tf_op jit(solution)/shard_map/all_gather | solution.py:65
  60.1 0.8 copy-done.8
  61.3 2.6 %conditional.9 = (f32[1,4,4,16]{3,2,1,0:T(4,128)}, f32[1,4,4,16]{3,2,1,0:T(4,128)S(1)}) conditional(s32[]{:T(128)} %bitcast.100, (f32[4,4,16]{2,1,0:T(4,128)S(1)}, f32[4,4,16]{2,1,0:T(4,128)S(1)}) %tuple.154, (s32[2,16]{1,0:T(2,128)S(1)}, s32[256]{0:T(256)S(1)}, bf16[2,16,4,4,128]{4,1,0,3,2:T(8,128)(2,1)S(1)}, bf16[256,4,128]{0,2,1:T(8,128)(2,1)S(1)}, ...), branch_computations={%region_5.6_spmd, %region_6.9_spmd} | conditional | flops 17109504 | bytes 872656 | solution.py:121
  61.7 0.6 max.5
  62.3 0.9 exponential_reduce_fusion.1
  63.2 0.7 add_bitcast_fusion.1
  63.9 2.6 %conditional.8 = (f32[1,4,4,16]{3,2,1,0:T(4,128)}, f32[1,4,4,16]{3,2,1,0:T(4,128)S(1)}) conditional(s32[]{:T(128)} %bitcast.96, (f32[4,4,16]{2,1,0:T(4,128)S(1)}, f32[4,4,16]{2,1,0:T(4,128)S(1)}) %tuple.154, (s32[2,16]{1,0:T(2,128)S(1)}, s32[256]{0:T(256)S(1)}, bf16[2,16,4,4,128]{4,1,0,3,2:T(8,128)(2,1)S(1)}, bf16[256,4,128]{0,2,1:T(8,128)(2,1)S(1)}, ...), branch_computations={%region_1.2_spmd, %region_2.5_spmd} | conditional | flops 17109504 | bytes 872656 | solution.py:121
  64.3 0.6 max.4
  64.9 0.9 exponential_reduce_fusion
  65.8 0.7 add_bitcast_fusion
  66.5 30.9 %all-gather.1 = bf16[1,256,512]{2,1,0:T(8,128)(2,1)S(1)} all-gather(bf16[1,32,512]{2,1,0:T(8,128)(2,1)S(1)} %copy-done.10), channel_id=3, replica_groups=mesh['dp'=4,'ctx'=8] {'ctx'}, dimensions={1}, use_global_device_ids=true | all-gather | bytes 294912 | tf_op jit(solution)/shard_map/all_gather | solution.py:66
  97.5 0.7 maximum_add_fusion
  98.3 0.5 conditional.11
  98.8 0.5 conditional.10
  98.9 0.3 fusion.12
  99.5 0.3 fusion.107
  100.0 0.9 copy-done.5
  101.1 0.3 multiply_reduce_fusion.1
  101.4 5.3 %conditional.14 = (f32[256,4,128]{2,0,1:T(8,128)}, f32[256,4,128]{2,0,1:T(8,128)}, (f32[256,4,128]{0,2,1:T(8,128)S(1)}, f32[256,4,128]{0,2,1:T(8,128)S(1)})) conditional(s32[]{:T(128)} %bitcast.96, () %tuple.158, (s32[2,16]{1,0:T(2,128)S(1)}, s32[256]{0:T(256)S(1)}, bf16[2,16,4,4,128]{4,1,0,3,2:T(8,128)(2,1)S(1)}, ...), branch_computations={%region_18.19_spmd.clone, %region_19.20_spmd.clone} | conditional | flops 67637248 | bytes 5014760 | solution.py:218
  101.9 1.2 convolution_bitcast_fusion.10
  103.1 1.1 convolution_bitcast_fusion.9
  104.2 1.2 copy.366
  105.4 1.2 copy.365
  106.7 4.7 %conditional.15 = (f32[256,1,512]{2,0,1:T(8,128)S(1)}, f32[256,1,512]{2,0,1:T(8,128)S(1)}) conditional(s32[]{:T(128)} %bitcast.100, (f32[256,4,128]{0,2,1:T(8,128)S(1)}, f32[256,4,128]{0,2,1:T(8,128)S(1)}) %get-tuple-element.874, (s32[2,16]{1,0:T(2,128)S(1)}, s32[256]{0:T(256)S(1)}, bf16[2,16,4,4,128]{4,1,0,3,2:T(8,128)(2,1)S(1)}, ...), branch_computations={%region_20.21_spmd, %region_21.22_spmd} | conditional | flops 67899392 | bytes 9209096 | solution.py:218
  106.7 0.6 copy-done.3
  107.4 1.3 copy.299
  109.6 1.2 copy.298
  110.9 0.4 fusion.72
  111.4 1.0 pad_maximum_fusion
  112.6 0.8 copy-done.2
  113.4 0.8 conditional.13
  114.2 0.8 conditional.12
  115.2 0.3 add_convert_fusion
  115.7 0.7 convert_element_type.164
  116.9 37.3 %psum.7 = f32[4096]{0:T(1024)S(1)} all-reduce(f32[4096]{0:T(1024)S(1)} %bitcast.470), channel_id=1, replica_groups=mesh['dp'=4,'ctx'=8] {'dp','ctx'}, use_global_device_ids=true, to_apply=%region_24.25 | all-reduce | flops 4096 | bytes 32768 | tf_op jit(solution)/shard_map/psum | solution.py:244
  154.2 0.6 broadcast_multiply_fusion
  154.8 19.5 %reduce-scatter.2.cloned.1.call-done = f32[32,2,512]{2,0,1:T(8,128)} async-done(((f32[256,2,512]{2,0,1:T(8,128)}), f32[32,2,512]{2,0,1:T(8,128)}) %reduce-scatter.2.cloned.1.call-update) | async-done | bytes 131088 | tf_op jit(solution)/shard_map/reduce_scatter | solution.py:226
  174.3 0.8 slice-done
  175.4 0.6 convert_element_type.165
  176.2 0.6 fusion.111
  (108 shorter events, 7.6 us)
Async XLA Ops:
  7.2 92.1 %copy-start = (bf16[1,32,4096]{2,1,0:T(8,128)(2,1)S(1)}, bf16[1,32,4096]{2,1,0:T(8,128)(2,1)}, u32[]{:S(2)}) copy-start(bf16[1,32,4096]{2,1,0:T(8,128)(2,1)} %param.31) | copy-start | bytes 786436
  7.2 2.7 %copy-start.14 = (u32[32]{0:T(128)S(1)}, u32[32]{0:T(128)}, u32[]{:S(2)}) copy-start(u32[32]{0:T(128)} %constant.129) | copy-start | bytes 388
  7.2 20.8 %copy-start.9 = (bf16[1,32,512]{2,1,0:T(8,128)(2,1)S(1)}, bf16[1,32,512]{2,1,0:T(8,128)(2,1)}, u32[]{:S(2)}) copy-start(bf16[1,32,512]{2,1,0:T(8,128)(2,1)} %param.28) | copy-start | bytes 98308
  7.2 167.1 %reduce-scatter.2.cloned.1.call-start = ((), (), s32[]{:S(2)}) async-start(), calls=%async_computation.1 | async-start | bytes 1179648 | tf_op jit(solution)/shard_map/reduce_scatter | solution.py:226
  28.1 0.7 copy-start.11
  28.1 0.7 copy-start.12
  59.9 0.9 copy-start.8
  61.3 45.4 %copy-start.1 = (bf16[2,16,4,4,128]{4,1,0,3,2:T(8,128)(2,1)}, bf16[2,16,4,4,128]{4,1,0,3,2:T(8,128)(2,1)S(1)}, u32[]{:S(2)}) copy-start(bf16[2,16,4,4,128]{4,1,0,3,2:T(8,128)(2,1)S(1)} %pad_maximum_fusion.2) | copy-start | bytes 393220
  63.9 2.6 %copy-start.10 = (bf16[1,32,512]{2,1,0:T(8,128)(2,1)S(1)}, bf16[1,32,512]{2,1,0:T(8,128)(2,1)}, u32[]{:S(2)}) copy-start(bf16[1,32,512]{2,1,0:T(8,128)(2,1)} %param.29) | copy-start | bytes 98308
  98.8 0.7 copy-start.13
  99.9 0.9 copy-start.5
  106.7 0.7 copy-start.3
  107.4 1.4 copy-start.4
  112.5 0.9 copy-start.2
  115.6 0.9 copy-start.6
  174.3 0.8 slice-start
  175.3 0.9 copy-start.7
Sparse Core Ops, SparseCore 0:
  112.6 61.6 reduce-scatter.1
where the time goes:
time: 185 us; the launch traced here: 184 us
  blocking collectives  112 us (61%)
  waiting for transfers between devices  19.5 us (11%)
  between operations  17.6 us (10%)
  local copies, waits for them, and re-layouts  16.6 us (9%)
  other arithmetic  11.4 us (6%)
  matrix products  6.1 us (3%)
    psum x1, blocking collectives, shards(): router_total = lax.psum(router_part, ('dp', 'ctx'))  37.3 us
    all_gather x1, blocking collectives, shards(): lax.all_gather(values[0], 'ctx', axis=0, tiled=True)  30.9 us
    all_gather x1, blocking collectives, shards(): lax.all_gather(key_rot, 'ctx', axis=0, tiled=True)  30.8 us
    reduce_scatter x1, waiting for transfers between devices, shards(): lax.psum_scatter(lax.fori_loop(0, lax.axis_size('ctx') * slots // tile_ro...  19.5 us
    all_gather x1, blocking collectives, shards(): lax.all_gather(own_places, 'ctx', axis=0, tiled=True)  13.1 us
    unnamed x32, local copies, waits for them, and re-layouts  4.85 us
  transfers between devices with their start and end apart: 1, of which 1 were waited for; matrix products, arithmetic and copies ran while one was open for 2% of the time, Pallas kernels for 0%

commit v1 on v0

v1 whole, which is shorter than its diff:
```python
import functools
import math

import jax
import jax.numpy as jnp
import numpy as np
from jax import lax
from jax.experimental import pallas as pl
from jax.experimental.pallas import tpu as pltpu
from jax.sharding import PartitionSpec as P

HQ = 16
KVH = 4
HD = 128
GROUP = HQ // KVH
ROPE_BASE = 500000.0
NEG_LARGE = -1e30
VMEM_LIMIT = 32 * 1024 * 1024
SCORES_COST = 20 * 10**9
TERMS_COST = 20 * 10**9
RIDE_COST = 20 * 10**9


def rope_table():
    half = HD // 2
    frequency = [ROPE_BASE ** (-number / half) for number in range(half)]
    coarse = [256.0 * factor % (2.0 * math.pi) for factor in frequency]
    return np.asarray([coarse + coarse, frequency + frequency], np.float32)


def turn(vectors, cosine, sine):
    return vectors * cosine + pltpu.roll(vectors, HD // 2, 1) * sine


def head(number):
    return slice(number * HD, (number + 1) * HD)


def rows_of(number, depth):
    return slice(number * depth, (number + 1) * depth)


def diagonal(slots, lanes):
    row = lax.broadcasted_iota(jnp.int32, (slots, lanes), 0)
    lane = lax.broadcasted_iota(jnp.int32, (slots, lanes), 1)
    return lax.rem(lane, slots) == row


def prepare_kernel(*refs):
    place_hbm, table_hbm, key_hbm, value_hbm, query_hbm, upstream_hbm = refs[:6]
    pair_ref, query_out, trig_ref = refs[6:9]
    place_ref, table_ref, key_ref, value_ref, query_ref, upstream_ref, semaphores = refs[9:]
    slots = key_ref.shape[0]
    copies = [
        pltpu.make_async_copy(source, target, semaphores.at[at])
        for at, (source, target) in enumerate(
            [
                (place_hbm, place_ref),
                (table_hbm, table_ref),
                (key_hbm, key_ref),
                (value_hbm, value_ref),
                (query_hbm, query_ref),
                (upstream_hbm, upstream_ref),
            ]
        )
    ]
    for copy in copies:
        copy.start()
    copies[0].wait()
    place = place_ref[...]
    upper = (place >> 8).astype(jnp.float32)
    lower = (place & 255).astype(jnp.float32)
    same = diagonal(slots, slots)
    upper = jnp.sum(jnp.where(same, upper, 0.0), axis=1, keepdims=True)
    lower = jnp.sum(jnp.where(same, lower, 0.0), axis=1, keepdims=True)
    copies[1].wait()
    angles = upper * table_ref[0:1, :] + lower * table_ref[1:2, :]
    cosine = jnp.cos(angles)
    lane = lax.broadcasted_iota(jnp.int32, angles.shape, 1)
    sine = jnp.sin(angles)
    sine = jnp.where(lane < HD // 2, -sine, sine)
    trig_ref[0:slots, :] = cosine
    trig_ref[slots : 2 * slots, :] = sine
    for copy in copies[2:]:
        copy.wait()
    for number in range(KVH):
        wide = key_ref[:, head(number)].astype(jnp.float32)
        pair_ref[rows_of(number, slots), :] = turn(wide, cosine, sine).astype(jnp.bfloat16)
        pair_ref[rows_of(KVH + number, slots), :] = value_ref[:, head(number)]
    for number in range(HQ):
        wide = query_ref[:, head(number)].astype(jnp.float32)
        query_out[rows_of(number, slots), :] = turn(wide, cosine, sine).astype(jnp.bfloat16)
        query_out[rows_of(HQ + number, slots), :] = upstream_ref[:, head(number)]


def gate_kernel(weight_hbm, input_hbm, gate_ref, input_ref, weight_ref, semaphores):
    copies = [
        pltpu.make_async_copy(weight_hbm, weight_ref, semaphores.at[0]),
        pltpu.make_async_copy(input_hbm, input_ref, semaphores.at[1]),
    ]
    for copy in copies:
        copy.start()
    for copy in copies:
        copy.wait()
    slots = input_ref.shape[0]
    blocks = weight_ref.shape[0]
    total = jnp.zeros((slots, HD), jnp.float32)
    for number in range(blocks):
        total += input_ref[:, head(number)].astype(jnp.float32) * weight_ref[number : number + 1, :]
    gate = jax.nn.sigmoid(jnp.sum(total, axis=1, keepdims=True))
    same = diagonal(slots, gate_ref.shape[1])
    gate_ref[...] = jnp.broadcast_to(
        jnp.sum(jnp.where(same, gate, 0.0), axis=0, keepdims=True), gate_ref.shape
    )


def tiles(pair_refs, query_refs, number, slots):
    rows = GROUP * slots
    key_tile = jnp.concatenate([ref[rows_of(number, slots), :] for ref in pair_refs], axis=0)
    value_tile = jnp.concatenate(
        [ref[rows_of(KVH + number, slots), :] for ref in pair_refs], axis=0
    )
    query_tile = jnp.concatenate([ref[rows_of(number, rows), :] for ref in query_refs], axis=0)
    upstream_tile = jnp.concatenate(
        [ref[rows_of(KVH + number, rows), :] for ref in query_refs], axis=0
    )
    return key_tile, value_tile, query_tile, upstream_tile


def scores_kernel(slots, *refs):
    gate_ref, own_ref, other_ref = refs[:3]
    pair_refs = refs[3:-3]
    grown_out, grad_out, stats_out = refs[-3:]
    rows = GROUP * slots
    keys_total = len(pair_refs) * slots
    own = lax.axis_index("ctx")
    other = own + 1 - 2 * lax.rem(own, 2)
    row = lax.broadcasted_iota(jnp.int32, (keys_total, 2 * rows), 0)
    lane = lax.broadcasted_iota(jnp.int32, (keys_total, 2 * rows), 1)
    owner = 2 * jnp.bitwise_xor(own // 2, row // slots) + lax.rem(own, 2)
    key_at = owner * slots + lax.rem(row, slots)
    query_at = lax.rem(lane, slots) + jnp.where(lane < rows, own, other) * slots
    bias = jnp.where(key_at <= query_at, 0.0, NEG_LARGE)
    across = (((1,), (1,)), ((), ()))
    for number in range(KVH):
        key_tile, value_tile, query_tile, upstream_tile = tiles(
            pair_refs, (own_ref, other_ref), number, slots
        )
        scores = lax.dot_general(
            key_tile, query_tile, across, preferred_element_type=jnp.float32
        )
        scores = scores * (1.0 / math.sqrt(HD)) + bias
        top = jnp.max(scores, axis=0, keepdims=True)
        grown = jnp.exp(scores - top)
        prob_grad = lax.dot_general(
            value_tile, upstream_tile, across, preferred_element_type=jnp.float32
        )
        grown_out[number] = grown
        grad_out[number] = prob_grad
        stats_out[number : number + 1, :] = top
        stats_out[KVH + number : KVH + number + 1, :] = jnp.sum(grown, axis=0, keepdims=True)
        stats_out[2 * KVH + number : 2 * KVH + number + 1, :] = jnp.sum(
            grown * prob_grad, axis=0, keepdims=True
        )
    stats_out[3 * KVH :, :] = jnp.concatenate(
        [gate_ref[0:KVH, :], jnp.zeros((KVH, rows), jnp.float32)], axis=1
    )


def combine_kernel(own_ref, other_ref, input_ref, input_other_ref, coef_out, router_out):
    slots = input_ref.shape[0]
    rows = GROUP * slots
    mine = own_ref[...]
    swapped = other_ref[...]
    theirs = jnp.concatenate([swapped[:, rows:], swapped[:, :rows]], axis=1)
    top = jnp.maximum(mine[0:KVH], theirs[0:KVH])
    mine_part = jnp.exp(mine[0:KVH] - top)
    their_part = jnp.exp(theirs[0:KVH] - top)
    mass = mine[KVH : 2 * KVH] * mine_part + theirs[KVH : 2 * KVH] * their_part
    inverse = 1.0 / mass
    inner = (
        mine[2 * KVH : 3 * KVH] * mine_part + theirs[2 * KVH : 3 * KVH] * their_part
    ) * inverse
    gate = mine[3 * KVH :] + theirs[3 * KVH :]
    coef_out[0:KVH, :] = mine_part * inverse * gate
    coef_out[KVH : 2 * KVH, :] = inner
    slope = gate[0:1] * (1.0 - gate[0:1]) * jnp.sum(inner, axis=0, keepdims=True)
    same = diagonal(slots, rows)
    own_slope = jnp.sum(jnp.where(same, slope[:, :rows], 0.0), axis=1, keepdims=True)
    other_slope = jnp.sum(jnp.where(same, slope[:, rows:], 0.0), axis=1, keepdims=True)
    for number in range(router_out.shape[0]):
        router_out[number : number + 1, :] = jnp.sum(
            own_slope * input_ref[:, head(number)].astype(jnp.float32)
            + other_slope * input_other_ref[:, head(number)].astype(jnp.float32),
            axis=0,
            keepdims=True,
        )


def terms_kernel(slots, half, *refs):
    coef_ref, grown_ref, grad_ref, own_ref, other_ref = refs[:5]
    pair_refs = refs[5 : 5 + half]
    query_out, query_send, term_own = refs[5 + half : 8 + half]
    term_refs = refs[8 + half :]
    rows = GROUP * slots
    scale = 1.0 / math.sqrt(HD)
    for number in range(KVH):
        key_tile, _, query_tile, upstream_tile = tiles(
            pair_refs, (own_ref, other_ref), number, slots
        )
        gated = grown_ref[number] * coef_ref[number : number + 1, :]
        inner = coef_ref[KVH + number : KVH + number + 1, :]
        score_grad = (gated * (grad_ref[number] - inner) * scale).astype(jnp.bfloat16)
        key_term = jnp.dot(score_grad, query_tile, preferred_element_type=jnp.float32)
        value_term = jnp.dot(
            gated.astype(jnp.bfloat16), upstream_tile, preferred_element_type=jnp.float32
        )
        key_rows, value_rows = rows_of(number, slots), rows_of(KVH + number, slots)
        term_own[key_rows, :] = key_term[0:slots]
        term_own[value_rows, :] = value_term[0:slots]
        for at, ref in enumerate(term_refs, 1):
            ref[key_rows, :] = key_term[rows_of(at, slots)].astype(jnp.bfloat16)
            ref[value_rows, :] = value_term[rows_of(at, slots)].astype(jnp.bfloat16)
        query_term = lax.dot_general(
            score_grad, key_tile, (((0,), (0,)), ((), ())), preferred_element_type=jnp.float32
        )
        query_out[rows_of(number, rows), :] = query_term[0:rows]
        query_send[rows_of(number, rows), :] = query_term[rows:].astype(jnp.bfloat16)


def ride_kernel(groups, *refs):
    router_refs = refs[:groups]
    count = (len(refs) - groups - 1) // 2
    term_refs = refs[groups : groups + count]
    router_out = refs[groups + count]
    router = router_refs[0][...]
    for ref in router_refs[1:]:
        router += ref[...]
    router_out[...] = router
    for term, out in zip(term_refs, refs[groups + count + 1 :]):
        out[0 : term.shape[0], :] = term[...]
        out[term.shape[0] :, :] = router.astype(jnp.bfloat16)


def query_kernel(trig_ref, own_ref, other_ref, query_out, trig_out):
    slots = query_out.shape[0]
    cosine = trig_ref[0:slots, :]
    sine = trig_ref[slots : 2 * slots, :]
    trig_out[...] = trig_ref[...]
    for number in range(HQ):
        part = rows_of(number, slots)
        total = own_ref[part, :] + other_ref[part, :].astype(jnp.float32)
        query_out[:, head(number)] = turn(total, cosine, -sine).astype(jnp.bfloat16)


def final_kernel(router_scale, *refs):
    trig_ref, own_ref, router_ref = refs[:3]
    term_refs = refs[3:-3]
    key_out, value_out, router_out = refs[-3:]
    slots = key_out.shape[0]
    cosine = trig_ref[0:slots, :]
    sine = trig_ref[slots : 2 * slots, :]
    for number in range(2 * KVH):
        part = rows_of(number, slots)
        total = own_ref[part, :]
        for ref in term_refs:
            total += ref[part, :].astype(jnp.float32)
        if number < KVH:
            key_out[:, head(number)] = turn(total, cosine, -sine).astype(jnp.bfloat16)
        else:
            value_out[:, head(number - KVH)] = total.astype(jnp.bfloat16)
    router = router_ref[...]
    for ref in term_refs:
        router += ref[2 * KVH * slots :, :].astype(jnp.float32)
    router_out[...] = router * router_scale


def call(kernel, outs, args, fetched=(), scratch=(), cost=None):
    local = pl.BlockSpec(memory_space=pltpu.VMEM)
    distant = pl.BlockSpec(memory_space=pl.ANY)
    scratch = list(scratch) + [pltpu.SemaphoreType.DMA((len(fetched),))] * bool(fetched)
    return pl.pallas_call(
        kernel,
        out_shape=outs,
        in_specs=[local] * len(args) + [distant] * len(fetched),
        out_specs=[local] * len(outs),
        scratch_shapes=scratch,
        compiler_params=pltpu.CompilerParams(vmem_limit_bytes=VMEM_LIMIT),
        cost_estimate=cost and pl.CostEstimate(cost, 0, 0),
    )(*args, *[pltpu.with_memory_space_constraint(array, pltpu.HBM) for array in fetched])


def exchange(array, axis, step, size):
    return lax.ppermute(array, axis, [(at, at ^ step) for at in range(size)])


def shards(queries, keys, values, out_grad, routed_inputs, router_weight, positions):
    slots = queries.shape[1]
    width = routed_inputs.shape[2]
    count = lax.axis_size("ctx")
    groups = lax.axis_size("dp")
    half = count // 2
    rows = GROUP * slots
    lines = width // HD
    bf16, f32 = jnp.bfloat16, jnp.float32

    def swap(array):
        return exchange(array, "ctx", 1, count)

    near = pltpu.VMEM
    fetched = [positions, jnp.asarray(rope_table()), keys[0], values[0], queries[0], out_grad[0]]
    pair, query, trig = call(
        prepare_kernel,
        [
            near((2 * KVH * slots, HD), bf16),
            near((2 * HQ * slots, HD), bf16),
            near((2 * slots, HD), f32),
        ],
        [],
        fetched,
        [near(array.shape, array.dtype) for array in fetched],
    )
    query_other = swap(query)
    pairs = [pair] + [
        exchange(pair, "ctx", 2 * step, count) for step in range(1, half)
    ]
    gate, inputs = call(
        gate_kernel,
        [near((8, rows), f32), near((slots, width), bf16)],
        [],
        [router_weight.reshape(lines, HD), routed_inputs[0]],
        [near((lines, HD), f32)],
    )
    inputs_other = swap(routed_inputs[0])
    grown, grad, stats = call(
        functools.partial(scores_kernel, slots),
        [
            near((KVH, half * slots, 2 * rows), f32),
            near((KVH, half * slots, 2 * rows), f32),
            near((4 * KVH, 2 * rows), f32),
        ],
        [gate, query, query_other, *pairs],
        cost=SCORES_COST,
    )
    coef, router = call(
        combine_kernel,
        [near((2 * KVH, 2 * rows), f32), near((lines, HD), f32)],
        [stats, swap(stats), inputs, inputs_other],
    )
    routers = [router] + [
        exchange(router, "dp", step, groups) for step in range(1, groups)
    ]
    query_own, query_send, term_own, *terms = call(
        functools.partial(terms_kernel, slots, half),
        [
            near((HQ * slots, HD), f32),
            near((HQ * slots, HD), bf16),
            near((2 * KVH * slots, HD), f32),
        ]
        + [near((2 * KVH * slots, HD), bf16)] * (half - 1),
        [coef, grown, grad, query, query_other, *pairs],
        cost=TERMS_COST,
    )
    query_back = swap(query_send)
    router, *terms = call(
        functools.partial(ride_kernel, groups),
        [near((lines, HD), f32)] + [near((2 * KVH * slots + lines, HD), bf16)] * (half - 1),
        [*routers, *terms],
        cost=RIDE_COST,
    )
    terms = [exchange(term, "ctx", 2 * step, count) for step, term in enumerate(terms, 1)]
    shape = jax.ShapeDtypeStruct
    query_grad, trig = call(
        query_kernel,
        [shape((slots, HQ * HD), bf16), near((2 * slots, HD), f32)],
        [trig, query_own, query_back],
    )
    key_grad, value_grad, router_grad = call(
        functools.partial(final_kernel, 1.0 / math.sqrt(groups * count * slots)),
        [shape((slots, KVH * HD), bf16), shape((slots, KVH * HD), bf16), shape((lines, HD), f32)],
        [trig, term_own, router, *terms],
    )
    return (query_grad[None], key_grad[None], value_grad[None], router_grad.reshape(width))


def solution(mesh):
    in_specs = (
        P("dp", "ctx", None),
        P("dp", "ctx", None),
        P("dp", "ctx", None),
        P("dp", "ctx", None),
        P("dp", "ctx", None),
        P(),
        P("dp", "ctx"),
    )
    out_specs = (P("dp", "ctx", None), P("dp", "ctx", None), P("dp", "ctx", None), P())
    return jax.shard_map(shards, mesh=mesh, in_specs=in_specs, out_specs=out_specs, check_vma=False)
```

time: 185 us -> 33.4 us (0.18)
  blocking collectives: 112 us -> 0 us
  between operations: 17.6 us -> 0.7 us
  local copies, waits for them, and re-layouts: 16.6 us -> 0.01 us
  starting transfers between devices: 0.04 us -> 15.4 us
  other arithmetic: 11.4 us -> 0 us
  waiting for transfers between devices: 19.5 us -> 12 us
  matrix products: 6.1 us -> 0 us
  Pallas kernels: 0 us -> 4.97 us
    all_gather x3 -> x0, blocking collectives: 74.7 us -> none  [the longest x1 30.9 us: shards(): lax.all_gather(values[0], 'ctx', axis=0, tiled=True)]
    psum x1 -> x0, blocking collectives: 37.3 us -> none  [shards(): router_total = lax.psum(router_part, ('dp', 'ctx'))]
    reduce_scatter x1 -> x0, waiting for transfers between devices: 19.5 us -> none  [shards(): lax.psum_scatter(lax.fori_loop(0, lax.axis_size('ctx') * slots // tile_ro...]
    ppermute x0 -> x13, starting transfers between devices: none -> 15.4 us  [exchange(): return lax.ppermute(array, axis, [(at, at ^ step) for at in range(size)])]
    ppermute x0 -> x13, waiting for transfers between devices: none -> 12 us  [exchange(): return lax.ppermute(array, axis, [(at, at ^ step) for at in range(size)])]
    dot_general x16 -> x0, matrix products: 6.1 us -> none  [the longest x2 1.6 us: term_live(): jnp.einsum('kgtu,tkgd->ukd', score_grad, query_rot[which], preferred_elem...]
    pallas_call x0 -> x8, Pallas kernels: none -> 4.97 us  [call(): pl.pallas_call(kernel, out_shape=outs, in_specs=[local] * len(args) + [di...]
    unnamed x32 -> x2, local copies, waits for them, and re-layouts: 4.85 us -> 0.01 us
  transfers between devices with their start and end apart: 1 -> 13, of which waited for: 1 -> 8; matrix products, arithmetic and copies ran while one was open for 2% -> 0% of each run, Pallas kernels for 0% -> 8%
where the time goes in v1:
time: 33.4 us; the launch traced here: 33.1 us
  starting transfers between devices  15.4 us (46%)
  waiting for transfers between devices  12 us (36%)
  Pallas kernels  4.97 us (15%)
  between operations  0.7 us (2%)
    ppermute x13, starting transfers between devices, exchange(): return lax.ppermute(array, axis, [(at, at ^ step) for at in range(size)])  15.4 us
    ppermute x13, waiting for transfers between devices, exchange(): return lax.ppermute(array, axis, [(at, at ^ step) for at in range(size)])  12 us
    pallas_call x8, Pallas kernels, call(): pl.pallas_call(kernel, out_shape=outs, in_specs=[local] * len(args) + [di...  4.97 us
  transfers between devices with their start and end apart: 13, of which 8 were waited for; matrix products, arithmetic and copies ran while one was open for 0% of the time, Pallas kernels for 8%

profile of v1, /device:TPU:0, one launch (start us, length us, event | category | flops | bytes accessed | tf_op | source)
XLA Modules:
  0.0 33.1 jit_solution(5938368495661379010)
XLA Ops:
  0.6 0.0 copy-start
  0.6 1.3 %shard_map.111 = (bf16[256,128]{1,0:T(8,128)(2,1)S(1)}, bf16[1024,128]{1,0:T(8,128)(2,1)S(1)}, f32[64,128]{1,0:T(8,128)S(1)}) custom-call(s32[1,32]{1,0:T(1,128)} %refs_0_.1, f32[2,128]{1,0:T(2,128)} %constant.2.clone.refs_1_, bf16[32,512]{1,0:T(8,128)(2,1)} %bitcast.14, bf16[32,512]{1,0:T(8,128)(2,1)} %bitcast.15, bf16[32,2048]{1,0:T(8,128)(2,1)} %bitcast.12, ...), custom_call_target="tpu_custom_call" | custom-call | tf_op jit(solution)/shard_map/pallas_call | solution.py:282
  1.9 3.0 %collective-permute-start = (bf16[1024,128]{1,0:T(8,128)(2,1)S(1)}, bf16[1024,128]{1,0:T(8,128)(2,1)S(1)}, u32[]{:S(2)}, u32[]{:S(2)}) collective-permute-start(bf16[1024,128]{1,0:T(8,128)(2,1)S(1)} %get-tuple-element.31.refs_1_.refs_3_), channel_id=1, source_target_pairs={{0,1},{1,0},{2,3},{3,2},{4,5},{5,4},{6,7},{7,6},{8,9},{9,8},{10,11... | collective-permute-start | bytes 786440 | tf_op jit(solution)/shard_map/ppermute | solution.py:294
  5.0 3.6 %collective-permute-start.3 = (bf16[256,128]{1,0:T(8,128)(2,1)S(1)}, bf16[256,128]{1,0:T(8,128)(2,1)S(1)}, u32[]{:S(2)}, u32[]{:S(2)}) collective-permute-start(bf16[256,128]{1,0:T(8,128)(2,1)S(1)} %get-tuple-element.32.refs_3_.refs_5_), channel_id=1, source_target_pairs={{0,6},{1,7},{2,4},{3,5},{4,2},{5,3},{6,0},{7,1},{8,14},{9,15},{10,... | collective-permute-start | bytes 196616 | tf_op jit(solution)/shard_map/ppermute | solution.py:294
  8.6 0.0 collective-permute-start.2
  8.6 0.8 %collective-permute-start.1 = (bf16[256,128]{1,0:T(8,128)(2,1)S(1)}, bf16[256,128]{1,0:T(8,128)(2,1)S(1)}, u32[]{:S(2)}, u32[]{:S(2)}) collective-permute-start(bf16[256,128]{1,0:T(8,128)(2,1)S(1)} %get-tuple-element.32.refs_3_.refs_5_), channel_id=1, source_target_pairs={{0,2},{1,3},{2,0},{3,1},{4,6},{5,7},{6,4},{7,5},{8,10},{9,11},{10,... | collective-permute-start | bytes 196616 | tf_op jit(solution)/shard_map/ppermute | solution.py:294
  9.4 0.0 copy-done
  9.4 0.3 collective-permute-start.5
  9.6 1.1 %shard_map.112 = (f32[8,128]{1,0:T(8,128)S(1)}, bf16[32,4096]{1,0:T(8,128)(2,1)S(1)}) custom-call(f32[32,128]{1,0:T(8,128)} %bitcast.16, bf16[32,4096]{1,0:T(8,128)(2,1)} %bitcast.10), custom_call_target="tpu_custom_call" | custom-call | tf_op jit(solution)/shard_map/pallas_call | solution.py:282
  10.8 1.0 %collective-permute-done.3.refs_6_.refs_8_ = bf16[256,128]{1,0:T(8,128)(2,1)S(1)} collective-permute-done((bf16[256,128]{1,0:T(8,128)(2,1)S(1)}, bf16[256,128]{1,0:T(8,128)(2,1)S(1)}, u32[]{:S(2)}, u32[]{:S(2)}) %collective-permute-start.3) | collective-permute-done | bytes 65568 | tf_op jit(solution)/shard_map/ppermute | solution.py:294
  11.8 2.1 %collective-permute-done.2.refs_5_.refs_7_ = bf16[256,128]{1,0:T(8,128)(2,1)S(1)} collective-permute-done((bf16[256,128]{1,0:T(8,128)(2,1)S(1)}, bf16[256,128]{1,0:T(8,128)(2,1)S(1)}, u32[]{:S(2)}, u32[]{:S(2)}) %collective-permute-start.2) | collective-permute-done | bytes 65568 | tf_op jit(solution)/shard_map/ppermute | solution.py:294
  13.9 0.1 collective-permute-done.1.refs_4_.refs_6_
  14.0 0.0 collective-permute-done.refs_2_.refs_4_
  14.0 0.4 %shard_map.113 = (f32[4,128,256]{2,1,0:T(8,128)S(1)}, f32[4,128,256]{2,1,0:T(8,128)S(1)}, f32[16,256]{1,0:T(8,128)S(1)}) custom-call(f32[8,128]{1,0:T(8,128)S(1)} %get-tuple-element.30.refs_0_, bf16[1024,128]{1,0:T(8,128)(2,1)S(1)} %get-tuple-element.31.refs_1_.refs_3_, bf16[1024,128]{1,0:T(8,128)(2,1)S(1)} %collective-permute-done.refs_2_.refs_4_, ...), custom_call_target="tpu_custom_call" | custom-call | flops 20000000000 | tf_op jit(solution)/shard_map/pallas_call | solution.py:282
  14.4 0.5 %collective-permute-start.4 = (f32[16,256]{1,0:T(8,128)S(1)}, f32[16,256]{1,0:T(8,128)S(1)}, u32[]{:S(2)}, u32[]{:S(2)}) collective-permute-start(f32[16,256]{1,0:T(8,128)S(1)} %get-tuple-element.33.own_ref), channel_id=1, source_target_pairs={{0,1},{1,0},{2,3},{3,2},{4,5},{5,4},{6,7},{7,6},{8,9},{9,8},{10,11... | collective-permute-start | bytes 49160 | tf_op jit(solution)/shard_map/ppermute | solution.py:294
  14.9 2.2 %collective-permute-done.5.input_other_ref = bf16[32,4096]{1,0:T(8,128)(2,1)S(1)} collective-permute-done((bf16[32,4096]{1,0:T(8,128)(2,1)S(1)}, bf16[32,4096]{1,0:T(8,128)(2,1)S(1)}, u32[]{:S(2)}, u32[]{:S(2)}) %collective-permute-start.5) | collective-permute-done | bytes 262176 | tf_op jit(solution)/shard_map/ppermute | solution.py:294
  17.1 1.1 %collective-permute-done.4.other_ref = f32[16,256]{1,0:T(8,128)S(1)} collective-permute-done((f32[16,256]{1,0:T(8,128)S(1)}, f32[16,256]{1,0:T(8,128)S(1)}, u32[]{:S(2)}, u32[]{:S(2)}) %collective-permute-start.4) | collective-permute-done | bytes 16416 | tf_op jit(solution)/shard_map/ppermute | solution.py:294
  18.2 0.2 shard_map.114
  18.4 0.1 collective-permute-start.9
  18.5 1.6 %collective-permute-start.8 = (f32[32,128]{1,0:T(8,128)S(1)}, f32[32,128]{1,0:T(8,128)S(1)}, u32[]{:S(2)}, u32[]{:S(2)}) collective-permute-start(f32[32,128]{1,0:T(8,128)S(1)} %get-tuple-element.43.refs_0_), channel_id=1, source_target_pairs={{0,16},{8,24},{16,0},{24,8},{1,17},{9,25},{17,1},{25,9},{2,18},{10... | collective-permute-start | bytes 49160 | tf_op jit(solution)/shard_map/ppermute | solution.py:294
  20.1 0.3 collective-permute-start.7
  20.4 0.4 %shard_map.115 = (f32[512,128]{1,0:T(8,128)S(1)}, bf16[512,128]{1,0:T(8,128)(2,1)S(1)}, f32[256,128]{1,0:T(8,128)S(1)}, bf16[256,128]{1,0:T(8,128)(2,1)S(1)}, bf...) custom-call(f32[8,256]{1,0:T(8,128)S(1)} %get-tuple-element.35.refs_0_, ...), custom_call_target="tpu_custom_call" | custom-call | flops 20000000000 | tf_op jit(solution)/shard_map/pallas_call | solution.py:282
  20.8 0.8 %collective-permute-start.6 = (bf16[512,128]{1,0:T(8,128)(2,1)S(1)}, bf16[512,128]{1,0:T(8,128)(2,1)S(1)}, u32[]{:S(2)}, u32[]{:S(2)}) collective-permute-start(bf16[512,128]{1,0:T(8,128)(2,1)S(1)} %get-tuple-element.39), channel_id=1, source_target_pairs={{0,1},{1,0},{2,3},{3,2},{4,5},{5,4},{6,7},{7,6},{8,9},{9,8},{10,11... | collective-permute-start | bytes 393224 | tf_op jit(solution)/shard_map/ppermute | solution.py:294
  21.6 0.2 collective-permute-done.9.refs_3_
  21.8 0.5 %collective-permute-done.8.refs_2_ = f32[32,128]{1,0:T(8,128)S(1)} collective-permute-done((f32[32,128]{1,0:T(8,128)S(1)}, f32[32,128]{1,0:T(8,128)S(1)}, u32[]{:S(2)}, u32[]{:S(2)}) %collective-permute-start.8) | collective-permute-done | bytes 16416 | tf_op jit(solution)/shard_map/ppermute | solution.py:294
  22.3 0.0 collective-permute-done.7.refs_1_
  22.3 1.1 %collective-permute-start.10 = (bf16[288,128]{1,0:T(8,128)(2,1)S(1)}, bf16[288,128]{1,0:T(8,128)(2,1)S(1)}, u32[]{:S(2)}, u32[]{:S(2)}) collective-permute-start(bf16[288,128]{1,0:T(8,128)(2,1)S(1)} %get-tuple-element.48), channel_id=1, source_target_pairs={{0,2},{1,3},{2,0},{3,1},{4,6},{5,7},{6,4},{7,5},{8,10},{9,11},{10,... | collective-permute-start | bytes 221192 | tf_op jit(solution)/shard_map/ppermute | solution.py:294
  23.4 2.5 %collective-permute-start.11 = (bf16[288,128]{1,0:T(8,128)(2,1)S(1)}, bf16[288,128]{1,0:T(8,128)(2,1)S(1)}, u32[]{:S(2)}, u32[]{:S(2)}) collective-permute-start(bf16[288,128]{1,0:T(8,128)(2,1)S(1)} %get-tuple-element.49), channel_id=1, source_target_pairs={{0,4},{1,5},{2,6},{3,7},{4,0},{5,1},{6,2},{7,3},{8,12},{9,13},{10,... | collective-permute-start | bytes 221192 | tf_op jit(solution)/shard_map/ppermute | solution.py:294
  25.9 0.9 %collective-permute-start.12 = (bf16[288,128]{1,0:T(8,128)(2,1)S(1)}, bf16[288,128]{1,0:T(8,128)(2,1)S(1)}, u32[]{:S(2)}, u32[]{:S(2)}) collective-permute-start(bf16[288,128]{1,0:T(8,128)(2,1)S(1)} %get-tuple-element.50), channel_id=1, source_target_pairs={{0,6},{1,7},{2,4},{3,5},{4,2},{5,3},{6,0},{7,1},{8,14},{9,15},{10,... | collective-permute-start | bytes 221192 | tf_op jit(solution)/shard_map/ppermute | solution.py:294
  26.8 0.0 collective-permute-done.6.other_ref
  26.8 0.8 %shard_map.116 = (bf16[32,2048]{1,0:T(8,128)(2,1)}, f32[64,128]{1,0:T(8,128)S(1)}) custom-call(f32[64,128]{1,0:T(8,128)S(1)} %get-tuple-element.29.trig_ref, f32[512,128]{1,0:T(8,128)S(1)} %get-tuple-element.38.own_ref, bf16[512,128]{1,0:T(8,128)(2,1)S(1)} %collective-permute-done.6.other_ref), custom_call_target="tpu_custom_call" | custom-call | tf_op jit(solution)/shard_map/pallas_call | solution.py:282
  27.6 0.0 collective-permute-done.10.refs_3_
  27.6 4.8 %collective-permute-done.11.refs_4_ = bf16[288,128]{1,0:T(8,128)(2,1)S(1)} collective-permute-done((bf16[288,128]{1,0:T(8,128)(2,1)S(1)}, bf16[288,128]{1,0:T(8,128)(2,1)S(1)}, u32[]{:S(2)}, u32[]{:S(2)}) %collective-permute-start.11) | collective-permute-done | bytes 73760 | tf_op jit(solution)/shard_map/ppermute | solution.py:294
  32.4 0.0 collective-permute-done.12.refs_5_
  32.4 0.7 %shard_map.118 = (bf16[32,512]{1,0:T(8,128)(2,1)}, bf16[32,512]{1,0:T(8,128)(2,1)}, f32[32,128]{1,0:T(8,128)}) custom-call(f32[64,128]{1,0:T(8,128)S(1)} %get-tuple-element.41.refs_0_, f32[256,128]{1,0:T(8,128)S(1)} %get-tuple-element.42.refs_1_, f32[32,128]{1,0:T(8,128)S(1)} %get-tuple-element.47.refs_2_, ...), custom_call_target="tpu_custom_call" | custom-call | tf_op jit(solution)/shard_map/pallas_call | solution.py:282
  (1 shorter events, 0.0 us)
Async XLA Ops:
  0.6 8.7 %copy-start = (bf16[1,32,4096]{2,1,0:T(8,128)(2,1)S(1)}, bf16[1,32,4096]{2,1,0:T(8,128)(2,1)}, u32[]{:S(2)}) copy-start(bf16[1,32,4096]{2,1,0:T(8,128)(2,1)} %param.12) | copy-start | bytes 786436
  1.9 12.1 %collective-permute-start = (bf16[1024,128]{1,0:T(8,128)(2,1)S(1)}, bf16[1024,128]{1,0:T(8,128)(2,1)S(1)}, u32[]{:S(2)}, u32[]{:S(2)}) collective-permute-start(bf16[1024,128]{1,0:T(8,128)(2,1)S(1)} %get-tuple-element.31.refs_1_.refs_3_), channel_id=1, source_target_pairs={{0,1},{1,0},{2,3},{3,2},{4,5},{5,4},{6,7},{7,6},{8,9},{9,8},{10,11... | collective-permute-start | bytes 786440 | tf_op jit(solution)/shard_map/ppermute | solution.py:294
  5.0 6.9 %collective-permute-start.3 = (bf16[256,128]{1,0:T(8,128)(2,1)S(1)}, bf16[256,128]{1,0:T(8,128)(2,1)S(1)}, u32[]{:S(2)}, u32[]{:S(2)}) collective-permute-start(bf16[256,128]{1,0:T(8,128)(2,1)S(1)} %get-tuple-element.32.refs_3_.refs_5_), channel_id=1, source_target_pairs={{0,6},{1,7},{2,4},{3,5},{4,2},{5,3},{6,0},{7,1},{8,14},{9,15},{10,... | collective-permute-start | bytes 196616 | tf_op jit(solution)/shard_map/ppermute | solution.py:294
  8.6 5.4 %collective-permute-start.2 = (bf16[256,128]{1,0:T(8,128)(2,1)S(1)}, bf16[256,128]{1,0:T(8,128)(2,1)S(1)}, u32[]{:S(2)}, u32[]{:S(2)}) collective-permute-start(bf16[256,128]{1,0:T(8,128)(2,1)S(1)} %get-tuple-element.32.refs_3_.refs_5_), channel_id=1, source_target_pairs={{0,4},{1,5},{2,6},{3,7},{4,0},{5,1},{6,2},{7,3},{8,12},{9,13},{10,... | collective-permute-start | bytes 196616 | tf_op jit(solution)/shard_map/ppermute | solution.py:294
  8.6 5.4 %collective-permute-start.1 = (bf16[256,128]{1,0:T(8,128)(2,1)S(1)}, bf16[256,128]{1,0:T(8,128)(2,1)S(1)}, u32[]{:S(2)}, u32[]{:S(2)}) collective-permute-start(bf16[256,128]{1,0:T(8,128)(2,1)S(1)} %get-tuple-element.32.refs_3_.refs_5_), channel_id=1, source_target_pairs={{0,2},{1,3},{2,0},{3,1},{4,6},{5,7},{6,4},{7,5},{8,10},{9,11},{10,... | collective-permute-start | bytes 196616 | tf_op jit(solution)/shard_map/ppermute | solution.py:294
  9.4 7.7 %collective-permute-start.5 = (bf16[32,4096]{1,0:T(8,128)(2,1)S(1)}, bf16[32,4096]{1,0:T(8,128)(2,1)S(1)}, u32[]{:S(2)}, u32[]{:S(2)}) collective-permute-start(bf16[32,4096]{1,0:T(8,128)(2,1)S(1)} %bitcast.11), channel_id=1, source_target_pairs={{0,1},{1,0},{2,3},{3,2},{4,5},{5,4},{6,7},{7,6},{8,9},{9,8},{10,11... | collective-permute-start | bytes 786440 | tf_op jit(solution)/shard_map/ppermute | solution.py:294
  14.4 3.8 %collective-permute-start.4 = (f32[16,256]{1,0:T(8,128)S(1)}, f32[16,256]{1,0:T(8,128)S(1)}, u32[]{:S(2)}, u32[]{:S(2)}) collective-permute-start(f32[16,256]{1,0:T(8,128)S(1)} %get-tuple-element.33.own_ref), channel_id=1, source_target_pairs={{0,1},{1,0},{2,3},{3,2},{4,5},{5,4},{6,7},{7,6},{8,9},{9,8},{10,11... | collective-permute-start | bytes 49160 | tf_op jit(solution)/shard_map/ppermute | solution.py:294
  18.4 3.4 %collective-permute-start.9 = (f32[32,128]{1,0:T(8,128)S(1)}, f32[32,128]{1,0:T(8,128)S(1)}, u32[]{:S(2)}, u32[]{:S(2)}) collective-permute-start(f32[32,128]{1,0:T(8,128)S(1)} %get-tuple-element.43.refs_0_), channel_id=1, source_target_pairs={{0,24},{8,16},{16,8},{24,0},{1,25},{9,17},{17,9},{25,1},{2,26},{10... | collective-permute-start | bytes 49160 | tf_op jit(solution)/shard_map/ppermute | solution.py:294
  18.5 3.8 %collective-permute-start.8 = (f32[32,128]{1,0:T(8,128)S(1)}, f32[32,128]{1,0:T(8,128)S(1)}, u32[]{:S(2)}, u32[]{:S(2)}) collective-permute-start(f32[32,128]{1,0:T(8,128)S(1)} %get-tuple-element.43.refs_0_), channel_id=1, source_target_pairs={{0,16},{8,24},{16,0},{24,8},{1,17},{9,25},{17,1},{25,9},{2,18},{10... | collective-permute-start | bytes 49160 | tf_op jit(solution)/shard_map/ppermute | solution.py:294
  20.1 2.2 %collective-permute-start.7 = (f32[32,128]{1,0:T(8,128)S(1)}, f32[32,128]{1,0:T(8,128)S(1)}, u32[]{:S(2)}, u32[]{:S(2)}) collective-permute-start(f32[32,128]{1,0:T(8,128)S(1)} %get-tuple-element.43.refs_0_), channel_id=1, source_target_pairs={{0,8},{8,0},{16,24},{24,16},{1,9},{9,1},{17,25},{25,17},{2,10},{10... | collective-permute-start | bytes 49160 | tf_op jit(solution)/shard_map/ppermute | solution.py:294
  20.8 6.1 %collective-permute-start.6 = (bf16[512,128]{1,0:T(8,128)(2,1)S(1)}, bf16[512,128]{1,0:T(8,128)(2,1)S(1)}, u32[]{:S(2)}, u32[]{:S(2)}) collective-permute-start(bf16[512,128]{1,0:T(8,128)(2,1)S(1)} %get-tuple-element.39), channel_id=1, source_target_pairs={{0,1},{1,0},{2,3},{3,2},{4,5},{5,4},{6,7},{7,6},{8,9},{9,8},{10,11... | collective-permute-start | bytes 393224 | tf_op jit(solution)/shard_map/ppermute | solution.py:294
  22.3 5.3 %collective-permute-start.10 = (bf16[288,128]{1,0:T(8,128)(2,1)S(1)}, bf16[288,128]{1,0:T(8,128)(2,1)S(1)}, u32[]{:S(2)}, u32[]{:S(2)}) collective-permute-start(bf16[288,128]{1,0:T(8,128)(2,1)S(1)} %get-tuple-element.48), channel_id=1, source_target_pairs={{0,2},{1,3},{2,0},{3,1},{4,6},{5,7},{6,4},{7,5},{8,10},{9,11},{10,... | collective-permute-start | bytes 221192 | tf_op jit(solution)/shard_map/ppermute | solution.py:294
  23.4 9.0 %collective-permute-start.11 = (bf16[288,128]{1,0:T(8,128)(2,1)S(1)}, bf16[288,128]{1,0:T(8,128)(2,1)S(1)}, u32[]{:S(2)}, u32[]{:S(2)}) collective-permute-start(bf16[288,128]{1,0:T(8,128)(2,1)S(1)} %get-tuple-element.49), channel_id=1, source_target_pairs={{0,4},{1,5},{2,6},{3,7},{4,0},{5,1},{6,2},{7,3},{8,12},{9,13},{10,... | collective-permute-start | bytes 221192 | tf_op jit(solution)/shard_map/ppermute | solution.py:294
  25.9 6.5 %collective-permute-start.12 = (bf16[288,128]{1,0:T(8,128)(2,1)S(1)}, bf16[288,128]{1,0:T(8,128)(2,1)S(1)}, u32[]{:S(2)}, u32[]{:S(2)}) collective-permute-start(bf16[288,128]{1,0:T(8,128)(2,1)S(1)} %get-tuple-element.50), channel_id=1, source_target_pairs={{0,6},{1,7},{2,4},{3,5},{4,2},{5,3},{6,0},{7,1},{8,14},{9,15},{10,... | collective-permute-start | bytes 221192 | tf_op jit(solution)/shard_map/ppermute | solution.py:294

commit v2 on v1

--- a/solution.py
+++ b/solution.py
@@ -18,7 +18,8 @@
 VMEM_LIMIT = 32 * 1024 * 1024
 SCORES_COST = 20 * 10**9
 TERMS_COST = 20 * 10**9
-RIDE_COST = 20 * 10**9
+ROUTER_COSTS = (20 * 10**9, 1)
+QUERY_COST = 1
 
 
 def rope_table():
@@ -167,7 +168,9 @@
     )
 
 
-def combine_kernel(own_ref, other_ref, input_ref, input_other_ref, coef_out, router_out):
+def combine_kernel(
+    own_ref, other_ref, input_ref, input_other_ref, coef_out, router_out, send_out
+):
     slots = input_ref.shape[0]
     rows = GROUP * slots
     mine = own_ref[...]
@@ -195,6 +198,7 @@
             axis=0,
             keepdims=True,
         )
+    send_out[...] = router_out[...].astype(jnp.bfloat16)
 
 
 def terms_kernel(slots, half, *refs):
@@ -228,18 +232,11 @@
         query_send[rows_of(number, rows), :] = query_term[rows:].astype(jnp.bfloat16)
 
 
-def ride_kernel(groups, *refs):
-    router_refs = refs[:groups]
-    count = (len(refs) - groups - 1) // 2
-    term_refs = refs[groups : groups + count]
-    router_out = refs[groups + count]
-    router = router_refs[0][...]
-    for ref in router_refs[1:]:
-        router += ref[...]
-    router_out[...] = router
-    for term, out in zip(term_refs, refs[groups + count + 1 :]):
-        out[0 : term.shape[0], :] = term[...]
-        out[term.shape[0] :, :] = router.astype(jnp.bfloat16)
+def router_kernel(*refs):
+    total = refs[0][...]
+    for ref in refs[1:-1]:
+        total += ref[...].astype(jnp.float32)
+    refs[-1][...] = total
 
 
 def query_kernel(trig_ref, own_ref, other_ref, query_out, trig_out):
@@ -254,8 +251,8 @@
 
 
 def final_kernel(router_scale, *refs):
-    trig_ref, own_ref, router_ref = refs[:3]
-    term_refs = refs[3:-3]
+    trig_ref, own_ref, router_ref, router_other_ref = refs[:4]
+    term_refs = refs[4:-3]
     key_out, value_out, router_out = refs[-3:]
     slots = key_out.shape[0]
     cosine = trig_ref[0:slots, :]
@@ -269,10 +266,7 @@
             key_out[:, head(number)] = turn(total, cosine, -sine).astype(jnp.bfloat16)
         else:
             value_out[:, head(number - KVH)] = total.astype(jnp.bfloat16)
-    router = router_ref[...]
-    for ref in term_refs:
-        router += ref[2 * KVH * slots :, :].astype(jnp.float32)
-    router_out[...] = router * router_scale
+    router_out[...] = (router_ref[...] + router_other_ref[...]) * router_scale
 
 
 def call(kernel, outs, args, fetched=(), scratch=(), cost=None):
@@ -342,13 +336,13 @@
         [gate, query, query_other, *pairs],
         cost=SCORES_COST,
     )
-    coef, router = call(
+    coef, router, router_send = call(
         combine_kernel,
-        [near((2 * KVH, 2 * rows), f32), near((lines, HD), f32)],
+        [near((2 * KVH, 2 * rows), f32), near((lines, HD), f32), near((lines, HD), bf16)],
         [stats, swap(stats), inputs, inputs_other],
     )
     routers = [router] + [
-        exchange(router, "dp", step, groups) for step in range(1, groups)
+        exchange(router_send, "ctx", 2 * step, count) for step in reversed(range(1, half))
     ]
     query_own, query_send, term_own, *terms = call(
         functools.partial(terms_kernel, slots, half),
@@ -362,23 +356,23 @@
         cost=TERMS_COST,
     )
     query_back = swap(query_send)
-    router, *terms = call(
-        functools.partial(ride_kernel, groups),
-        [near((lines, HD), f32)] + [near((2 * KVH * slots + lines, HD), bf16)] * (half - 1),
-        [*routers, *terms],
-        cost=RIDE_COST,
-    )
-    terms = [exchange(term, "ctx", 2 * step, count) for step, term in enumerate(terms, 1)]
+    terms = [
+        exchange(terms[step - 1], "ctx", 2 * step, count) for step in reversed(range(1, half))
+    ]
+    for bit in range(groups.bit_length() - 1):
+        (router,) = call(router_kernel, [near((lines, HD), f32)], routers, cost=ROUTER_COSTS[bit > 0])
+        routers = [router, exchange(router, "dp", 1 << bit, groups)]
     shape = jax.ShapeDtypeStruct
     query_grad, trig = call(
         query_kernel,
         [shape((slots, HQ * HD), bf16), near((2 * slots, HD), f32)],
         [trig, query_own, query_back],
+        cost=QUERY_COST,
     )
     key_grad, value_grad, router_grad = call(
         functools.partial(final_kernel, 1.0 / math.sqrt(groups * count * slots)),
         [shape((slots, KVH * HD), bf16), shape((slots, KVH * HD), bf16), shape((lines, HD), f32)],
-        [trig, term_own, router, *terms],
+        [trig, term_own, *routers, *terms],
     )
     return (query_grad[None], key_grad[None], value_grad[None], router_grad.reshape(width))
 

time: 33.4 us -> 34.5 us (1.033)
  starting transfers between devices: 15.4 us -> 19.4 us
  waiting for transfers between devices: 12 us -> 9.17 us
    ppermute x13 -> x15, starting transfers between devices: 15.4 us -> 19.4 us  [exchange(): return lax.ppermute(array, axis, [(at, at ^ step) for at in range(size)])]
    ppermute x13 -> x15, waiting for transfers between devices: 12 us -> 9.17 us  [exchange(): return lax.ppermute(array, axis, [(at, at ^ step) for at in range(size)])]
    pallas_call x8 -> x9, Pallas kernels: 4.97 us -> 4.95 us  [call(): pl.pallas_call(kernel, out_shape=outs, in_specs=[local] * len(args) + [di...]
  transfers between devices with their start and end apart: 13 -> 15, of which waited for: 8 -> 7; matrix products, arithmetic and copies ran while one was open for 0% -> 0% of each run, Pallas kernels for 8% -> 8%
where the time goes in v2:
time: 34.5 us; the launch traced here: 34.3 us
  starting transfers between devices  19.4 us (56%)
  waiting for transfers between devices  9.17 us (27%)
  Pallas kernels  4.95 us (14%)
  between operations  0.7 us (2%)
    ppermute x15, starting transfers between devices, exchange(): return lax.ppermute(array, axis, [(at, at ^ step) for at in range(size)])  19.4 us
    ppermute x15, waiting for transfers between devices, exchange(): return lax.ppermute(array, axis, [(at, at ^ step) for at in range(size)])  9.17 us
    pallas_call x9, Pallas kernels, call(): pl.pallas_call(kernel, out_shape=outs, in_specs=[local] * len(args) + [di...  4.95 us
  transfers between devices with their start and end apart: 15, of which 7 were waited for; matrix products, arithmetic and copies ran while one was open for 0% of the time, Pallas kernels for 8%

profile of v2, /device:TPU:0, one launch (start us, length us, event | category | flops | bytes accessed | tf_op | source)
XLA Modules:
  0.0 34.3 jit_solution(6835999200275906475)
XLA Ops:
  0.6 0.0 copy-start
  0.6 1.3 %shard_map.111 = (bf16[256,128]{1,0:T(8,128)(2,1)S(1)}, bf16[1024,128]{1,0:T(8,128)(2,1)S(1)}, f32[64,128]{1,0:T(8,128)S(1)}) custom-call(s32[1,32]{1,0:T(1,128)} %refs_0_.1, f32[2,128]{1,0:T(2,128)} %constant.2.clone.refs_1_, bf16[32,512]{1,0:T(8,128)(2,1)} %bitcast.14, bf16[32,512]{1,0:T(8,128)(2,1)} %bitcast.15, bf16[32,2048]{1,0:T(8,128)(2,1)} %bitcast.12, ...), custom_call_target="tpu_custom_call" | custom-call | tf_op jit(solution)/shard_map/pallas_call | solution.py:276
  1.9 3.0 %collective-permute-start = (bf16[1024,128]{1,0:T(8,128)(2,1)S(1)}, bf16[1024,128]{1,0:T(8,128)(2,1)S(1)}, u32[]{:S(2)}, u32[]{:S(2)}) collective-permute-start(bf16[1024,128]{1,0:T(8,128)(2,1)S(1)} %get-tuple-element.28.refs_1_.refs_3_), channel_id=1, source_target_pairs={{0,1},{1,0},{2,3},{3,2},{4,5},{5,4},{6,7},{7,6},{8,9},{9,8},{10,11... | collective-permute-start | bytes 786440 | tf_op jit(solution)/shard_map/ppermute | solution.py:288
  5.0 3.6 %collective-permute-start.3 = (bf16[256,128]{1,0:T(8,128)(2,1)S(1)}, bf16[256,128]{1,0:T(8,128)(2,1)S(1)}, u32[]{:S(2)}, u32[]{:S(2)}) collective-permute-start(bf16[256,128]{1,0:T(8,128)(2,1)S(1)} %get-tuple-element.29.refs_3_.refs_5_), channel_id=1, source_target_pairs={{0,6},{1,7},{2,4},{3,5},{4,2},{5,3},{6,0},{7,1},{8,14},{9,15},{10,... | collective-permute-start | bytes 196616 | tf_op jit(solution)/shard_map/ppermute | solution.py:288
  8.6 0.0 collective-permute-start.2
  8.6 0.8 %collective-permute-start.1 = (bf16[256,128]{1,0:T(8,128)(2,1)S(1)}, bf16[256,128]{1,0:T(8,128)(2,1)S(1)}, u32[]{:S(2)}, u32[]{:S(2)}) collective-permute-start(bf16[256,128]{1,0:T(8,128)(2,1)S(1)} %get-tuple-element.29.refs_3_.refs_5_), channel_id=1, source_target_pairs={{0,2},{1,3},{2,0},{3,1},{4,6},{5,7},{6,4},{7,5},{8,10},{9,11},{10,... | collective-permute-start | bytes 196616 | tf_op jit(solution)/shard_map/ppermute | solution.py:288
  9.4 0.0 copy-done
  9.4 0.3 collective-permute-start.5
  9.6 1.1 %shard_map.112 = (f32[8,128]{1,0:T(8,128)S(1)}, bf16[32,4096]{1,0:T(8,128)(2,1)S(1)}) custom-call(f32[32,128]{1,0:T(8,128)} %bitcast.16, bf16[32,4096]{1,0:T(8,128)(2,1)} %bitcast.10), custom_call_target="tpu_custom_call" | custom-call | tf_op jit(solution)/shard_map/pallas_call | solution.py:276
  10.8 1.0 %collective-permute-done.3.refs_6_.refs_8_ = bf16[256,128]{1,0:T(8,128)(2,1)S(1)} collective-permute-done((bf16[256,128]{1,0:T(8,128)(2,1)S(1)}, bf16[256,128]{1,0:T(8,128)(2,1)S(1)}, u32[]{:S(2)}, u32[]{:S(2)}) %collective-permute-start.3) | collective-permute-done | bytes 65568 | tf_op jit(solution)/shard_map/ppermute | solution.py:288
  11.8 2.1 %collective-permute-done.2.refs_5_.refs_7_ = bf16[256,128]{1,0:T(8,128)(2,1)S(1)} collective-permute-done((bf16[256,128]{1,0:T(8,128)(2,1)S(1)}, bf16[256,128]{1,0:T(8,128)(2,1)S(1)}, u32[]{:S(2)}, u32[]{:S(2)}) %collective-permute-start.2) | collective-permute-done | bytes 65568 | tf_op jit(solution)/shard_map/ppermute | solution.py:288
  13.9 0.1 collective-permute-done.1.refs_4_.refs_6_
  14.0 0.0 collective-permute-done.refs_2_.refs_4_
  14.0 0.4 %shard_map.113 = (f32[4,128,256]{2,1,0:T(8,128)S(1)}, f32[4,128,256]{2,1,0:T(8,128)S(1)}, f32[16,256]{1,0:T(8,128)S(1)}) custom-call(f32[8,128]{1,0:T(8,128)S(1)} %get-tuple-element.27.refs_0_, bf16[1024,128]{1,0:T(8,128)(2,1)S(1)} %get-tuple-element.28.refs_1_.refs_3_, bf16[1024,128]{1,0:T(8,128)(2,1)S(1)} %collective-permute-done.refs_2_.refs_4_, ...), custom_call_target="tpu_custom_call" | custom-call | flops 20000000000 | tf_op jit(solution)/shard_map/pallas_call | solution.py:276
  14.4 0.5 %collective-permute-start.4 = (f32[16,256]{1,0:T(8,128)S(1)}, f32[16,256]{1,0:T(8,128)S(1)}, u32[]{:S(2)}, u32[]{:S(2)}) collective-permute-start(f32[16,256]{1,0:T(8,128)S(1)} %get-tuple-element.30.own_ref), channel_id=1, source_target_pairs={{0,1},{1,0},{2,3},{3,2},{4,5},{5,4},{6,7},{7,6},{8,9},{9,8},{10,11... | collective-permute-start | bytes 49160 | tf_op jit(solution)/shard_map/ppermute | solution.py:288
  14.9 2.2 %collective-permute-done.5.input_other_ref = bf16[32,4096]{1,0:T(8,128)(2,1)S(1)} collective-permute-done((bf16[32,4096]{1,0:T(8,128)(2,1)S(1)}, bf16[32,4096]{1,0:T(8,128)(2,1)S(1)}, u32[]{:S(2)}, u32[]{:S(2)}) %collective-permute-start.5) | collective-permute-done | bytes 262176 | tf_op jit(solution)/shard_map/ppermute | solution.py:288
  17.1 1.1 %collective-permute-done.4.other_ref = f32[16,256]{1,0:T(8,128)S(1)} collective-permute-done((f32[16,256]{1,0:T(8,128)S(1)}, f32[16,256]{1,0:T(8,128)S(1)}, u32[]{:S(2)}, u32[]{:S(2)}) %collective-permute-start.4) | collective-permute-done | bytes 16416 | tf_op jit(solution)/shard_map/ppermute | solution.py:288
  18.2 0.2 shard_map.114
  18.4 1.0 %collective-permute-start.9 = (bf16[32,128]{1,0:T(8,128)(2,1)S(1)}, bf16[32,128]{1,0:T(8,128)(2,1)S(1)}, u32[]{:S(2)}, u32[]{:S(2)}) collective-permute-start(bf16[32,128]{1,0:T(8,128)(2,1)S(1)} %get-tuple-element.41), channel_id=1, source_target_pairs={{0,2},{1,3},{2,0},{3,1},{4,6},{5,7},{6,4},{7,5},{8,10},{9,11},{10,... | collective-permute-start | bytes 24584 | tf_op jit(solution)/shard_map/ppermute | solution.py:288
  19.5 2.5 %collective-permute-start.8 = (bf16[32,128]{1,0:T(8,128)(2,1)S(1)}, bf16[32,128]{1,0:T(8,128)(2,1)S(1)}, u32[]{:S(2)}, u32[]{:S(2)}) collective-permute-start(bf16[32,128]{1,0:T(8,128)(2,1)S(1)} %get-tuple-element.41), channel_id=1, source_target_pairs={{0,4},{1,5},{2,6},{3,7},{4,0},{5,1},{6,2},{7,3},{8,12},{9,13},{10,... | collective-permute-start | bytes 24584 | tf_op jit(solution)/shard_map/ppermute | solution.py:288
  21.9 1.0 %collective-permute-start.7 = (bf16[32,128]{1,0:T(8,128)(2,1)S(1)}, bf16[32,128]{1,0:T(8,128)(2,1)S(1)}, u32[]{:S(2)}, u32[]{:S(2)}) collective-permute-start(bf16[32,128]{1,0:T(8,128)(2,1)S(1)} %get-tuple-element.41), channel_id=1, source_target_pairs={{0,6},{1,7},{2,4},{3,5},{4,2},{5,3},{6,0},{7,1},{8,14},{9,15},{10,... | collective-permute-start | bytes 24584 | tf_op jit(solution)/shard_map/ppermute | solution.py:288
  22.9 0.4 %shard_map.115 = (f32[512,128]{1,0:T(8,128)S(1)}, bf16[512,128]{1,0:T(8,128)(2,1)S(1)}, f32[256,128]{1,0:T(8,128)S(1)}, bf16[256,128]{1,0:T(8,128)(2,1)S(1)}, bf...) custom-call(f32[8,256]{1,0:T(8,128)S(1)} %get-tuple-element.32.refs_0_, ...), custom_call_target="tpu_custom_call" | custom-call | flops 20000000000 | tf_op jit(solution)/shard_map/pallas_call | solution.py:276
  23.3 2.9 %collective-permute-start.12 = (bf16[256,128]{1,0:T(8,128)(2,1)S(1)}, bf16[256,128]{1,0:T(8,128)(2,1)S(1)}, u32[]{:S(2)}, u32[]{:S(2)}) collective-permute-start(bf16[256,128]{1,0:T(8,128)(2,1)S(1)} %get-tuple-element.42), channel_id=1, source_target_pairs={{0,6},{1,7},{2,4},{3,5},{4,2},{5,3},{6,0},{7,1},{8,14},{9,15},{10,... | collective-permute-start | bytes 196616 | tf_op jit(solution)/shard_map/ppermute | solution.py:288
  26.2 0.0 collective-permute-start.13
  26.2 0.0 collective-permute-done.9.refs_3_
  26.2 1.5 %collective-permute-start.14 = (bf16[256,128]{1,0:T(8,128)(2,1)S(1)}, bf16[256,128]{1,0:T(8,128)(2,1)S(1)}, u32[]{:S(2)}, u32[]{:S(2)}) collective-permute-start(bf16[256,128]{1,0:T(8,128)(2,1)S(1)} %get-tuple-element.44), channel_id=1, source_target_pairs={{0,2},{1,3},{2,0},{3,1},{4,6},{5,7},{6,4},{7,5},{8,10},{9,11},{10,... | collective-permute-start | bytes 196616 | tf_op jit(solution)/shard_map/ppermute | solution.py:288
  27.7 0.0 collective-permute-done.8.refs_2_
  27.7 0.8 %collective-permute-start.6 = (bf16[512,128]{1,0:T(8,128)(2,1)S(1)}, bf16[512,128]{1,0:T(8,128)(2,1)S(1)}, u32[]{:S(2)}, u32[]{:S(2)}) collective-permute-start(bf16[512,128]{1,0:T(8,128)(2,1)S(1)} %get-tuple-element.36), channel_id=1, source_target_pairs={{0,1},{1,0},{2,3},{3,2},{4,5},{5,4},{6,7},{7,6},{8,9},{9,8},{10,11... | collective-permute-start | bytes 393224 | tf_op jit(solution)/shard_map/ppermute | solution.py:288
  28.5 0.0 collective-permute-done.7.refs_1_
  28.5 0.1 collective-permute-start.10
  28.6 1.2 %collective-permute-done.10.refs_1_ = f32[32,128]{1,0:T(8,128)S(1)} collective-permute-done((f32[32,128]{1,0:T(8,128)S(1)}, f32[32,128]{1,0:T(8,128)S(1)}, u32[]{:S(2)}, u32[]{:S(2)}) %collective-permute-start.10) | collective-permute-done | bytes 16416 | tf_op jit(solution)/shard_map/ppermute | solution.py:288
  29.8 1.5 %collective-permute-start.11 = (f32[32,128]{1,0:T(8,128)S(1)}, f32[32,128]{1,0:T(8,128)S(1)}, u32[]{:S(2)}, u32[]{:S(2)}) collective-permute-start(f32[32,128]{1,0:T(8,128)S(1)} %shard_map.118.refs_2_), channel_id=1, source_target_pairs={{0,16},{8,24},{16,0},{24,8},{1,17},{9,25},{17,1},{25,9},{2,18},{10... | collective-permute-start | bytes 49160 | tf_op jit(solution)/shard_map/ppermute | solution.py:288
  31.3 1.4 %collective-permute-done.6.other_ref = bf16[512,128]{1,0:T(8,128)(2,1)S(1)} collective-permute-done((bf16[512,128]{1,0:T(8,128)(2,1)S(1)}, bf16[512,128]{1,0:T(8,128)(2,1)S(1)}, u32[]{:S(2)}, u32[]{:S(2)}) %collective-permute-start.6) | collective-permute-done | bytes 131104 | tf_op jit(solution)/shard_map/ppermute | solution.py:288
  32.7 0.8 %shard_map.116 = (bf16[32,2048]{1,0:T(8,128)(2,1)}, f32[64,128]{1,0:T(8,128)S(1)}) custom-call(f32[64,128]{1,0:T(8,128)S(1)} %get-tuple-element.26.trig_ref, f32[512,128]{1,0:T(8,128)S(1)} %get-tuple-element.35.own_ref, bf16[512,128]{1,0:T(8,128)(2,1)S(1)} %collective-permute-done.6.other_ref), custom_call_target="tpu_custom_call" | custom-call | flops 1 | tf_op jit(solution)/shard_map/pallas_call | solution.py:276
  33.5 0.0 collective-permute-done.11.refs_3_
  33.5 0.0 collective-permute-done.12.refs_4_
  33.5 0.0 collective-permute-done.13.refs_5_
  33.5 0.0 collective-permute-done.14.refs_6_
  33.5 0.7 %shard_map.119 = (bf16[32,512]{1,0:T(8,128)(2,1)}, bf16[32,512]{1,0:T(8,128)(2,1)}, f32[32,128]{1,0:T(8,128)}) custom-call(f32[64,128]{1,0:T(8,128)S(1)} %get-tuple-element.38.refs_0_, f32[256,128]{1,0:T(8,128)S(1)} %get-tuple-element.39.refs_1_, f32[32,128]{1,0:T(8,128)S(1)} %shard_map.118.refs_2_, f32[32,128]{1,0:T(8,128)S(1)} %collective-permute-done.11.refs_3_, ...), custom_call_target="tpu_custom_call" | custom-call | tf_op jit(solution)/shard_map/pallas_call | solution.py:276
  (2 shorter events, 0.0 us)
Async XLA Ops:
  0.6 8.7 %copy-start = (bf16[1,32,4096]{2,1,0:T(8,128)(2,1)S(1)}, bf16[1,32,4096]{2,1,0:T(8,128)(2,1)}, u32[]{:S(2)}) copy-start(bf16[1,32,4096]{2,1,0:T(8,128)(2,1)} %param.12) | copy-start | bytes 786436
  1.9 12.1 %collective-permute-start = (bf16[1024,128]{1,0:T(8,128)(2,1)S(1)}, bf16[1024,128]{1,0:T(8,128)(2,1)S(1)}, u32[]{:S(2)}, u32[]{:S(2)}) collective-permute-start(bf16[1024,128]{1,0:T(8,128)(2,1)S(1)} %get-tuple-element.28.refs_1_.refs_3_), channel_id=1, source_target_pairs={{0,1},{1,0},{2,3},{3,2},{4,5},{5,4},{6,7},{7,6},{8,9},{9,8},{10,11... | collective-permute-start | bytes 786440 | tf_op jit(solution)/shard_map/ppermute | solution.py:288
  5.0 6.9 %collective-permute-start.3 = (bf16[256,128]{1,0:T(8,128)(2,1)S(1)}, bf16[256,128]{1,0:T(8,128)(2,1)S(1)}, u32[]{:S(2)}, u32[]{:S(2)}) collective-permute-start(bf16[256,128]{1,0:T(8,128)(2,1)S(1)} %get-tuple-element.29.refs_3_.refs_5_), channel_id=1, source_target_pairs={{0,6},{1,7},{2,4},{3,5},{4,2},{5,3},{6,0},{7,1},{8,14},{9,15},{10,... | collective-permute-start | bytes 196616 | tf_op jit(solution)/shard_map/ppermute | solution.py:288
  8.6 5.4 %collective-permute-start.2 = (bf16[256,128]{1,0:T(8,128)(2,1)S(1)}, bf16[256,128]{1,0:T(8,128)(2,1)S(1)}, u32[]{:S(2)}, u32[]{:S(2)}) collective-permute-start(bf16[256,128]{1,0:T(8,128)(2,1)S(1)} %get-tuple-element.29.refs_3_.refs_5_), channel_id=1, source_target_pairs={{0,4},{1,5},{2,6},{3,7},{4,0},{5,1},{6,2},{7,3},{8,12},{9,13},{10,... | collective-permute-start | bytes 196616 | tf_op jit(solution)/shard_map/ppermute | solution.py:288
  8.6 5.4 %collective-permute-start.1 = (bf16[256,128]{1,0:T(8,128)(2,1)S(1)}, bf16[256,128]{1,0:T(8,128)(2,1)S(1)}, u32[]{:S(2)}, u32[]{:S(2)}) collective-permute-start(bf16[256,128]{1,0:T(8,128)(2,1)S(1)} %get-tuple-element.29.refs_3_.refs_5_), channel_id=1, source_target_pairs={{0,2},{1,3},{2,0},{3,1},{4,6},{5,7},{6,4},{7,5},{8,10},{9,11},{10,... | collective-permute-start | bytes 196616 | tf_op jit(solution)/shard_map/ppermute | solution.py:288
  9.4 7.7 %collective-permute-start.5 = (bf16[32,4096]{1,0:T(8,128)(2,1)S(1)}, bf16[32,4096]{1,0:T(8,128)(2,1)S(1)}, u32[]{:S(2)}, u32[]{:S(2)}) collective-permute-start(bf16[32,4096]{1,0:T(8,128)(2,1)S(1)} %bitcast.11), channel_id=1, source_target_pairs={{0,1},{1,0},{2,3},{3,2},{4,5},{5,4},{6,7},{7,6},{8,9},{9,8},{10,11... | collective-permute-start | bytes 786440 | tf_op jit(solution)/shard_map/ppermute | solution.py:288
  14.4 3.8 %collective-permute-start.4 = (f32[16,256]{1,0:T(8,128)S(1)}, f32[16,256]{1,0:T(8,128)S(1)}, u32[]{:S(2)}, u32[]{:S(2)}) collective-permute-start(f32[16,256]{1,0:T(8,128)S(1)} %get-tuple-element.30.own_ref), channel_id=1, source_target_pairs={{0,1},{1,0},{2,3},{3,2},{4,5},{5,4},{6,7},{7,6},{8,9},{9,8},{10,11... | collective-permute-start | bytes 49160 | tf_op jit(solution)/shard_map/ppermute | solution.py:288
  18.4 7.8 %collective-permute-start.9 = (bf16[32,128]{1,0:T(8,128)(2,1)S(1)}, bf16[32,128]{1,0:T(8,128)(2,1)S(1)}, u32[]{:S(2)}, u32[]{:S(2)}) collective-permute-start(bf16[32,128]{1,0:T(8,128)(2,1)S(1)} %get-tuple-element.41), channel_id=1, source_target_pairs={{0,2},{1,3},{2,0},{3,1},{4,6},{5,7},{6,4},{7,5},{8,10},{9,11},{10,... | collective-permute-start | bytes 24584 | tf_op jit(solution)/shard_map/ppermute | solution.py:288
  19.5 8.3 %collective-permute-start.8 = (bf16[32,128]{1,0:T(8,128)(2,1)S(1)}, bf16[32,128]{1,0:T(8,128)(2,1)S(1)}, u32[]{:S(2)}, u32[]{:S(2)}) collective-permute-start(bf16[32,128]{1,0:T(8,128)(2,1)S(1)} %get-tuple-element.41), channel_id=1, source_target_pairs={{0,4},{1,5},{2,6},{3,7},{4,0},{5,1},{6,2},{7,3},{8,12},{9,13},{10,... | collective-permute-start | bytes 24584 | tf_op jit(solution)/shard_map/ppermute | solution.py:288
  21.9 6.6 %collective-permute-start.7 = (bf16[32,128]{1,0:T(8,128)(2,1)S(1)}, bf16[32,128]{1,0:T(8,128)(2,1)S(1)}, u32[]{:S(2)}, u32[]{:S(2)}) collective-permute-start(bf16[32,128]{1,0:T(8,128)(2,1)S(1)} %get-tuple-element.41), channel_id=1, source_target_pairs={{0,6},{1,7},{2,4},{3,5},{4,2},{5,3},{6,0},{7,1},{8,14},{9,15},{10,... | collective-permute-start | bytes 24584 | tf_op jit(solution)/shard_map/ppermute | solution.py:288
  23.3 10.3 %collective-permute-start.12 = (bf16[256,128]{1,0:T(8,128)(2,1)S(1)}, bf16[256,128]{1,0:T(8,128)(2,1)S(1)}, u32[]{:S(2)}, u32[]{:S(2)}) collective-permute-start(bf16[256,128]{1,0:T(8,128)(2,1)S(1)} %get-tuple-element.42), channel_id=1, source_target_pairs={{0,6},{1,7},{2,4},{3,5},{4,2},{5,3},{6,0},{7,1},{8,14},{9,15},{10,... | collective-permute-start | bytes 196616 | tf_op jit(solution)/shard_map/ppermute | solution.py:288
  26.2 7.3 %collective-permute-start.13 = (bf16[256,128]{1,0:T(8,128)(2,1)S(1)}, bf16[256,128]{1,0:T(8,128)(2,1)S(1)}, u32[]{:S(2)}, u32[]{:S(2)}) collective-permute-start(bf16[256,128]{1,0:T(8,128)(2,1)S(1)} %get-tuple-element.43), channel_id=1, source_target_pairs={{0,4},{1,5},{2,6},{3,7},{4,0},{5,1},{6,2},{7,3},{8,12},{9,13},{10,... | collective-permute-start | bytes 196616 | tf_op jit(solution)/shard_map/ppermute | solution.py:288
  26.2 7.3 %collective-permute-start.14 = (bf16[256,128]{1,0:T(8,128)(2,1)S(1)}, bf16[256,128]{1,0:T(8,128)(2,1)S(1)}, u32[]{:S(2)}, u32[]{:S(2)}) collective-permute-start(bf16[256,128]{1,0:T(8,128)(2,1)S(1)} %get-tuple-element.44), channel_id=1, source_target_pairs={{0,2},{1,3},{2,0},{3,1},{4,6},{5,7},{6,4},{7,5},{8,10},{9,11},{10,... | collective-permute-start | bytes 196616 | tf_op jit(solution)/shard_map/ppermute | solution.py:288
  27.7 5.0 %collective-permute-start.6 = (bf16[512,128]{1,0:T(8,128)(2,1)S(1)}, bf16[512,128]{1,0:T(8,128)(2,1)S(1)}, u32[]{:S(2)}, u32[]{:S(2)}) collective-permute-start(bf16[512,128]{1,0:T(8,128)(2,1)S(1)} %get-tuple-element.36), channel_id=1, source_target_pairs={{0,1},{1,0},{2,3},{3,2},{4,5},{5,4},{6,7},{7,6},{8,9},{9,8},{10,11... | collective-permute-start | bytes 393224 | tf_op jit(solution)/shard_map/ppermute | solution.py:288
  28.5 1.2 %collective-permute-start.10 = (f32[32,128]{1,0:T(8,128)S(1)}, f32[32,128]{1,0:T(8,128)S(1)}, u32[]{:S(2)}, u32[]{:S(2)}) collective-permute-start(f32[32,128]{1,0:T(8,128)S(1)} %shard_map.117.refs_0_), channel_id=1, source_target_pairs={{0,8},{8,0},{16,24},{24,16},{1,9},{9,1},{17,25},{25,17},{2,10},{10... | collective-permute-start | bytes 49160 | tf_op jit(solution)/shard_map/ppermute | solution.py:288
  29.8 3.7 %collective-permute-start.11 = (f32[32,128]{1,0:T(8,128)S(1)}, f32[32,128]{1,0:T(8,128)S(1)}, u32[]{:S(2)}, u32[]{:S(2)}) collective-permute-start(f32[32,128]{1,0:T(8,128)S(1)} %shard_map.118.refs_2_), channel_id=1, source_target_pairs={{0,16},{8,24},{16,0},{24,8},{1,17},{9,25},{17,1},{25,9},{2,18},{10... | collective-permute-start | bytes 49160 | tf_op jit(solution)/shard_map/ppermute | solution.py:288

commit v3 on v1

--- a/solution.py
+++ b/solution.py
@@ -75,10 +75,11 @@
     lower = jnp.sum(jnp.where(same, lower, 0.0), axis=1, keepdims=True)
     copies[1].wait()
     angles = upper * table_ref[0:1, :] + lower * table_ref[1:2, :]
-    cosine = jnp.cos(angles)
-    lane = lax.broadcasted_iota(jnp.int32, angles.shape, 1)
-    sine = jnp.sin(angles)
-    sine = jnp.where(lane < HD // 2, -sine, sine)
+    low = lax.broadcasted_iota(jnp.int32, angles.shape, 1) < HD // 2
+    mixed = jnp.cos(jnp.where(low, angles, angles - 0.5 * math.pi))
+    turned = pltpu.roll(mixed, HD // 2, 1)
+    cosine = jnp.where(low, mixed, turned)
+    sine = jnp.where(low, -turned, mixed)
     trig_ref[0:slots, :] = cosine
     trig_ref[slots : 2 * slots, :] = sine
     for copy in copies[2:]:
@@ -368,7 +369,9 @@
         [*routers, *terms],
         cost=RIDE_COST,
     )
-    terms = [exchange(term, "ctx", 2 * step, count) for step, term in enumerate(terms, 1)]
+    terms = [
+        exchange(terms[step - 1], "ctx", 2 * step, count) for step in reversed(range(1, half))
+    ]
     shape = jax.ShapeDtypeStruct
     query_grad, trig = call(
         query_kernel,

time: 33.4 us -> 33.1 us (level)
  transfers between devices with their start and end apart: 13 -> 13, of which waited for: 8 -> 9; matrix products, arithmetic and copies ran while one was open for 0% -> 0% of each run, Pallas kernels for 8% -> 8%
where the time goes in v3:
time: 33.1 us; the launch traced here: 32.8 us
  starting transfers between devices  15.4 us (47%)
  waiting for transfers between devices  11.7 us (35%)
  Pallas kernels  4.97 us (15%)
  between operations  0.7 us (2%)
    ppermute x13, starting transfers between devices, exchange(): return lax.ppermute(array, axis, [(at, at ^ step) for at in range(size)])  15.4 us
    ppermute x13, waiting for transfers between devices, exchange(): return lax.ppermute(array, axis, [(at, at ^ step) for at in range(size)])  11.7 us
    pallas_call x8, Pallas kernels, call(): pl.pallas_call(kernel, out_shape=outs, in_specs=[local] * len(args) + [di...  4.97 us
  transfers between devices with their start and end apart: 13, of which 9 were waited for; matrix products, arithmetic and copies ran while one was open for 0% of the time, Pallas kernels for 8%

profile of v3, /device:TPU:0, one launch (start us, length us, event | category | flops | bytes accessed | tf_op | source)
XLA Modules:
  0.0 32.8 jit_solution(3374024385422141008)
XLA Ops:
  0.6 0.0 copy-start
  0.6 1.3 %shard_map.111 = (bf16[256,128]{1,0:T(8,128)(2,1)S(1)}, bf16[1024,128]{1,0:T(8,128)(2,1)S(1)}, f32[64,128]{1,0:T(8,128)S(1)}) custom-call(s32[1,32]{1,0:T(1,128)} %refs_0_.1, f32[2,128]{1,0:T(2,128)} %constant.2.clone.refs_1_, bf16[32,512]{1,0:T(8,128)(2,1)} %bitcast.14, bf16[32,512]{1,0:T(8,128)(2,1)} %bitcast.15, bf16[32,2048]{1,0:T(8,128)(2,1)} %bitcast.12, ...), custom_call_target="tpu_custom_call" | custom-call | tf_op jit(solution)/shard_map/pallas_call | solution.py:283
  1.9 3.0 %collective-permute-start = (bf16[1024,128]{1,0:T(8,128)(2,1)S(1)}, bf16[1024,128]{1,0:T(8,128)(2,1)S(1)}, u32[]{:S(2)}, u32[]{:S(2)}) collective-permute-start(bf16[1024,128]{1,0:T(8,128)(2,1)S(1)} %get-tuple-element.31.refs_1_.refs_3_), channel_id=1, source_target_pairs={{0,1},{1,0},{2,3},{3,2},{4,5},{5,4},{6,7},{7,6},{8,9},{9,8},{10,11... | collective-permute-start | bytes 786440 | tf_op jit(solution)/shard_map/ppermute | solution.py:295
  5.0 3.6 %collective-permute-start.3 = (bf16[256,128]{1,0:T(8,128)(2,1)S(1)}, bf16[256,128]{1,0:T(8,128)(2,1)S(1)}, u32[]{:S(2)}, u32[]{:S(2)}) collective-permute-start(bf16[256,128]{1,0:T(8,128)(2,1)S(1)} %get-tuple-element.32.refs_3_.refs_5_), channel_id=1, source_target_pairs={{0,6},{1,7},{2,4},{3,5},{4,2},{5,3},{6,0},{7,1},{8,14},{9,15},{10,... | collective-permute-start | bytes 196616 | tf_op jit(solution)/shard_map/ppermute | solution.py:295
  8.6 0.0 collective-permute-start.2
  8.6 0.8 %collective-permute-start.1 = (bf16[256,128]{1,0:T(8,128)(2,1)S(1)}, bf16[256,128]{1,0:T(8,128)(2,1)S(1)}, u32[]{:S(2)}, u32[]{:S(2)}) collective-permute-start(bf16[256,128]{1,0:T(8,128)(2,1)S(1)} %get-tuple-element.32.refs_3_.refs_5_), channel_id=1, source_target_pairs={{0,2},{1,3},{2,0},{3,1},{4,6},{5,7},{6,4},{7,5},{8,10},{9,11},{10,... | collective-permute-start | bytes 196616 | tf_op jit(solution)/shard_map/ppermute | solution.py:295
  9.4 0.0 copy-done
  9.4 0.3 collective-permute-start.5
  9.6 1.1 %shard_map.112 = (f32[8,128]{1,0:T(8,128)S(1)}, bf16[32,4096]{1,0:T(8,128)(2,1)S(1)}) custom-call(f32[32,128]{1,0:T(8,128)} %bitcast.16, bf16[32,4096]{1,0:T(8,128)(2,1)} %bitcast.10), custom_call_target="tpu_custom_call" | custom-call | tf_op jit(solution)/shard_map/pallas_call | solution.py:283
  10.8 1.0 %collective-permute-done.3.refs_6_.refs_8_ = bf16[256,128]{1,0:T(8,128)(2,1)S(1)} collective-permute-done((bf16[256,128]{1,0:T(8,128)(2,1)S(1)}, bf16[256,128]{1,0:T(8,128)(2,1)S(1)}, u32[]{:S(2)}, u32[]{:S(2)}) %collective-permute-start.3) | collective-permute-done | bytes 65568 | tf_op jit(solution)/shard_map/ppermute | solution.py:295
  11.8 2.1 %collective-permute-done.2.refs_5_.refs_7_ = bf16[256,128]{1,0:T(8,128)(2,1)S(1)} collective-permute-done((bf16[256,128]{1,0:T(8,128)(2,1)S(1)}, bf16[256,128]{1,0:T(8,128)(2,1)S(1)}, u32[]{:S(2)}, u32[]{:S(2)}) %collective-permute-start.2) | collective-permute-done | bytes 65568 | tf_op jit(solution)/shard_map/ppermute | solution.py:295
  13.9 0.1 collective-permute-done.1.refs_4_.refs_6_
  14.0 0.0 collective-permute-done.refs_2_.refs_4_
  14.0 0.4 %shard_map.113 = (f32[4,128,256]{2,1,0:T(8,128)S(1)}, f32[4,128,256]{2,1,0:T(8,128)S(1)}, f32[16,256]{1,0:T(8,128)S(1)}) custom-call(f32[8,128]{1,0:T(8,128)S(1)} %get-tuple-element.30.refs_0_, bf16[1024,128]{1,0:T(8,128)(2,1)S(1)} %get-tuple-element.31.refs_1_.refs_3_, bf16[1024,128]{1,0:T(8,128)(2,1)S(1)} %collective-permute-done.refs_2_.refs_4_, ...), custom_call_target="tpu_custom_call" | custom-call | flops 20000000000 | tf_op jit(solution)/shard_map/pallas_call | solution.py:283
  14.4 0.5 %collective-permute-start.4 = (f32[16,256]{1,0:T(8,128)S(1)}, f32[16,256]{1,0:T(8,128)S(1)}, u32[]{:S(2)}, u32[]{:S(2)}) collective-permute-start(f32[16,256]{1,0:T(8,128)S(1)} %get-tuple-element.33.own_ref), channel_id=1, source_target_pairs={{0,1},{1,0},{2,3},{3,2},{4,5},{5,4},{6,7},{7,6},{8,9},{9,8},{10,11... | collective-permute-start | bytes 49160 | tf_op jit(solution)/shard_map/ppermute | solution.py:295
  14.9 2.2 %collective-permute-done.5.input_other_ref = bf16[32,4096]{1,0:T(8,128)(2,1)S(1)} collective-permute-done((bf16[32,4096]{1,0:T(8,128)(2,1)S(1)}, bf16[32,4096]{1,0:T(8,128)(2,1)S(1)}, u32[]{:S(2)}, u32[]{:S(2)}) %collective-permute-start.5) | collective-permute-done | bytes 262176 | tf_op jit(solution)/shard_map/ppermute | solution.py:295
  17.1 1.1 %collective-permute-done.4.other_ref = f32[16,256]{1,0:T(8,128)S(1)} collective-permute-done((f32[16,256]{1,0:T(8,128)S(1)}, f32[16,256]{1,0:T(8,128)S(1)}, u32[]{:S(2)}, u32[]{:S(2)}) %collective-permute-start.4) | collective-permute-done | bytes 16416 | tf_op jit(solution)/shard_map/ppermute | solution.py:295
  18.2 0.2 shard_map.114
  18.4 0.1 collective-permute-start.9
  18.5 1.6 %collective-permute-start.8 = (f32[32,128]{1,0:T(8,128)S(1)}, f32[32,128]{1,0:T(8,128)S(1)}, u32[]{:S(2)}, u32[]{:S(2)}) collective-permute-start(f32[32,128]{1,0:T(8,128)S(1)} %get-tuple-element.43.refs_0_), channel_id=1, source_target_pairs={{0,16},{8,24},{16,0},{24,8},{1,17},{9,25},{17,1},{25,9},{2,18},{10... | collective-permute-start | bytes 49160 | tf_op jit(solution)/shard_map/ppermute | solution.py:295
  20.1 0.3 collective-permute-start.7
  20.4 0.4 %shard_map.115 = (f32[512,128]{1,0:T(8,128)S(1)}, bf16[512,128]{1,0:T(8,128)(2,1)S(1)}, f32[256,128]{1,0:T(8,128)S(1)}, bf16[256,128]{1,0:T(8,128)(2,1)S(1)}, bf...) custom-call(f32[8,256]{1,0:T(8,128)S(1)} %get-tuple-element.35.refs_0_, ...), custom_call_target="tpu_custom_call" | custom-call | flops 20000000000 | tf_op jit(solution)/shard_map/pallas_call | solution.py:283
  20.8 0.8 %collective-permute-start.6 = (bf16[512,128]{1,0:T(8,128)(2,1)S(1)}, bf16[512,128]{1,0:T(8,128)(2,1)S(1)}, u32[]{:S(2)}, u32[]{:S(2)}) collective-permute-start(bf16[512,128]{1,0:T(8,128)(2,1)S(1)} %get-tuple-element.39), channel_id=1, source_target_pairs={{0,1},{1,0},{2,3},{3,2},{4,5},{5,4},{6,7},{7,6},{8,9},{9,8},{10,11... | collective-permute-start | bytes 393224 | tf_op jit(solution)/shard_map/ppermute | solution.py:295
  21.6 0.2 collective-permute-done.9.refs_3_
  21.8 0.5 %collective-permute-done.8.refs_2_ = f32[32,128]{1,0:T(8,128)S(1)} collective-permute-done((f32[32,128]{1,0:T(8,128)S(1)}, f32[32,128]{1,0:T(8,128)S(1)}, u32[]{:S(2)}, u32[]{:S(2)}) %collective-permute-start.8) | collective-permute-done | bytes 16416 | tf_op jit(solution)/shard_map/ppermute | solution.py:295
  22.3 0.0 collective-permute-done.7.refs_1_
  22.3 3.0 %collective-permute-start.10 = (bf16[288,128]{1,0:T(8,128)(2,1)S(1)}, bf16[288,128]{1,0:T(8,128)(2,1)S(1)}, u32[]{:S(2)}, u32[]{:S(2)}) collective-permute-start(bf16[288,128]{1,0:T(8,128)(2,1)S(1)} %get-tuple-element.48), channel_id=1, source_target_pairs={{0,6},{1,7},{2,4},{3,5},{4,2},{5,3},{6,0},{7,1},{8,14},{9,15},{10,... | collective-permute-start | bytes 221192 | tf_op jit(solution)/shard_map/ppermute | solution.py:295
  25.3 0.0 collective-permute-start.11
  25.3 1.5 %collective-permute-start.12 = (bf16[288,128]{1,0:T(8,128)(2,1)S(1)}, bf16[288,128]{1,0:T(8,128)(2,1)S(1)}, u32[]{:S(2)}, u32[]{:S(2)}) collective-permute-start(bf16[288,128]{1,0:T(8,128)(2,1)S(1)} %get-tuple-element.50), channel_id=1, source_target_pairs={{0,2},{1,3},{2,0},{3,1},{4,6},{5,7},{6,4},{7,5},{8,10},{9,11},{10,... | collective-permute-start | bytes 221192 | tf_op jit(solution)/shard_map/ppermute | solution.py:295
  26.8 0.0 collective-permute-done.6.other_ref
  26.8 0.8 %shard_map.116 = (bf16[32,2048]{1,0:T(8,128)(2,1)}, f32[64,128]{1,0:T(8,128)S(1)}) custom-call(f32[64,128]{1,0:T(8,128)S(1)} %get-tuple-element.29.trig_ref, f32[512,128]{1,0:T(8,128)S(1)} %get-tuple-element.38.own_ref, bf16[512,128]{1,0:T(8,128)(2,1)S(1)} %collective-permute-done.6.other_ref), custom_call_target="tpu_custom_call" | custom-call | tf_op jit(solution)/shard_map/pallas_call | solution.py:283
  27.6 1.8 %collective-permute-done.10.refs_3_ = bf16[288,128]{1,0:T(8,128)(2,1)S(1)} collective-permute-done((bf16[288,128]{1,0:T(8,128)(2,1)S(1)}, bf16[288,128]{1,0:T(8,128)(2,1)S(1)}, u32[]{:S(2)}, u32[]{:S(2)}) %collective-permute-start.10) | collective-permute-done | bytes 73760 | tf_op jit(solution)/shard_map/ppermute | solution.py:295
  29.4 2.7 %collective-permute-done.11.refs_4_ = bf16[288,128]{1,0:T(8,128)(2,1)S(1)} collective-permute-done((bf16[288,128]{1,0:T(8,128)(2,1)S(1)}, bf16[288,128]{1,0:T(8,128)(2,1)S(1)}, u32[]{:S(2)}, u32[]{:S(2)}) %collective-permute-start.11) | collective-permute-done | bytes 73760 | tf_op jit(solution)/shard_map/ppermute | solution.py:295
  32.1 0.0 collective-permute-done.12.refs_5_
  32.1 0.7 %shard_map.118 = (bf16[32,512]{1,0:T(8,128)(2,1)}, bf16[32,512]{1,0:T(8,128)(2,1)}, f32[32,128]{1,0:T(8,128)}) custom-call(f32[64,128]{1,0:T(8,128)S(1)} %get-tuple-element.41.refs_0_, f32[256,128]{1,0:T(8,128)S(1)} %get-tuple-element.42.refs_1_, f32[32,128]{1,0:T(8,128)S(1)} %get-tuple-element.47.refs_2_, ...), custom_call_target="tpu_custom_call" | custom-call | tf_op jit(solution)/shard_map/pallas_call | solution.py:283
  (1 shorter events, 0.0 us)
Async XLA Ops:
  0.6 8.7 %copy-start = (bf16[1,32,4096]{2,1,0:T(8,128)(2,1)S(1)}, bf16[1,32,4096]{2,1,0:T(8,128)(2,1)}, u32[]{:S(2)}) copy-start(bf16[1,32,4096]{2,1,0:T(8,128)(2,1)} %param.12) | copy-start | bytes 786436
  1.9 12.1 %collective-permute-start = (bf16[1024,128]{1,0:T(8,128)(2,1)S(1)}, bf16[1024,128]{1,0:T(8,128)(2,1)S(1)}, u32[]{:S(2)}, u32[]{:S(2)}) collective-permute-start(bf16[1024,128]{1,0:T(8,128)(2,1)S(1)} %get-tuple-element.31.refs_1_.refs_3_), channel_id=1, source_target_pairs={{0,1},{1,0},{2,3},{3,2},{4,5},{5,4},{6,7},{7,6},{8,9},{9,8},{10,11... | collective-permute-start | bytes 786440 | tf_op jit(solution)/shard_map/ppermute | solution.py:295
  5.0 6.9 %collective-permute-start.3 = (bf16[256,128]{1,0:T(8,128)(2,1)S(1)}, bf16[256,128]{1,0:T(8,128)(2,1)S(1)}, u32[]{:S(2)}, u32[]{:S(2)}) collective-permute-start(bf16[256,128]{1,0:T(8,128)(2,1)S(1)} %get-tuple-element.32.refs_3_.refs_5_), channel_id=1, source_target_pairs={{0,6},{1,7},{2,4},{3,5},{4,2},{5,3},{6,0},{7,1},{8,14},{9,15},{10,... | collective-permute-start | bytes 196616 | tf_op jit(solution)/shard_map/ppermute | solution.py:295
  8.6 5.4 %collective-permute-start.2 = (bf16[256,128]{1,0:T(8,128)(2,1)S(1)}, bf16[256,128]{1,0:T(8,128)(2,1)S(1)}, u32[]{:S(2)}, u32[]{:S(2)}) collective-permute-start(bf16[256,128]{1,0:T(8,128)(2,1)S(1)} %get-tuple-element.32.refs_3_.refs_5_), channel_id=1, source_target_pairs={{0,4},{1,5},{2,6},{3,7},{4,0},{5,1},{6,2},{7,3},{8,12},{9,13},{10,... | collective-permute-start | bytes 196616 | tf_op jit(solution)/shard_map/ppermute | solution.py:295
  8.6 5.4 %collective-permute-start.1 = (bf16[256,128]{1,0:T(8,128)(2,1)S(1)}, bf16[256,128]{1,0:T(8,128)(2,1)S(1)}, u32[]{:S(2)}, u32[]{:S(2)}) collective-permute-start(bf16[256,128]{1,0:T(8,128)(2,1)S(1)} %get-tuple-element.32.refs_3_.refs_5_), channel_id=1, source_target_pairs={{0,2},{1,3},{2,0},{3,1},{4,6},{5,7},{6,4},{7,5},{8,10},{9,11},{10,... | collective-permute-start | bytes 196616 | tf_op jit(solution)/shard_map/ppermute | solution.py:295
  9.4 7.7 %collective-permute-start.5 = (bf16[32,4096]{1,0:T(8,128)(2,1)S(1)}, bf16[32,4096]{1,0:T(8,128)(2,1)S(1)}, u32[]{:S(2)}, u32[]{:S(2)}) collective-permute-start(bf16[32,4096]{1,0:T(8,128)(2,1)S(1)} %bitcast.11), channel_id=1, source_target_pairs={{0,1},{1,0},{2,3},{3,2},{4,5},{5,4},{6,7},{7,6},{8,9},{9,8},{10,11... | collective-permute-start | bytes 786440 | tf_op jit(solution)/shard_map/ppermute | solution.py:295
  14.4 3.8 %collective-permute-start.4 = (f32[16,256]{1,0:T(8,128)S(1)}, f32[16,256]{1,0:T(8,128)S(1)}, u32[]{:S(2)}, u32[]{:S(2)}) collective-permute-start(f32[16,256]{1,0:T(8,128)S(1)} %get-tuple-element.33.own_ref), channel_id=1, source_target_pairs={{0,1},{1,0},{2,3},{3,2},{4,5},{5,4},{6,7},{7,6},{8,9},{9,8},{10,11... | collective-permute-start | bytes 49160 | tf_op jit(solution)/shard_map/ppermute | solution.py:295
  18.4 3.4 %collective-permute-start.9 = (f32[32,128]{1,0:T(8,128)S(1)}, f32[32,128]{1,0:T(8,128)S(1)}, u32[]{:S(2)}, u32[]{:S(2)}) collective-permute-start(f32[32,128]{1,0:T(8,128)S(1)} %get-tuple-element.43.refs_0_), channel_id=1, source_target_pairs={{0,24},{8,16},{16,8},{24,0},{1,25},{9,17},{17,9},{25,1},{2,26},{10... | collective-permute-start | bytes 49160 | tf_op jit(solution)/shard_map/ppermute | solution.py:295
  18.5 3.8 %collective-permute-start.8 = (f32[32,128]{1,0:T(8,128)S(1)}, f32[32,128]{1,0:T(8,128)S(1)}, u32[]{:S(2)}, u32[]{:S(2)}) collective-permute-start(f32[32,128]{1,0:T(8,128)S(1)} %get-tuple-element.43.refs_0_), channel_id=1, source_target_pairs={{0,16},{8,24},{16,0},{24,8},{1,17},{9,25},{17,1},{25,9},{2,18},{10... | collective-permute-start | bytes 49160 | tf_op jit(solution)/shard_map/ppermute | solution.py:295
  20.1 2.2 %collective-permute-start.7 = (f32[32,128]{1,0:T(8,128)S(1)}, f32[32,128]{1,0:T(8,128)S(1)}, u32[]{:S(2)}, u32[]{:S(2)}) collective-permute-start(f32[32,128]{1,0:T(8,128)S(1)} %get-tuple-element.43.refs_0_), channel_id=1, source_target_pairs={{0,8},{8,0},{16,24},{24,16},{1,9},{9,1},{17,25},{25,17},{2,10},{10... | collective-permute-start | bytes 49160 | tf_op jit(solution)/shard_map/ppermute | solution.py:295
  20.8 6.1 %collective-permute-start.6 = (bf16[512,128]{1,0:T(8,128)(2,1)S(1)}, bf16[512,128]{1,0:T(8,128)(2,1)S(1)}, u32[]{:S(2)}, u32[]{:S(2)}) collective-permute-start(bf16[512,128]{1,0:T(8,128)(2,1)S(1)} %get-tuple-element.39), channel_id=1, source_target_pairs={{0,1},{1,0},{2,3},{3,2},{4,5},{5,4},{6,7},{7,6},{8,9},{9,8},{10,11... | collective-permute-start | bytes 393224 | tf_op jit(solution)/shard_map/ppermute | solution.py:295
  22.3 7.1 %collective-permute-start.10 = (bf16[288,128]{1,0:T(8,128)(2,1)S(1)}, bf16[288,128]{1,0:T(8,128)(2,1)S(1)}, u32[]{:S(2)}, u32[]{:S(2)}) collective-permute-start(bf16[288,128]{1,0:T(8,128)(2,1)S(1)} %get-tuple-element.48), channel_id=1, source_target_pairs={{0,6},{1,7},{2,4},{3,5},{4,2},{5,3},{6,0},{7,1},{8,14},{9,15},{10,... | collective-permute-start | bytes 221192 | tf_op jit(solution)/shard_map/ppermute | solution.py:295
  25.3 6.8 %collective-permute-start.11 = (bf16[288,128]{1,0:T(8,128)(2,1)S(1)}, bf16[288,128]{1,0:T(8,128)(2,1)S(1)}, u32[]{:S(2)}, u32[]{:S(2)}) collective-permute-start(bf16[288,128]{1,0:T(8,128)(2,1)S(1)} %get-tuple-element.49), channel_id=1, source_target_pairs={{0,4},{1,5},{2,6},{3,7},{4,0},{5,1},{6,2},{7,3},{8,12},{9,13},{10,... | collective-permute-start | bytes 221192 | tf_op jit(solution)/shard_map/ppermute | solution.py:295
  25.3 6.8 %collective-permute-start.12 = (bf16[288,128]{1,0:T(8,128)(2,1)S(1)}, bf16[288,128]{1,0:T(8,128)(2,1)S(1)}, u32[]{:S(2)}, u32[]{:S(2)}) collective-permute-start(bf16[288,128]{1,0:T(8,128)(2,1)S(1)} %get-tuple-element.50), channel_id=1, source_target_pairs={{0,2},{1,3},{2,0},{3,1},{4,6},{5,7},{6,4},{7,5},{8,10},{9,11},{10,... | collective-permute-start | bytes 221192 | tf_op jit(solution)/shard_map/ppermute | solution.py:295

commit v4 on v3

--- a/solution.py
+++ b/solution.py
@@ -16,6 +16,7 @@
 ROPE_BASE = 500000.0
 NEG_LARGE = -1e30
 VMEM_LIMIT = 32 * 1024 * 1024
+CHUNKS = 4
 SCORES_COST = 20 * 10**9
 TERMS_COST = 20 * 10**9
 RIDE_COST = 20 * 10**9
@@ -51,18 +52,15 @@
     pair_ref, query_out, trig_ref = refs[6:9]
     place_ref, table_ref, key_ref, value_ref, query_ref, upstream_ref, semaphores = refs[9:]
     slots = key_ref.shape[0]
+    chunk = query_ref.shape[1] // CHUNKS
+    parts = [slice(at * chunk, (at + 1) * chunk) for at in range(CHUNKS)]
+    moves = [(place_hbm, place_ref), (table_hbm, table_ref), (key_hbm, key_ref)]
+    moves += [(query_hbm.at[:, part], query_ref.at[:, part]) for part in parts]
+    moves += [(value_hbm, value_ref)]
+    moves += [(upstream_hbm.at[:, part], upstream_ref.at[:, part]) for part in parts]
     copies = [
         pltpu.make_async_copy(source, target, semaphores.at[at])
-        for at, (source, target) in enumerate(
-            [
-                (place_hbm, place_ref),
-                (table_hbm, table_ref),
-                (key_hbm, key_ref),
-                (value_hbm, value_ref),
-                (query_hbm, query_ref),
-                (upstream_hbm, upstream_ref),
-            ]
-        )
+        for at, (source, target) in enumerate(moves)
     ]
     for copy in copies:
         copy.start()
@@ -82,15 +80,20 @@
     sine = jnp.where(low, -turned, mixed)
     trig_ref[0:slots, :] = cosine
     trig_ref[slots : 2 * slots, :] = sine
-    for copy in copies[2:]:
-        copy.wait()
+    copies[2].wait()
     for number in range(KVH):
         wide = key_ref[:, head(number)].astype(jnp.float32)
         pair_ref[rows_of(number, slots), :] = turn(wide, cosine, sine).astype(jnp.bfloat16)
+    for number in range(HQ):
+        if number % (HQ // CHUNKS) == 0:
+            copies[3 + number // (HQ // CHUNKS)].wait()
+        wide = query_ref[:, head(number)].astype(jnp.float32)
+        query_out[rows_of(number, slots), :] = turn(wide, cosine, sine).astype(jnp.bfloat16)
+    for copy in copies[3 + CHUNKS :]:
+        copy.wait()
+    for number in range(KVH):
         pair_ref[rows_of(KVH + number, slots), :] = value_ref[:, head(number)]
     for number in range(HQ):
-        wide = query_ref[:, head(number)].astype(jnp.float32)
-        query_out[rows_of(number, slots), :] = turn(wide, cosine, sine).astype(jnp.bfloat16)
         query_out[rows_of(HQ + number, slots), :] = upstream_ref[:, head(number)]
 
 
@@ -256,35 +259,48 @@
 
 def final_kernel(router_scale, *refs):
     trig_ref, own_ref, router_ref = refs[:3]
-    term_refs = refs[3:-3]
-    key_out, value_out, router_out = refs[-3:]
+    term_refs = refs[3:-7]
+    results = refs[-7:-4]
+    key_out, value_out, router_out, semaphores = refs[-4:]
+    copies = [
+        pltpu.make_async_copy(source, target, semaphores.at[at])
+        for at, (source, target) in enumerate(zip((key_out, value_out, router_out), results))
+    ]
     slots = key_out.shape[0]
-    cosine = trig_ref[0:slots, :]
-    sine = trig_ref[slots : 2 * slots, :]
-    for number in range(2 * KVH):
-        part = rows_of(number, slots)
-        total = own_ref[part, :]
-        for ref in term_refs:
-            total += ref[part, :].astype(jnp.float32)
-        if number < KVH:
-            key_out[:, head(number)] = turn(total, cosine, -sine).astype(jnp.bfloat16)
-        else:
-            value_out[:, head(number - KVH)] = total.astype(jnp.bfloat16)
     router = router_ref[...]
     for ref in term_refs:
         router += ref[2 * KVH * slots :, :].astype(jnp.float32)
     router_out[...] = router * router_scale
-
-
-def call(kernel, outs, args, fetched=(), scratch=(), cost=None):
+    copies[2].start()
+
+    def total(number):
+        part = rows_of(number, slots)
+        result = own_ref[part, :]
+        for ref in term_refs:
+            result += ref[part, :].astype(jnp.float32)
+        return result
+
+    for number in range(KVH):
+        value_out[:, head(number)] = total(KVH + number).astype(jnp.bfloat16)
+    copies[1].start()
+    cosine = trig_ref[0:slots, :]
+    sine = trig_ref[slots : 2 * slots, :]
+    for number in range(KVH):
+        key_out[:, head(number)] = turn(total(number), cosine, -sine).astype(jnp.bfloat16)
+    copies[0].start()
+    for copy in copies:
+        copy.wait()
+
+
+def call(kernel, outs, args, fetched=(), scratch=(), cost=None, copies=0, kept=0):
     local = pl.BlockSpec(memory_space=pltpu.VMEM)
     distant = pl.BlockSpec(memory_space=pl.ANY)
-    scratch = list(scratch) + [pltpu.SemaphoreType.DMA((len(fetched),))] * bool(fetched)
+    scratch = list(scratch) + [pltpu.SemaphoreType.DMA((copies,))] * bool(copies)
     return pl.pallas_call(
         kernel,
         out_shape=outs,
         in_specs=[local] * len(args) + [distant] * len(fetched),
-        out_specs=[local] * len(outs),
+        out_specs=[distant] * kept + [local] * (len(outs) - kept),
         scratch_shapes=scratch,
         compiler_params=pltpu.CompilerParams(vmem_limit_bytes=VMEM_LIMIT),
         cost_estimate=cost and pl.CostEstimate(cost, 0, 0),
@@ -320,6 +336,7 @@
         [],
         fetched,
         [near(array.shape, array.dtype) for array in fetched],
+        copies=4 + 2 * CHUNKS,
     )
     query_other = swap(query)
     pairs = [pair] + [
@@ -331,6 +348,7 @@
         [],
         [router_weight.reshape(lines, HD), routed_inputs[0]],
         [near((lines, HD), f32)],
+        copies=2,
     )
     inputs_other = swap(routed_inputs[0])
     grown, grad, stats = call(
@@ -382,6 +400,13 @@
         functools.partial(final_kernel, 1.0 / math.sqrt(groups * count * slots)),
         [shape((slots, KVH * HD), bf16), shape((slots, KVH * HD), bf16), shape((lines, HD), f32)],
         [trig, term_own, router, *terms],
+        scratch=[
+            near((slots, KVH * HD), bf16),
+            near((slots, KVH * HD), bf16),
+            near((lines, HD), f32),
+        ],
+        copies=3,
+        kept=3,
     )
     return (query_grad[None], key_grad[None], value_grad[None], router_grad.reshape(width))
 

time: 33.1 us -> 33.3 us (level)
  no operation moved by 1% of the time
where the time goes in v4:
time: 33.3 us; the launch traced here: 33.1 us
  starting transfers between devices  15.4 us (46%)
  waiting for transfers between devices  11.8 us (35%)
  Pallas kernels  5.2 us (16%)
  between operations  0.7 us (2%)
    ppermute x13, starting transfers between devices, exchange(): return lax.ppermute(array, axis, [(at, at ^ step) for at in range(size)])  15.4 us
    ppermute x13, waiting for transfers between devices, exchange(): return lax.ppermute(array, axis, [(at, at ^ step) for at in range(size)])  11.8 us
    pallas_call x8, Pallas kernels, call(): pl.pallas_call(kernel, out_shape=outs, in_specs=[local] * len(args) + [di...  5.2 us
  transfers between devices with their start and end apart: 13, of which 9 were waited for; matrix products, arithmetic and copies ran while one was open for 0% of the time, Pallas kernels for 8%

profile of v4, /device:TPU:0, one launch (start us, length us, event | category | flops | bytes accessed | tf_op | source)
XLA Modules:
  0.0 33.1 jit_solution(752439457268625377)
XLA Ops:
  0.6 0.0 copy-start
  0.6 1.5 %shard_map.111 = (bf16[256,128]{1,0:T(8,128)(2,1)S(1)}, bf16[1024,128]{1,0:T(8,128)(2,1)S(1)}, f32[64,128]{1,0:T(8,128)S(1)}) custom-call(s32[1,32]{1,0:T(1,128)} %refs_0_.1, f32[2,128]{1,0:T(2,128)} %constant.2.clone.refs_1_, bf16[32,512]{1,0:T(8,128)(2,1)} %bitcast.14, bf16[32,512]{1,0:T(8,128)(2,1)} %bitcast.15, bf16[32,2048]{1,0:T(8,128)(2,1)} %bitcast.12, ...), custom_call_target="tpu_custom_call" | custom-call | tf_op jit(solution)/shard_map/pallas_call | solution.py:299
  2.1 3.0 %collective-permute-start = (bf16[1024,128]{1,0:T(8,128)(2,1)S(1)}, bf16[1024,128]{1,0:T(8,128)(2,1)S(1)}, u32[]{:S(2)}, u32[]{:S(2)}) collective-permute-start(bf16[1024,128]{1,0:T(8,128)(2,1)S(1)} %get-tuple-element.31.refs_1_.refs_3_), channel_id=1, source_target_pairs={{0,1},{1,0},{2,3},{3,2},{4,5},{5,4},{6,7},{7,6},{8,9},{9,8},{10,11... | collective-permute-start | bytes 786440 | tf_op jit(solution)/shard_map/ppermute | solution.py:311
  5.2 3.6 %collective-permute-start.3 = (bf16[256,128]{1,0:T(8,128)(2,1)S(1)}, bf16[256,128]{1,0:T(8,128)(2,1)S(1)}, u32[]{:S(2)}, u32[]{:S(2)}) collective-permute-start(bf16[256,128]{1,0:T(8,128)(2,1)S(1)} %get-tuple-element.32.refs_3_.refs_5_), channel_id=1, source_target_pairs={{0,6},{1,7},{2,4},{3,5},{4,2},{5,3},{6,0},{7,1},{8,14},{9,15},{10,... | collective-permute-start | bytes 196616 | tf_op jit(solution)/shard_map/ppermute | solution.py:311
  8.8 0.0 collective-permute-start.2
  8.8 0.8 %collective-permute-start.1 = (bf16[256,128]{1,0:T(8,128)(2,1)S(1)}, bf16[256,128]{1,0:T(8,128)(2,1)S(1)}, u32[]{:S(2)}, u32[]{:S(2)}) collective-permute-start(bf16[256,128]{1,0:T(8,128)(2,1)S(1)} %get-tuple-element.32.refs_3_.refs_5_), channel_id=1, source_target_pairs={{0,2},{1,3},{2,0},{3,1},{4,6},{5,7},{6,4},{7,5},{8,10},{9,11},{10,... | collective-permute-start | bytes 196616 | tf_op jit(solution)/shard_map/ppermute | solution.py:311
  9.6 0.0 copy-done
  9.6 0.3 collective-permute-start.5
  9.9 1.1 %shard_map.112 = (f32[8,128]{1,0:T(8,128)S(1)}, bf16[32,4096]{1,0:T(8,128)(2,1)S(1)}) custom-call(f32[32,128]{1,0:T(8,128)} %bitcast.16, bf16[32,4096]{1,0:T(8,128)(2,1)} %bitcast.10), custom_call_target="tpu_custom_call" | custom-call | tf_op jit(solution)/shard_map/pallas_call | solution.py:299
  11.0 1.0 %collective-permute-done.3.refs_6_.refs_8_ = bf16[256,128]{1,0:T(8,128)(2,1)S(1)} collective-permute-done((bf16[256,128]{1,0:T(8,128)(2,1)S(1)}, bf16[256,128]{1,0:T(8,128)(2,1)S(1)}, u32[]{:S(2)}, u32[]{:S(2)}) %collective-permute-start.3) | collective-permute-done | bytes 65568 | tf_op jit(solution)/shard_map/ppermute | solution.py:311
  12.0 2.1 %collective-permute-done.2.refs_5_.refs_7_ = bf16[256,128]{1,0:T(8,128)(2,1)S(1)} collective-permute-done((bf16[256,128]{1,0:T(8,128)(2,1)S(1)}, bf16[256,128]{1,0:T(8,128)(2,1)S(1)}, u32[]{:S(2)}, u32[]{:S(2)}) %collective-permute-start.2) | collective-permute-done | bytes 65568 | tf_op jit(solution)/shard_map/ppermute | solution.py:311
  14.2 0.1 collective-permute-done.1.refs_4_.refs_6_
  14.2 0.0 collective-permute-done.refs_2_.refs_4_
  14.2 0.4 %shard_map.113 = (f32[4,128,256]{2,1,0:T(8,128)S(1)}, f32[4,128,256]{2,1,0:T(8,128)S(1)}, f32[16,256]{1,0:T(8,128)S(1)}) custom-call(f32[8,128]{1,0:T(8,128)S(1)} %get-tuple-element.30.refs_0_, bf16[1024,128]{1,0:T(8,128)(2,1)S(1)} %get-tuple-element.31.refs_1_.refs_3_, bf16[1024,128]{1,0:T(8,128)(2,1)S(1)} %collective-permute-done.refs_2_.refs_4_, ...), custom_call_target="tpu_custom_call" | custom-call | flops 20000000000 | tf_op jit(solution)/shard_map/pallas_call | solution.py:299
  14.6 0.5 %collective-permute-start.4 = (f32[16,256]{1,0:T(8,128)S(1)}, f32[16,256]{1,0:T(8,128)S(1)}, u32[]{:S(2)}, u32[]{:S(2)}) collective-permute-start(f32[16,256]{1,0:T(8,128)S(1)} %get-tuple-element.33.own_ref), channel_id=1, source_target_pairs={{0,1},{1,0},{2,3},{3,2},{4,5},{5,4},{6,7},{7,6},{8,9},{9,8},{10,11... | collective-permute-start | bytes 49160 | tf_op jit(solution)/shard_map/ppermute | solution.py:311
  15.1 2.2 %collective-permute-done.5.input_other_ref = bf16[32,4096]{1,0:T(8,128)(2,1)S(1)} collective-permute-done((bf16[32,4096]{1,0:T(8,128)(2,1)S(1)}, bf16[32,4096]{1,0:T(8,128)(2,1)S(1)}, u32[]{:S(2)}, u32[]{:S(2)}) %collective-permute-start.5) | collective-permute-done | bytes 262176 | tf_op jit(solution)/shard_map/ppermute | solution.py:311
  17.3 1.1 %collective-permute-done.4.other_ref = f32[16,256]{1,0:T(8,128)S(1)} collective-permute-done((f32[16,256]{1,0:T(8,128)S(1)}, f32[16,256]{1,0:T(8,128)S(1)}, u32[]{:S(2)}, u32[]{:S(2)}) %collective-permute-start.4) | collective-permute-done | bytes 16416 | tf_op jit(solution)/shard_map/ppermute | solution.py:311
  18.4 0.2 shard_map.114
  18.7 0.1 collective-permute-start.9
  18.7 1.6 %collective-permute-start.8 = (f32[32,128]{1,0:T(8,128)S(1)}, f32[32,128]{1,0:T(8,128)S(1)}, u32[]{:S(2)}, u32[]{:S(2)}) collective-permute-start(f32[32,128]{1,0:T(8,128)S(1)} %get-tuple-element.43.refs_0_), channel_id=1, source_target_pairs={{0,16},{8,24},{16,0},{24,8},{1,17},{9,25},{17,1},{25,9},{2,18},{10... | collective-permute-start | bytes 49160 | tf_op jit(solution)/shard_map/ppermute | solution.py:311
  20.3 0.3 collective-permute-start.7
  20.6 0.4 %shard_map.115 = (f32[512,128]{1,0:T(8,128)S(1)}, bf16[512,128]{1,0:T(8,128)(2,1)S(1)}, f32[256,128]{1,0:T(8,128)S(1)}, bf16[256,128]{1,0:T(8,128)(2,1)S(1)}, bf...) custom-call(f32[8,256]{1,0:T(8,128)S(1)} %get-tuple-element.35.refs_0_, ...), custom_call_target="tpu_custom_call" | custom-call | flops 20000000000 | tf_op jit(solution)/shard_map/pallas_call | solution.py:299
  21.0 0.8 %collective-permute-start.6 = (bf16[512,128]{1,0:T(8,128)(2,1)S(1)}, bf16[512,128]{1,0:T(8,128)(2,1)S(1)}, u32[]{:S(2)}, u32[]{:S(2)}) collective-permute-start(bf16[512,128]{1,0:T(8,128)(2,1)S(1)} %get-tuple-element.39), channel_id=1, source_target_pairs={{0,1},{1,0},{2,3},{3,2},{4,5},{5,4},{6,7},{7,6},{8,9},{9,8},{10,11... | collective-permute-start | bytes 393224 | tf_op jit(solution)/shard_map/ppermute | solution.py:311
  21.8 0.2 collective-permute-done.9.refs_3_
  22.0 0.5 %collective-permute-done.8.refs_2_ = f32[32,128]{1,0:T(8,128)S(1)} collective-permute-done((f32[32,128]{1,0:T(8,128)S(1)}, f32[32,128]{1,0:T(8,128)S(1)}, u32[]{:S(2)}, u32[]{:S(2)}) %collective-permute-start.8) | collective-permute-done | bytes 16416 | tf_op jit(solution)/shard_map/ppermute | solution.py:311
  22.5 0.0 collective-permute-done.7.refs_1_
  22.6 3.0 %collective-permute-start.10 = (bf16[288,128]{1,0:T(8,128)(2,1)S(1)}, bf16[288,128]{1,0:T(8,128)(2,1)S(1)}, u32[]{:S(2)}, u32[]{:S(2)}) collective-permute-start(bf16[288,128]{1,0:T(8,128)(2,1)S(1)} %get-tuple-element.48), channel_id=1, source_target_pairs={{0,6},{1,7},{2,4},{3,5},{4,2},{5,3},{6,0},{7,1},{8,14},{9,15},{10,... | collective-permute-start | bytes 221192 | tf_op jit(solution)/shard_map/ppermute | solution.py:311
  25.5 0.0 collective-permute-start.11
  25.5 1.5 %collective-permute-start.12 = (bf16[288,128]{1,0:T(8,128)(2,1)S(1)}, bf16[288,128]{1,0:T(8,128)(2,1)S(1)}, u32[]{:S(2)}, u32[]{:S(2)}) collective-permute-start(bf16[288,128]{1,0:T(8,128)(2,1)S(1)} %get-tuple-element.50), channel_id=1, source_target_pairs={{0,2},{1,3},{2,0},{3,1},{4,6},{5,7},{6,4},{7,5},{8,10},{9,11},{10,... | collective-permute-start | bytes 221192 | tf_op jit(solution)/shard_map/ppermute | solution.py:311
  27.0 0.0 collective-permute-done.6.other_ref
  27.0 0.8 %shard_map.116 = (bf16[32,2048]{1,0:T(8,128)(2,1)}, f32[64,128]{1,0:T(8,128)S(1)}) custom-call(f32[64,128]{1,0:T(8,128)S(1)} %get-tuple-element.29.trig_ref, f32[512,128]{1,0:T(8,128)S(1)} %get-tuple-element.38.own_ref, bf16[512,128]{1,0:T(8,128)(2,1)S(1)} %collective-permute-done.6.other_ref), custom_call_target="tpu_custom_call" | custom-call | tf_op jit(solution)/shard_map/pallas_call | solution.py:299
  27.8 1.8 %collective-permute-done.10.refs_3_ = bf16[288,128]{1,0:T(8,128)(2,1)S(1)} collective-permute-done((bf16[288,128]{1,0:T(8,128)(2,1)S(1)}, bf16[288,128]{1,0:T(8,128)(2,1)S(1)}, u32[]{:S(2)}, u32[]{:S(2)}) %collective-permute-start.10) | collective-permute-done | bytes 73760 | tf_op jit(solution)/shard_map/ppermute | solution.py:311
  29.6 2.7 %collective-permute-done.11.refs_4_ = bf16[288,128]{1,0:T(8,128)(2,1)S(1)} collective-permute-done((bf16[288,128]{1,0:T(8,128)(2,1)S(1)}, bf16[288,128]{1,0:T(8,128)(2,1)S(1)}, u32[]{:S(2)}, u32[]{:S(2)}) %collective-permute-start.11) | collective-permute-done | bytes 73760 | tf_op jit(solution)/shard_map/ppermute | solution.py:311
  32.3 0.0 collective-permute-done.12.refs_5_
  32.3 0.7 %shard_map.118 = (bf16[32,512]{1,0:T(8,128)(2,1)}, bf16[32,512]{1,0:T(8,128)(2,1)}, f32[32,128]{1,0:T(8,128)}) custom-call(f32[64,128]{1,0:T(8,128)S(1)} %get-tuple-element.41.refs_0_, f32[256,128]{1,0:T(8,128)S(1)} %get-tuple-element.42.refs_1_, f32[32,128]{1,0:T(8,128)S(1)} %get-tuple-element.47.refs_2_, ...), custom_call_target="tpu_custom_call" | custom-call | tf_op jit(solution)/shard_map/pallas_call | solution.py:299
  (1 shorter events, 0.0 us)
Async XLA Ops:
  0.6 8.9 %copy-start = (bf16[1,32,4096]{2,1,0:T(8,128)(2,1)S(1)}, bf16[1,32,4096]{2,1,0:T(8,128)(2,1)}, u32[]{:S(2)}) copy-start(bf16[1,32,4096]{2,1,0:T(8,128)(2,1)} %param.12) | copy-start | bytes 786436
  2.1 12.1 %collective-permute-start = (bf16[1024,128]{1,0:T(8,128)(2,1)S(1)}, bf16[1024,128]{1,0:T(8,128)(2,1)S(1)}, u32[]{:S(2)}, u32[]{:S(2)}) collective-permute-start(bf16[1024,128]{1,0:T(8,128)(2,1)S(1)} %get-tuple-element.31.refs_1_.refs_3_), channel_id=1, source_target_pairs={{0,1},{1,0},{2,3},{3,2},{4,5},{5,4},{6,7},{7,6},{8,9},{9,8},{10,11... | collective-permute-start | bytes 786440 | tf_op jit(solution)/shard_map/ppermute | solution.py:311
  5.2 6.9 %collective-permute-start.3 = (bf16[256,128]{1,0:T(8,128)(2,1)S(1)}, bf16[256,128]{1,0:T(8,128)(2,1)S(1)}, u32[]{:S(2)}, u32[]{:S(2)}) collective-permute-start(bf16[256,128]{1,0:T(8,128)(2,1)S(1)} %get-tuple-element.32.refs_3_.refs_5_), channel_id=1, source_target_pairs={{0,6},{1,7},{2,4},{3,5},{4,2},{5,3},{6,0},{7,1},{8,14},{9,15},{10,... | collective-permute-start | bytes 196616 | tf_op jit(solution)/shard_map/ppermute | solution.py:311
  8.8 5.4 %collective-permute-start.2 = (bf16[256,128]{1,0:T(8,128)(2,1)S(1)}, bf16[256,128]{1,0:T(8,128)(2,1)S(1)}, u32[]{:S(2)}, u32[]{:S(2)}) collective-permute-start(bf16[256,128]{1,0:T(8,128)(2,1)S(1)} %get-tuple-element.32.refs_3_.refs_5_), channel_id=1, source_target_pairs={{0,4},{1,5},{2,6},{3,7},{4,0},{5,1},{6,2},{7,3},{8,12},{9,13},{10,... | collective-permute-start | bytes 196616 | tf_op jit(solution)/shard_map/ppermute | solution.py:311
  8.8 5.4 %collective-permute-start.1 = (bf16[256,128]{1,0:T(8,128)(2,1)S(1)}, bf16[256,128]{1,0:T(8,128)(2,1)S(1)}, u32[]{:S(2)}, u32[]{:S(2)}) collective-permute-start(bf16[256,128]{1,0:T(8,128)(2,1)S(1)} %get-tuple-element.32.refs_3_.refs_5_), channel_id=1, source_target_pairs={{0,2},{1,3},{2,0},{3,1},{4,6},{5,7},{6,4},{7,5},{8,10},{9,11},{10,... | collective-permute-start | bytes 196616 | tf_op jit(solution)/shard_map/ppermute | solution.py:311
  9.6 7.7 %collective-permute-start.5 = (bf16[32,4096]{1,0:T(8,128)(2,1)S(1)}, bf16[32,4096]{1,0:T(8,128)(2,1)S(1)}, u32[]{:S(2)}, u32[]{:S(2)}) collective-permute-start(bf16[32,4096]{1,0:T(8,128)(2,1)S(1)} %bitcast.11), channel_id=1, source_target_pairs={{0,1},{1,0},{2,3},{3,2},{4,5},{5,4},{6,7},{7,6},{8,9},{9,8},{10,11... | collective-permute-start | bytes 786440 | tf_op jit(solution)/shard_map/ppermute | solution.py:311
  14.6 3.8 %collective-permute-start.4 = (f32[16,256]{1,0:T(8,128)S(1)}, f32[16,256]{1,0:T(8,128)S(1)}, u32[]{:S(2)}, u32[]{:S(2)}) collective-permute-start(f32[16,256]{1,0:T(8,128)S(1)} %get-tuple-element.33.own_ref), channel_id=1, source_target_pairs={{0,1},{1,0},{2,3},{3,2},{4,5},{5,4},{6,7},{7,6},{8,9},{9,8},{10,11... | collective-permute-start | bytes 49160 | tf_op jit(solution)/shard_map/ppermute | solution.py:311
  18.7 3.4 %collective-permute-start.9 = (f32[32,128]{1,0:T(8,128)S(1)}, f32[32,128]{1,0:T(8,128)S(1)}, u32[]{:S(2)}, u32[]{:S(2)}) collective-permute-start(f32[32,128]{1,0:T(8,128)S(1)} %get-tuple-element.43.refs_0_), channel_id=1, source_target_pairs={{0,24},{8,16},{16,8},{24,0},{1,25},{9,17},{17,9},{25,1},{2,26},{10... | collective-permute-start | bytes 49160 | tf_op jit(solution)/shard_map/ppermute | solution.py:311
  18.7 3.8 %collective-permute-start.8 = (f32[32,128]{1,0:T(8,128)S(1)}, f32[32,128]{1,0:T(8,128)S(1)}, u32[]{:S(2)}, u32[]{:S(2)}) collective-permute-start(f32[32,128]{1,0:T(8,128)S(1)} %get-tuple-element.43.refs_0_), channel_id=1, source_target_pairs={{0,16},{8,24},{16,0},{24,8},{1,17},{9,25},{17,1},{25,9},{2,18},{10... | collective-permute-start | bytes 49160 | tf_op jit(solution)/shard_map/ppermute | solution.py:311
  20.3 2.3 %collective-permute-start.7 = (f32[32,128]{1,0:T(8,128)S(1)}, f32[32,128]{1,0:T(8,128)S(1)}, u32[]{:S(2)}, u32[]{:S(2)}) collective-permute-start(f32[32,128]{1,0:T(8,128)S(1)} %get-tuple-element.43.refs_0_), channel_id=1, source_target_pairs={{0,8},{8,0},{16,24},{24,16},{1,9},{9,1},{17,25},{25,17},{2,10},{10... | collective-permute-start | bytes 49160 | tf_op jit(solution)/shard_map/ppermute | solution.py:311
  21.0 6.1 %collective-permute-start.6 = (bf16[512,128]{1,0:T(8,128)(2,1)S(1)}, bf16[512,128]{1,0:T(8,128)(2,1)S(1)}, u32[]{:S(2)}, u32[]{:S(2)}) collective-permute-start(bf16[512,128]{1,0:T(8,128)(2,1)S(1)} %get-tuple-element.39), channel_id=1, source_target_pairs={{0,1},{1,0},{2,3},{3,2},{4,5},{5,4},{6,7},{7,6},{8,9},{9,8},{10,11... | collective-permute-start | bytes 393224 | tf_op jit(solution)/shard_map/ppermute | solution.py:311
  22.6 7.1 %collective-permute-start.10 = (bf16[288,128]{1,0:T(8,128)(2,1)S(1)}, bf16[288,128]{1,0:T(8,128)(2,1)S(1)}, u32[]{:S(2)}, u32[]{:S(2)}) collective-permute-start(bf16[288,128]{1,0:T(8,128)(2,1)S(1)} %get-tuple-element.48), channel_id=1, source_target_pairs={{0,6},{1,7},{2,4},{3,5},{4,2},{5,3},{6,0},{7,1},{8,14},{9,15},{10,... | collective-permute-start | bytes 221192 | tf_op jit(solution)/shard_map/ppermute | solution.py:311
  25.5 6.8 %collective-permute-start.11 = (bf16[288,128]{1,0:T(8,128)(2,1)S(1)}, bf16[288,128]{1,0:T(8,128)(2,1)S(1)}, u32[]{:S(2)}, u32[]{:S(2)}) collective-permute-start(bf16[288,128]{1,0:T(8,128)(2,1)S(1)} %get-tuple-element.49), channel_id=1, source_target_pairs={{0,4},{1,5},{2,6},{3,7},{4,0},{5,1},{6,2},{7,3},{8,12},{9,13},{10,... | collective-permute-start | bytes 221192 | tf_op jit(solution)/shard_map/ppermute | solution.py:311
  25.5 6.8 %collective-permute-start.12 = (bf16[288,128]{1,0:T(8,128)(2,1)S(1)}, bf16[288,128]{1,0:T(8,128)(2,1)S(1)}, u32[]{:S(2)}, u32[]{:S(2)}) collective-permute-start(bf16[288,128]{1,0:T(8,128)(2,1)S(1)} %get-tuple-element.50), channel_id=1, source_target_pairs={{0,2},{1,3},{2,0},{3,1},{4,6},{5,7},{6,4},{7,5},{8,10},{9,11},{10,... | collective-permute-start | bytes 221192 | tf_op jit(solution)/shard_map/ppermute | solution.py:311

commit v5 on v3

--- a/solution.py
+++ b/solution.py
@@ -18,7 +18,8 @@
 VMEM_LIMIT = 32 * 1024 * 1024
 SCORES_COST = 20 * 10**9
 TERMS_COST = 20 * 10**9
-RIDE_COST = 20 * 10**9
+RIDE_COST = 10**9
+QUERY_COST = 5 * 10**8
 
 
 def rope_table():
@@ -230,24 +231,26 @@
 
 
 def ride_kernel(groups, *refs):
-    router_refs = refs[:groups]
-    count = (len(refs) - groups - 1) // 2
+    count = (len(refs) - groups - 2) // 2
     term_refs = refs[groups : groups + count]
-    router_out = refs[groups + count]
-    router = router_refs[0][...]
-    for ref in router_refs[1:]:
+    router_out, send_out = refs[groups + count : groups + count + 2]
+    router = refs[0][...]
+    for ref in refs[1:groups]:
         router += ref[...]
     router_out[...] = router
-    for term, out in zip(term_refs, refs[groups + count + 1 :]):
+    narrow = router.astype(jnp.bfloat16)
+    send_out[...] = narrow
+    for term, out in zip(term_refs, refs[groups + count + 2 :]):
         out[0 : term.shape[0], :] = term[...]
-        out[term.shape[0] :, :] = router.astype(jnp.bfloat16)
-
-
-def query_kernel(trig_ref, own_ref, other_ref, query_out, trig_out):
+        out[term.shape[0] :, :] = narrow
+
+
+def query_kernel(trig_ref, own_ref, other_ref, far_ref, term_ref, query_out, trig_out, term_out):
     slots = query_out.shape[0]
     cosine = trig_ref[0:slots, :]
     sine = trig_ref[slots : 2 * slots, :]
     trig_out[...] = trig_ref[...]
+    term_out[...] = term_ref[...] + far_ref[...].astype(jnp.float32)
     for number in range(HQ):
         part = rows_of(number, slots)
         total = own_ref[part, :] + other_ref[part, :].astype(jnp.float32)
@@ -255,8 +258,8 @@
 
 
 def final_kernel(router_scale, *refs):
-    trig_ref, own_ref, router_ref = refs[:3]
-    term_refs = refs[3:-3]
+    trig_ref, own_ref, router_ref, alone_ref = refs[:4]
+    term_refs = refs[4:-3]
     key_out, value_out, router_out = refs[-3:]
     slots = key_out.shape[0]
     cosine = trig_ref[0:slots, :]
@@ -270,7 +273,7 @@
             key_out[:, head(number)] = turn(total, cosine, -sine).astype(jnp.bfloat16)
         else:
             value_out[:, head(number - KVH)] = total.astype(jnp.bfloat16)
-    router = router_ref[...]
+    router = router_ref[...] + alone_ref[...].astype(jnp.float32)
     for ref in term_refs:
         router += ref[2 * KVH * slots :, :].astype(jnp.float32)
     router_out[...] = router * router_scale
@@ -363,25 +366,33 @@
         cost=TERMS_COST,
     )
     query_back = swap(query_send)
-    router, *terms = call(
+    far = exchange(terms[-1], "ctx", 2 * (half - 1), count)
+    router, router_send, *terms = call(
         functools.partial(ride_kernel, groups),
-        [near((lines, HD), f32)] + [near((2 * KVH * slots + lines, HD), bf16)] * (half - 1),
-        [*routers, *terms],
+        [near((lines, HD), f32), near((lines, HD), bf16)]
+        + [near((2 * KVH * slots + lines, HD), bf16)] * (half - 2),
+        [*routers, *terms[:-1]],
         cost=RIDE_COST,
     )
     terms = [
-        exchange(terms[step - 1], "ctx", 2 * step, count) for step in reversed(range(1, half))
+        exchange(terms[step - 1], "ctx", 2 * step, count) for step in reversed(range(1, half - 1))
     ]
+    alone = exchange(router_send, "ctx", 2 * (half - 1), count)
     shape = jax.ShapeDtypeStruct
-    query_grad, trig = call(
+    query_grad, trig, term_own = call(
         query_kernel,
-        [shape((slots, HQ * HD), bf16), near((2 * slots, HD), f32)],
-        [trig, query_own, query_back],
+        [
+            shape((slots, HQ * HD), bf16),
+            near((2 * slots, HD), f32),
+            near((2 * KVH * slots, HD), f32),
+        ],
+        [trig, query_own, query_back, far, term_own],
+        cost=QUERY_COST,
     )
     key_grad, value_grad, router_grad = call(
         functools.partial(final_kernel, 1.0 / math.sqrt(groups * count * slots)),
         [shape((slots, KVH * HD), bf16), shape((slots, KVH * HD), bf16), shape((lines, HD), f32)],
-        [trig, term_own, router, *terms],
+        [trig, term_own, router, alone, *terms],
     )
     return (query_grad[None], key_grad[None], value_grad[None], router_grad.reshape(width))
 

time: 33.1 us -> 33.1 us (level)
  starting transfers between devices: 15.4 us -> 19 us
  waiting for transfers between devices: 11.7 us -> 8.15 us
    ppermute x13 -> x14, waiting for transfers between devices: 11.7 us -> 8.15 us  [exchange(): return lax.ppermute(array, axis, [(at, at ^ step) for at in range(size)])]
    ppermute x13 -> x14, starting transfers between devices: 15.4 us -> 19 us  [exchange(): return lax.ppermute(array, axis, [(at, at ^ step) for at in range(size)])]
  transfers between devices with their start and end apart: 13 -> 14, of which waited for: 9 -> 6; matrix products, arithmetic and copies ran while one was open for 0% -> 0% of each run, Pallas kernels for 8% -> 8%
where the time goes in v5:
time: 33.1 us; the launch traced here: 32.8 us
  starting transfers between devices  19 us (57%)
  waiting for transfers between devices  8.15 us (25%)
  Pallas kernels  4.96 us (15%)
  between operations  0.71 us (2%)
    ppermute x14, starting transfers between devices, exchange(): return lax.ppermute(array, axis, [(at, at ^ step) for at in range(size)])  19 us
    ppermute x14, waiting for transfers between devices, exchange(): return lax.ppermute(array, axis, [(at, at ^ step) for at in range(size)])  8.15 us
    pallas_call x8, Pallas kernels, call(): pl.pallas_call(kernel, out_shape=outs, in_specs=[local] * len(args) + [di...  4.96 us
  transfers between devices with their start and end apart: 14, of which 6 were waited for; matrix products, arithmetic and copies ran while one was open for 0% of the time, Pallas kernels for 8%

profile of v5, /device:TPU:0, one launch (start us, length us, event | category | flops | bytes accessed | tf_op | source)
XLA Modules:
  0.0 32.8 jit_solution(418834552378157144)
XLA Ops:
  0.6 0.0 copy-start
  0.6 1.3 %shard_map.111 = (bf16[256,128]{1,0:T(8,128)(2,1)S(1)}, bf16[1024,128]{1,0:T(8,128)(2,1)S(1)}, f32[64,128]{1,0:T(8,128)S(1)}) custom-call(s32[1,32]{1,0:T(1,128)} %refs_0_.1, f32[2,128]{1,0:T(2,128)} %constant.2.clone.refs_1_, bf16[32,512]{1,0:T(8,128)(2,1)} %bitcast.14, bf16[32,512]{1,0:T(8,128)(2,1)} %bitcast.15, bf16[32,2048]{1,0:T(8,128)(2,1)} %bitcast.12, ...), custom_call_target="tpu_custom_call" | custom-call | tf_op jit(solution)/shard_map/pallas_call | solution.py:286
  1.9 3.0 %collective-permute-start = (bf16[1024,128]{1,0:T(8,128)(2,1)S(1)}, bf16[1024,128]{1,0:T(8,128)(2,1)S(1)}, u32[]{:S(2)}, u32[]{:S(2)}) collective-permute-start(bf16[1024,128]{1,0:T(8,128)(2,1)S(1)} %get-tuple-element.32.refs_1_.refs_3_), channel_id=1, source_target_pairs={{0,1},{1,0},{2,3},{3,2},{4,5},{5,4},{6,7},{7,6},{8,9},{9,8},{10,11... | collective-permute-start | bytes 786440 | tf_op jit(solution)/shard_map/ppermute | solution.py:298
  5.0 3.6 %collective-permute-start.3 = (bf16[256,128]{1,0:T(8,128)(2,1)S(1)}, bf16[256,128]{1,0:T(8,128)(2,1)S(1)}, u32[]{:S(2)}, u32[]{:S(2)}) collective-permute-start(bf16[256,128]{1,0:T(8,128)(2,1)S(1)} %get-tuple-element.33.refs_3_.refs_5_), channel_id=1, source_target_pairs={{0,6},{1,7},{2,4},{3,5},{4,2},{5,3},{6,0},{7,1},{8,14},{9,15},{10,... | collective-permute-start | bytes 196616 | tf_op jit(solution)/shard_map/ppermute | solution.py:298
  8.6 0.0 collective-permute-start.2
  8.6 0.8 %collective-permute-start.1 = (bf16[256,128]{1,0:T(8,128)(2,1)S(1)}, bf16[256,128]{1,0:T(8,128)(2,1)S(1)}, u32[]{:S(2)}, u32[]{:S(2)}) collective-permute-start(bf16[256,128]{1,0:T(8,128)(2,1)S(1)} %get-tuple-element.33.refs_3_.refs_5_), channel_id=1, source_target_pairs={{0,2},{1,3},{2,0},{3,1},{4,6},{5,7},{6,4},{7,5},{8,10},{9,11},{10,... | collective-permute-start | bytes 196616 | tf_op jit(solution)/shard_map/ppermute | solution.py:298
  9.4 0.0 copy-done
  9.4 0.3 collective-permute-start.5
  9.6 1.1 %shard_map.112 = (f32[8,128]{1,0:T(8,128)S(1)}, bf16[32,4096]{1,0:T(8,128)(2,1)S(1)}) custom-call(f32[32,128]{1,0:T(8,128)} %bitcast.16, bf16[32,4096]{1,0:T(8,128)(2,1)} %bitcast.10), custom_call_target="tpu_custom_call" | custom-call | tf_op jit(solution)/shard_map/pallas_call | solution.py:286
  10.8 1.0 %collective-permute-done.3.refs_6_.refs_8_ = bf16[256,128]{1,0:T(8,128)(2,1)S(1)} collective-permute-done((bf16[256,128]{1,0:T(8,128)(2,1)S(1)}, bf16[256,128]{1,0:T(8,128)(2,1)S(1)}, u32[]{:S(2)}, u32[]{:S(2)}) %collective-permute-start.3) | collective-permute-done | bytes 65568 | tf_op jit(solution)/shard_map/ppermute | solution.py:298
  11.8 2.1 %collective-permute-done.2.refs_5_.refs_7_ = bf16[256,128]{1,0:T(8,128)(2,1)S(1)} collective-permute-done((bf16[256,128]{1,0:T(8,128)(2,1)S(1)}, bf16[256,128]{1,0:T(8,128)(2,1)S(1)}, u32[]{:S(2)}, u32[]{:S(2)}) %collective-permute-start.2) | collective-permute-done | bytes 65568 | tf_op jit(solution)/shard_map/ppermute | solution.py:298
  13.9 0.1 collective-permute-done.1.refs_4_.refs_6_
  14.0 0.0 collective-permute-done.refs_2_.refs_4_
  14.0 0.4 %shard_map.113 = (f32[4,128,256]{2,1,0:T(8,128)S(1)}, f32[4,128,256]{2,1,0:T(8,128)S(1)}, f32[16,256]{1,0:T(8,128)S(1)}) custom-call(f32[8,128]{1,0:T(8,128)S(1)} %get-tuple-element.31.refs_0_, bf16[1024,128]{1,0:T(8,128)(2,1)S(1)} %get-tuple-element.32.refs_1_.refs_3_, bf16[1024,128]{1,0:T(8,128)(2,1)S(1)} %collective-permute-done.refs_2_.refs_4_, ...), custom_call_target="tpu_custom_call" | custom-call | flops 20000000000 | tf_op jit(solution)/shard_map/pallas_call | solution.py:286
  14.4 0.5 %collective-permute-start.4 = (f32[16,256]{1,0:T(8,128)S(1)}, f32[16,256]{1,0:T(8,128)S(1)}, u32[]{:S(2)}, u32[]{:S(2)}) collective-permute-start(f32[16,256]{1,0:T(8,128)S(1)} %get-tuple-element.34.own_ref), channel_id=1, source_target_pairs={{0,1},{1,0},{2,3},{3,2},{4,5},{5,4},{6,7},{7,6},{8,9},{9,8},{10,11... | collective-permute-start | bytes 49160 | tf_op jit(solution)/shard_map/ppermute | solution.py:298
  14.9 2.2 %collective-permute-done.5.input_other_ref = bf16[32,4096]{1,0:T(8,128)(2,1)S(1)} collective-permute-done((bf16[32,4096]{1,0:T(8,128)(2,1)S(1)}, bf16[32,4096]{1,0:T(8,128)(2,1)S(1)}, u32[]{:S(2)}, u32[]{:S(2)}) %collective-permute-start.5) | collective-permute-done | bytes 262176 | tf_op jit(solution)/shard_map/ppermute | solution.py:298
  17.1 1.1 %collective-permute-done.4.other_ref = f32[16,256]{1,0:T(8,128)S(1)} collective-permute-done((f32[16,256]{1,0:T(8,128)S(1)}, f32[16,256]{1,0:T(8,128)S(1)}, u32[]{:S(2)}, u32[]{:S(2)}) %collective-permute-start.4) | collective-permute-done | bytes 16416 | tf_op jit(solution)/shard_map/ppermute | solution.py:298
  18.2 0.2 shard_map.114
  18.4 0.1 collective-permute-start.10
  18.5 1.6 %collective-permute-start.9 = (f32[32,128]{1,0:T(8,128)S(1)}, f32[32,128]{1,0:T(8,128)S(1)}, u32[]{:S(2)}, u32[]{:S(2)}) collective-permute-start(f32[32,128]{1,0:T(8,128)S(1)} %get-tuple-element.46.refs_0_), channel_id=1, source_target_pairs={{0,16},{8,24},{16,0},{24,8},{1,17},{9,25},{17,1},{25,9},{2,18},{10... | collective-permute-start | bytes 49160 | tf_op jit(solution)/shard_map/ppermute | solution.py:298
  20.1 0.3 collective-permute-start.8
  20.4 0.4 %shard_map.115 = (f32[512,128]{1,0:T(8,128)S(1)}, bf16[512,128]{1,0:T(8,128)(2,1)S(1)}, f32[256,128]{1,0:T(8,128)S(1)}, bf16[256,128]{1,0:T(8,128)(2,1)S(1)}, bf...) custom-call(f32[8,256]{1,0:T(8,128)S(1)} %get-tuple-element.36.refs_0_, ...), custom_call_target="tpu_custom_call" | custom-call | flops 20000000000 | tf_op jit(solution)/shard_map/pallas_call | solution.py:286
  20.8 0.8 %collective-permute-start.6 = (bf16[512,128]{1,0:T(8,128)(2,1)S(1)}, bf16[512,128]{1,0:T(8,128)(2,1)S(1)}, u32[]{:S(2)}, u32[]{:S(2)}) collective-permute-start(bf16[512,128]{1,0:T(8,128)(2,1)S(1)} %get-tuple-element.40), channel_id=1, source_target_pairs={{0,1},{1,0},{2,3},{3,2},{4,5},{5,4},{6,7},{7,6},{8,9},{9,8},{10,11... | collective-permute-start | bytes 393224 | tf_op jit(solution)/shard_map/ppermute | solution.py:298
  21.6 3.6 %collective-permute-start.7 = (bf16[256,128]{1,0:T(8,128)(2,1)S(1)}, bf16[256,128]{1,0:T(8,128)(2,1)S(1)}, u32[]{:S(2)}, u32[]{:S(2)}) collective-permute-start(bf16[256,128]{1,0:T(8,128)(2,1)S(1)} %get-tuple-element.41), channel_id=1, source_target_pairs={{0,6},{1,7},{2,4},{3,5},{4,2},{5,3},{6,0},{7,1},{8,14},{9,15},{10,... | collective-permute-start | bytes 196616 | tf_op jit(solution)/shard_map/ppermute | solution.py:298
  25.2 0.0 collective-permute-done.10.refs_3_
  25.2 0.0 collective-permute-done.9.refs_2_
  25.2 0.0 collective-permute-done.8.refs_1_
  25.2 0.1 collective-permute-start.12
  25.3 0.8 %collective-permute-start.13 = (bf16[288,128]{1,0:T(8,128)(2,1)S(1)}, bf16[288,128]{1,0:T(8,128)(2,1)S(1)}, u32[]{:S(2)}, u32[]{:S(2)}) collective-permute-start(bf16[288,128]{1,0:T(8,128)(2,1)S(1)} %get-tuple-element.52), channel_id=1, source_target_pairs={{0,2},{1,3},{2,0},{3,1},{4,6},{5,7},{6,4},{7,5},{8,10},{9,11},{10,... | collective-permute-start | bytes 221192 | tf_op jit(solution)/shard_map/ppermute | solution.py:298
  26.1 3.6 %collective-permute-start.11 = (bf16[32,128]{1,0:T(8,128)(2,1)S(1)}, bf16[32,128]{1,0:T(8,128)(2,1)S(1)}, u32[]{:S(2)}, u32[]{:S(2)}) collective-permute-start(bf16[32,128]{1,0:T(8,128)(2,1)S(1)} %get-tuple-element.50), channel_id=1, source_target_pairs={{0,6},{1,7},{2,4},{3,5},{4,2},{5,3},{6,0},{7,1},{8,14},{9,15},{10,... | collective-permute-start | bytes 24584 | tf_op jit(solution)/shard_map/ppermute | solution.py:298
  29.7 0.0 collective-permute-done.7.far_ref
  29.7 0.0 collective-permute-done.6.other_ref
  29.7 0.8 %shard_map.116 = (bf16[32,2048]{1,0:T(8,128)(2,1)}, f32[64,128]{1,0:T(8,128)S(1)}, f32[256,128]{1,0:T(8,128)S(1)}) custom-call(f32[64,128]{1,0:T(8,128)S(1)} %get-tuple-element.30.trig_ref, f32[512,128]{1,0:T(8,128)S(1)} %get-tuple-element.39.own_ref, bf16[512,128]{1,0:T(8,128)(2,1)S(1)} %collective-permute-done.6.other_ref, ...), custom_call_target="tpu_custom_call" | custom-call | flops 500000000 | tf_op jit(solution)/shard_map/pallas_call | solution.py:286
  30.5 1.6 %collective-permute-done.11.refs_3_ = bf16[32,128]{1,0:T(8,128)(2,1)S(1)} collective-permute-done((bf16[32,128]{1,0:T(8,128)(2,1)S(1)}, bf16[32,128]{1,0:T(8,128)(2,1)S(1)}, u32[]{:S(2)}, u32[]{:S(2)}) %collective-permute-start.11) | collective-permute-done | bytes 8224 | tf_op jit(solution)/shard_map/ppermute | solution.py:298
  32.1 0.0 collective-permute-done.12.refs_4_
  32.1 0.0 collective-permute-done.13.refs_5_
  32.1 0.7 %shard_map.118 = (bf16[32,512]{1,0:T(8,128)(2,1)}, bf16[32,512]{1,0:T(8,128)(2,1)}, f32[32,128]{1,0:T(8,128)}) custom-call(f32[64,128]{1,0:T(8,128)S(1)} %get-tuple-element.44.refs_0_, f32[256,128]{1,0:T(8,128)S(1)} %get-tuple-element.45.refs_1_, f32[32,128]{1,0:T(8,128)S(1)} %get-tuple-element.49.refs_2_, ...), custom_call_target="tpu_custom_call" | custom-call | tf_op jit(solution)/shard_map/pallas_call | solution.py:286
  (1 shorter events, 0.0 us)
Async XLA Ops:
  0.6 8.7 %copy-start = (bf16[1,32,4096]{2,1,0:T(8,128)(2,1)S(1)}, bf16[1,32,4096]{2,1,0:T(8,128)(2,1)}, u32[]{:S(2)}) copy-start(bf16[1,32,4096]{2,1,0:T(8,128)(2,1)} %param.12) | copy-start | bytes 786436
  1.9 12.1 %collective-permute-start = (bf16[1024,128]{1,0:T(8,128)(2,1)S(1)}, bf16[1024,128]{1,0:T(8,128)(2,1)S(1)}, u32[]{:S(2)}, u32[]{:S(2)}) collective-permute-start(bf16[1024,128]{1,0:T(8,128)(2,1)S(1)} %get-tuple-element.32.refs_1_.refs_3_), channel_id=1, source_target_pairs={{0,1},{1,0},{2,3},{3,2},{4,5},{5,4},{6,7},{7,6},{8,9},{9,8},{10,11... | collective-permute-start | bytes 786440 | tf_op jit(solution)/shard_map/ppermute | solution.py:298
  5.0 6.9 %collective-permute-start.3 = (bf16[256,128]{1,0:T(8,128)(2,1)S(1)}, bf16[256,128]{1,0:T(8,128)(2,1)S(1)}, u32[]{:S(2)}, u32[]{:S(2)}) collective-permute-start(bf16[256,128]{1,0:T(8,128)(2,1)S(1)} %get-tuple-element.33.refs_3_.refs_5_), channel_id=1, source_target_pairs={{0,6},{1,7},{2,4},{3,5},{4,2},{5,3},{6,0},{7,1},{8,14},{9,15},{10,... | collective-permute-start | bytes 196616 | tf_op jit(solution)/shard_map/ppermute | solution.py:298
  8.6 5.4 %collective-permute-start.2 = (bf16[256,128]{1,0:T(8,128)(2,1)S(1)}, bf16[256,128]{1,0:T(8,128)(2,1)S(1)}, u32[]{:S(2)}, u32[]{:S(2)}) collective-permute-start(bf16[256,128]{1,0:T(8,128)(2,1)S(1)} %get-tuple-element.33.refs_3_.refs_5_), channel_id=1, source_target_pairs={{0,4},{1,5},{2,6},{3,7},{4,0},{5,1},{6,2},{7,3},{8,12},{9,13},{10,... | collective-permute-start | bytes 196616 | tf_op jit(solution)/shard_map/ppermute | solution.py:298
  8.6 5.4 %collective-permute-start.1 = (bf16[256,128]{1,0:T(8,128)(2,1)S(1)}, bf16[256,128]{1,0:T(8,128)(2,1)S(1)}, u32[]{:S(2)}, u32[]{:S(2)}) collective-permute-start(bf16[256,128]{1,0:T(8,128)(2,1)S(1)} %get-tuple-element.33.refs_3_.refs_5_), channel_id=1, source_target_pairs={{0,2},{1,3},{2,0},{3,1},{4,6},{5,7},{6,4},{7,5},{8,10},{9,11},{10,... | collective-permute-start | bytes 196616 | tf_op jit(solution)/shard_map/ppermute | solution.py:298
  9.4 7.7 %collective-permute-start.5 = (bf16[32,4096]{1,0:T(8,128)(2,1)S(1)}, bf16[32,4096]{1,0:T(8,128)(2,1)S(1)}, u32[]{:S(2)}, u32[]{:S(2)}) collective-permute-start(bf16[32,4096]{1,0:T(8,128)(2,1)S(1)} %bitcast.11), channel_id=1, source_target_pairs={{0,1},{1,0},{2,3},{3,2},{4,5},{5,4},{6,7},{7,6},{8,9},{9,8},{10,11... | collective-permute-start | bytes 786440 | tf_op jit(solution)/shard_map/ppermute | solution.py:298
  14.4 3.8 %collective-permute-start.4 = (f32[16,256]{1,0:T(8,128)S(1)}, f32[16,256]{1,0:T(8,128)S(1)}, u32[]{:S(2)}, u32[]{:S(2)}) collective-permute-start(f32[16,256]{1,0:T(8,128)S(1)} %get-tuple-element.34.own_ref), channel_id=1, source_target_pairs={{0,1},{1,0},{2,3},{3,2},{4,5},{5,4},{6,7},{7,6},{8,9},{9,8},{10,11... | collective-permute-start | bytes 49160 | tf_op jit(solution)/shard_map/ppermute | solution.py:298
  18.4 6.8 %collective-permute-start.10 = (f32[32,128]{1,0:T(8,128)S(1)}, f32[32,128]{1,0:T(8,128)S(1)}, u32[]{:S(2)}, u32[]{:S(2)}) collective-permute-start(f32[32,128]{1,0:T(8,128)S(1)} %get-tuple-element.46.refs_0_), channel_id=1, source_target_pairs={{0,24},{8,16},{16,8},{24,0},{1,25},{9,17},{17,9},{25,1},{2,26},{10... | collective-permute-start | bytes 49160 | tf_op jit(solution)/shard_map/ppermute | solution.py:298
  18.5 6.7 %collective-permute-start.9 = (f32[32,128]{1,0:T(8,128)S(1)}, f32[32,128]{1,0:T(8,128)S(1)}, u32[]{:S(2)}, u32[]{:S(2)}) collective-permute-start(f32[32,128]{1,0:T(8,128)S(1)} %get-tuple-element.46.refs_0_), channel_id=1, source_target_pairs={{0,16},{8,24},{16,0},{24,8},{1,17},{9,25},{17,1},{25,9},{2,18},{10... | collective-permute-start | bytes 49160 | tf_op jit(solution)/shard_map/ppermute | solution.py:298
  20.1 5.1 %collective-permute-start.8 = (f32[32,128]{1,0:T(8,128)S(1)}, f32[32,128]{1,0:T(8,128)S(1)}, u32[]{:S(2)}, u32[]{:S(2)}) collective-permute-start(f32[32,128]{1,0:T(8,128)S(1)} %get-tuple-element.46.refs_0_), channel_id=1, source_target_pairs={{0,8},{8,0},{16,24},{24,16},{1,9},{9,1},{17,25},{25,17},{2,10},{10... | collective-permute-start | bytes 49160 | tf_op jit(solution)/shard_map/ppermute | solution.py:298
  20.8 8.9 %collective-permute-start.6 = (bf16[512,128]{1,0:T(8,128)(2,1)S(1)}, bf16[512,128]{1,0:T(8,128)(2,1)S(1)}, u32[]{:S(2)}, u32[]{:S(2)}) collective-permute-start(bf16[512,128]{1,0:T(8,128)(2,1)S(1)} %get-tuple-element.40), channel_id=1, source_target_pairs={{0,1},{1,0},{2,3},{3,2},{4,5},{5,4},{6,7},{7,6},{8,9},{9,8},{10,11... | collective-permute-start | bytes 393224 | tf_op jit(solution)/shard_map/ppermute | solution.py:298
  21.6 8.1 %collective-permute-start.7 = (bf16[256,128]{1,0:T(8,128)(2,1)S(1)}, bf16[256,128]{1,0:T(8,128)(2,1)S(1)}, u32[]{:S(2)}, u32[]{:S(2)}) collective-permute-start(bf16[256,128]{1,0:T(8,128)(2,1)S(1)} %get-tuple-element.41), channel_id=1, source_target_pairs={{0,6},{1,7},{2,4},{3,5},{4,2},{5,3},{6,0},{7,1},{8,14},{9,15},{10,... | collective-permute-start | bytes 196616 | tf_op jit(solution)/shard_map/ppermute | solution.py:298
  25.2 6.9 %collective-permute-start.12 = (bf16[288,128]{1,0:T(8,128)(2,1)S(1)}, bf16[288,128]{1,0:T(8,128)(2,1)S(1)}, u32[]{:S(2)}, u32[]{:S(2)}) collective-permute-start(bf16[288,128]{1,0:T(8,128)(2,1)S(1)} %get-tuple-element.51), channel_id=1, source_target_pairs={{0,4},{1,5},{2,6},{3,7},{4,0},{5,1},{6,2},{7,3},{8,12},{9,13},{10,... | collective-permute-start | bytes 221192 | tf_op jit(solution)/shard_map/ppermute | solution.py:298
  25.3 6.8 %collective-permute-start.13 = (bf16[288,128]{1,0:T(8,128)(2,1)S(1)}, bf16[288,128]{1,0:T(8,128)(2,1)S(1)}, u32[]{:S(2)}, u32[]{:S(2)}) collective-permute-start(bf16[288,128]{1,0:T(8,128)(2,1)S(1)} %get-tuple-element.52), channel_id=1, source_target_pairs={{0,2},{1,3},{2,0},{3,1},{4,6},{5,7},{6,4},{7,5},{8,10},{9,11},{10,... | collective-permute-start | bytes 221192 | tf_op jit(solution)/shard_map/ppermute | solution.py:298
  26.1 6.0 %collective-permute-start.11 = (bf16[32,128]{1,0:T(8,128)(2,1)S(1)}, bf16[32,128]{1,0:T(8,128)(2,1)S(1)}, u32[]{:S(2)}, u32[]{:S(2)}) collective-permute-start(bf16[32,128]{1,0:T(8,128)(2,1)S(1)} %get-tuple-element.50), channel_id=1, source_target_pairs={{0,6},{1,7},{2,4},{3,5},{4,2},{5,3},{6,0},{7,1},{8,14},{9,15},{10,... | collective-permute-start | bytes 24584 | tf_op jit(solution)/shard_map/ppermute | solution.py:298

commit v6 on v5

--- a/solution.py
+++ b/solution.py
@@ -18,7 +18,7 @@
 VMEM_LIMIT = 32 * 1024 * 1024
 SCORES_COST = 20 * 10**9
 TERMS_COST = 20 * 10**9
-RIDE_COST = 10**9
+RIDE_COST = 20 * 10**9
 QUERY_COST = 5 * 10**8
 
 
@@ -366,18 +366,18 @@
         cost=TERMS_COST,
     )
     query_back = swap(query_send)
-    far = exchange(terms[-1], "ctx", 2 * (half - 1), count)
+    early = half // 2
+    far = exchange(terms[early - 1], "ctx", 2 * early, count)
+    others = [step for step in reversed(range(1, half)) if step != early]
     router, router_send, *terms = call(
         functools.partial(ride_kernel, groups),
         [near((lines, HD), f32), near((lines, HD), bf16)]
-        + [near((2 * KVH * slots + lines, HD), bf16)] * (half - 2),
-        [*routers, *terms[:-1]],
+        + [near((2 * KVH * slots + lines, HD), bf16)] * len(others),
+        [*routers, *[terms[step - 1] for step in others]],
         cost=RIDE_COST,
     )
-    terms = [
-        exchange(terms[step - 1], "ctx", 2 * step, count) for step in reversed(range(1, half - 1))
-    ]
-    alone = exchange(router_send, "ctx", 2 * (half - 1), count)
+    terms = [exchange(term, "ctx", 2 * step, count) for step, term in zip(others, terms)]
+    alone = exchange(router_send, "ctx", 2 * early, count)
     shape = jax.ShapeDtypeStruct
     query_grad, trig, term_own = call(
         query_kernel,

time: 33.1 us -> 32.3 us (0.976)
  starting transfers between devices: 19 us -> 18 us
    ppermute x14, starting transfers between devices: 19 us -> 18 us  [exchange(): return lax.ppermute(array, axis, [(at, at ^ step) for at in range(size)])]
  transfers between devices with their start and end apart: 14 -> 14, of which waited for: 6 -> 7; matrix products, arithmetic and copies ran while one was open for 0% -> 0% of each run, Pallas kernels for 8% -> 9%
where the time goes in v6:
time: 32.3 us; the launch traced here: 32 us
  starting transfers between devices  18 us (56%)
  waiting for transfers between devices  8.35 us (26%)
  Pallas kernels  4.96 us (15%)
  between operations  0.71 us (2%)
    ppermute x14, starting transfers between devices, exchange(): return lax.ppermute(array, axis, [(at, at ^ step) for at in range(size)])  18 us
    ppermute x14, waiting for transfers between devices, exchange(): return lax.ppermute(array, axis, [(at, at ^ step) for at in range(size)])  8.35 us
    pallas_call x8, Pallas kernels, call(): pl.pallas_call(kernel, out_shape=outs, in_specs=[local] * len(args) + [di...  4.96 us
  transfers between devices with their start and end apart: 14, of which 7 were waited for; matrix products, arithmetic and copies ran while one was open for 0% of the time, Pallas kernels for 9%

profile of v6, /device:TPU:0, one launch (start us, length us, event | category | flops | bytes accessed | tf_op | source)
XLA Modules:
  0.0 32.0 jit_solution(3498720200750124583)
XLA Ops:
  0.6 0.0 copy-start
  0.6 1.3 %shard_map.111 = (bf16[256,128]{1,0:T(8,128)(2,1)S(1)}, bf16[1024,128]{1,0:T(8,128)(2,1)S(1)}, f32[64,128]{1,0:T(8,128)S(1)}) custom-call(s32[1,32]{1,0:T(1,128)} %refs_0_.1, f32[2,128]{1,0:T(2,128)} %constant.2.clone.refs_1_, bf16[32,512]{1,0:T(8,128)(2,1)} %bitcast.14, bf16[32,512]{1,0:T(8,128)(2,1)} %bitcast.15, bf16[32,2048]{1,0:T(8,128)(2,1)} %bitcast.12, ...), custom_call_target="tpu_custom_call" | custom-call | tf_op jit(solution)/shard_map/pallas_call | solution.py:286
  1.9 3.0 %collective-permute-start = (bf16[1024,128]{1,0:T(8,128)(2,1)S(1)}, bf16[1024,128]{1,0:T(8,128)(2,1)S(1)}, u32[]{:S(2)}, u32[]{:S(2)}) collective-permute-start(bf16[1024,128]{1,0:T(8,128)(2,1)S(1)} %get-tuple-element.32.refs_1_.refs_3_), channel_id=1, source_target_pairs={{0,1},{1,0},{2,3},{3,2},{4,5},{5,4},{6,7},{7,6},{8,9},{9,8},{10,11... | collective-permute-start | bytes 786440 | tf_op jit(solution)/shard_map/ppermute | solution.py:298
  5.0 3.6 %collective-permute-start.3 = (bf16[256,128]{1,0:T(8,128)(2,1)S(1)}, bf16[256,128]{1,0:T(8,128)(2,1)S(1)}, u32[]{:S(2)}, u32[]{:S(2)}) collective-permute-start(bf16[256,128]{1,0:T(8,128)(2,1)S(1)} %get-tuple-element.33.refs_3_.refs_5_), channel_id=1, source_target_pairs={{0,6},{1,7},{2,4},{3,5},{4,2},{5,3},{6,0},{7,1},{8,14},{9,15},{10,... | collective-permute-start | bytes 196616 | tf_op jit(solution)/shard_map/ppermute | solution.py:298
  8.6 0.0 collective-permute-start.2
  8.6 0.8 %collective-permute-start.1 = (bf16[256,128]{1,0:T(8,128)(2,1)S(1)}, bf16[256,128]{1,0:T(8,128)(2,1)S(1)}, u32[]{:S(2)}, u32[]{:S(2)}) collective-permute-start(bf16[256,128]{1,0:T(8,128)(2,1)S(1)} %get-tuple-element.33.refs_3_.refs_5_), channel_id=1, source_target_pairs={{0,2},{1,3},{2,0},{3,1},{4,6},{5,7},{6,4},{7,5},{8,10},{9,11},{10,... | collective-permute-start | bytes 196616 | tf_op jit(solution)/shard_map/ppermute | solution.py:298
  9.4 0.0 copy-done
  9.4 0.3 collective-permute-start.5
  9.6 1.1 %shard_map.112 = (f32[8,128]{1,0:T(8,128)S(1)}, bf16[32,4096]{1,0:T(8,128)(2,1)S(1)}) custom-call(f32[32,128]{1,0:T(8,128)} %bitcast.16, bf16[32,4096]{1,0:T(8,128)(2,1)} %bitcast.10), custom_call_target="tpu_custom_call" | custom-call | tf_op jit(solution)/shard_map/pallas_call | solution.py:286
  10.8 1.0 %collective-permute-done.3.refs_6_.refs_8_ = bf16[256,128]{1,0:T(8,128)(2,1)S(1)} collective-permute-done((bf16[256,128]{1,0:T(8,128)(2,1)S(1)}, bf16[256,128]{1,0:T(8,128)(2,1)S(1)}, u32[]{:S(2)}, u32[]{:S(2)}) %collective-permute-start.3) | collective-permute-done | bytes 65568 | tf_op jit(solution)/shard_map/ppermute | solution.py:298
  11.8 2.1 %collective-permute-done.2.refs_5_.refs_7_ = bf16[256,128]{1,0:T(8,128)(2,1)S(1)} collective-permute-done((bf16[256,128]{1,0:T(8,128)(2,1)S(1)}, bf16[256,128]{1,0:T(8,128)(2,1)S(1)}, u32[]{:S(2)}, u32[]{:S(2)}) %collective-permute-start.2) | collective-permute-done | bytes 65568 | tf_op jit(solution)/shard_map/ppermute | solution.py:298
  13.9 0.1 collective-permute-done.1.refs_4_.refs_6_
  14.0 0.0 collective-permute-done.refs_2_.refs_4_
  14.0 0.4 %shard_map.113 = (f32[4,128,256]{2,1,0:T(8,128)S(1)}, f32[4,128,256]{2,1,0:T(8,128)S(1)}, f32[16,256]{1,0:T(8,128)S(1)}) custom-call(f32[8,128]{1,0:T(8,128)S(1)} %get-tuple-element.31.refs_0_, bf16[1024,128]{1,0:T(8,128)(2,1)S(1)} %get-tuple-element.32.refs_1_.refs_3_, bf16[1024,128]{1,0:T(8,128)(2,1)S(1)} %collective-permute-done.refs_2_.refs_4_, ...), custom_call_target="tpu_custom_call" | custom-call | flops 20000000000 | tf_op jit(solution)/shard_map/pallas_call | solution.py:286
  14.4 0.5 %collective-permute-start.4 = (f32[16,256]{1,0:T(8,128)S(1)}, f32[16,256]{1,0:T(8,128)S(1)}, u32[]{:S(2)}, u32[]{:S(2)}) collective-permute-start(f32[16,256]{1,0:T(8,128)S(1)} %get-tuple-element.34.own_ref), channel_id=1, source_target_pairs={{0,1},{1,0},{2,3},{3,2},{4,5},{5,4},{6,7},{7,6},{8,9},{9,8},{10,11... | collective-permute-start | bytes 49160 | tf_op jit(solution)/shard_map/ppermute | solution.py:298
  14.9 2.2 %collective-permute-done.5.input_other_ref = bf16[32,4096]{1,0:T(8,128)(2,1)S(1)} collective-permute-done((bf16[32,4096]{1,0:T(8,128)(2,1)S(1)}, bf16[32,4096]{1,0:T(8,128)(2,1)S(1)}, u32[]{:S(2)}, u32[]{:S(2)}) %collective-permute-start.5) | collective-permute-done | bytes 262176 | tf_op jit(solution)/shard_map/ppermute | solution.py:298
  17.1 1.1 %collective-permute-done.4.other_ref = f32[16,256]{1,0:T(8,128)S(1)} collective-permute-done((f32[16,256]{1,0:T(8,128)S(1)}, f32[16,256]{1,0:T(8,128)S(1)}, u32[]{:S(2)}, u32[]{:S(2)}) %collective-permute-start.4) | collective-permute-done | bytes 16416 | tf_op jit(solution)/shard_map/ppermute | solution.py:298
  18.2 0.2 shard_map.114
  18.4 0.1 collective-permute-start.10
  18.5 1.6 %collective-permute-start.9 = (f32[32,128]{1,0:T(8,128)S(1)}, f32[32,128]{1,0:T(8,128)S(1)}, u32[]{:S(2)}, u32[]{:S(2)}) collective-permute-start(f32[32,128]{1,0:T(8,128)S(1)} %get-tuple-element.46.refs_0_), channel_id=1, source_target_pairs={{0,16},{8,24},{16,0},{24,8},{1,17},{9,25},{17,1},{25,9},{2,18},{10... | collective-permute-start | bytes 49160 | tf_op jit(solution)/shard_map/ppermute | solution.py:298
  20.1 0.3 collective-permute-start.8
  20.4 0.4 %shard_map.115 = (f32[512,128]{1,0:T(8,128)S(1)}, bf16[512,128]{1,0:T(8,128)(2,1)S(1)}, f32[256,128]{1,0:T(8,128)S(1)}, bf16[256,128]{1,0:T(8,128)(2,1)S(1)}, bf...) custom-call(f32[8,256]{1,0:T(8,128)S(1)} %get-tuple-element.36.refs_0_, ...), custom_call_target="tpu_custom_call" | custom-call | flops 20000000000 | tf_op jit(solution)/shard_map/pallas_call | solution.py:286
  20.8 1.9 %collective-permute-start.7 = (bf16[256,128]{1,0:T(8,128)(2,1)S(1)}, bf16[256,128]{1,0:T(8,128)(2,1)S(1)}, u32[]{:S(2)}, u32[]{:S(2)}) collective-permute-start(bf16[256,128]{1,0:T(8,128)(2,1)S(1)} %get-tuple-element.41), channel_id=1, source_target_pairs={{0,4},{1,5},{2,6},{3,7},{4,0},{5,1},{6,2},{7,3},{8,12},{9,13},{10,... | collective-permute-start | bytes 196616 | tf_op jit(solution)/shard_map/ppermute | solution.py:298
  22.7 1.5 %collective-permute-start.6 = (bf16[512,128]{1,0:T(8,128)(2,1)S(1)}, bf16[512,128]{1,0:T(8,128)(2,1)S(1)}, u32[]{:S(2)}, u32[]{:S(2)}) collective-permute-start(bf16[512,128]{1,0:T(8,128)(2,1)S(1)} %get-tuple-element.40), channel_id=1, source_target_pairs={{0,1},{1,0},{2,3},{3,2},{4,5},{5,4},{6,7},{7,6},{8,9},{9,8},{10,11... | collective-permute-start | bytes 393224 | tf_op jit(solution)/shard_map/ppermute | solution.py:298
  24.2 0.0 collective-permute-done.10.refs_3_
  24.2 0.0 collective-permute-done.9.refs_2_
  24.2 0.0 collective-permute-done.8.refs_1_
  24.2 1.4 %collective-permute-start.12 = (bf16[288,128]{1,0:T(8,128)(2,1)S(1)}, bf16[288,128]{1,0:T(8,128)(2,1)S(1)}, u32[]{:S(2)}, u32[]{:S(2)}) collective-permute-start(bf16[288,128]{1,0:T(8,128)(2,1)S(1)} %get-tuple-element.51), channel_id=1, source_target_pairs={{0,6},{1,7},{2,4},{3,5},{4,2},{5,3},{6,0},{7,1},{8,14},{9,15},{10,... | collective-permute-start | bytes 221192 | tf_op jit(solution)/shard_map/ppermute | solution.py:298
  25.6 0.3 collective-permute-start.13
  25.9 2.7 %collective-permute-start.11 = (bf16[32,128]{1,0:T(8,128)(2,1)S(1)}, bf16[32,128]{1,0:T(8,128)(2,1)S(1)}, u32[]{:S(2)}, u32[]{:S(2)}) collective-permute-start(bf16[32,128]{1,0:T(8,128)(2,1)S(1)} %get-tuple-element.50), channel_id=1, source_target_pairs={{0,4},{1,5},{2,6},{3,7},{4,0},{5,1},{6,2},{7,3},{8,12},{9,13},{10,... | collective-permute-start | bytes 24584 | tf_op jit(solution)/shard_map/ppermute | solution.py:298
  28.7 0.0 collective-permute-done.7.far_ref
  28.7 0.0 collective-permute-done.6.other_ref
  28.7 0.8 %shard_map.116 = (bf16[32,2048]{1,0:T(8,128)(2,1)}, f32[64,128]{1,0:T(8,128)S(1)}, f32[256,128]{1,0:T(8,128)S(1)}) custom-call(f32[64,128]{1,0:T(8,128)S(1)} %get-tuple-element.30.trig_ref, f32[512,128]{1,0:T(8,128)S(1)} %get-tuple-element.39.own_ref, bf16[512,128]{1,0:T(8,128)(2,1)S(1)} %collective-permute-done.6.other_ref, ...), custom_call_target="tpu_custom_call" | custom-call | flops 500000000 | tf_op jit(solution)/shard_map/pallas_call | solution.py:286
  29.5 1.6 %collective-permute-done.11.refs_3_ = bf16[32,128]{1,0:T(8,128)(2,1)S(1)} collective-permute-done((bf16[32,128]{1,0:T(8,128)(2,1)S(1)}, bf16[32,128]{1,0:T(8,128)(2,1)S(1)}, u32[]{:S(2)}, u32[]{:S(2)}) %collective-permute-start.11) | collective-permute-done | bytes 8224 | tf_op jit(solution)/shard_map/ppermute | solution.py:298
  31.0 0.0 collective-permute-done.12.refs_4_
  31.0 0.3 collective-permute-done.13.refs_5_
  31.3 0.7 %shard_map.118 = (bf16[32,512]{1,0:T(8,128)(2,1)}, bf16[32,512]{1,0:T(8,128)(2,1)}, f32[32,128]{1,0:T(8,128)}) custom-call(f32[64,128]{1,0:T(8,128)S(1)} %get-tuple-element.44.refs_0_, f32[256,128]{1,0:T(8,128)S(1)} %get-tuple-element.45.refs_1_, f32[32,128]{1,0:T(8,128)S(1)} %get-tuple-element.49.refs_2_, ...), custom_call_target="tpu_custom_call" | custom-call | tf_op jit(solution)/shard_map/pallas_call | solution.py:286
  (1 shorter events, 0.0 us)
Async XLA Ops:
  0.6 8.7 %copy-start = (bf16[1,32,4096]{2,1,0:T(8,128)(2,1)S(1)}, bf16[1,32,4096]{2,1,0:T(8,128)(2,1)}, u32[]{:S(2)}) copy-start(bf16[1,32,4096]{2,1,0:T(8,128)(2,1)} %param.12) | copy-start | bytes 786436
  1.9 12.1 %collective-permute-start = (bf16[1024,128]{1,0:T(8,128)(2,1)S(1)}, bf16[1024,128]{1,0:T(8,128)(2,1)S(1)}, u32[]{:S(2)}, u32[]{:S(2)}) collective-permute-start(bf16[1024,128]{1,0:T(8,128)(2,1)S(1)} %get-tuple-element.32.refs_1_.refs_3_), channel_id=1, source_target_pairs={{0,1},{1,0},{2,3},{3,2},{4,5},{5,4},{6,7},{7,6},{8,9},{9,8},{10,11... | collective-permute-start | bytes 786440 | tf_op jit(solution)/shard_map/ppermute | solution.py:298
  5.0 6.9 %collective-permute-start.3 = (bf16[256,128]{1,0:T(8,128)(2,1)S(1)}, bf16[256,128]{1,0:T(8,128)(2,1)S(1)}, u32[]{:S(2)}, u32[]{:S(2)}) collective-permute-start(bf16[256,128]{1,0:T(8,128)(2,1)S(1)} %get-tuple-element.33.refs_3_.refs_5_), channel_id=1, source_target_pairs={{0,6},{1,7},{2,4},{3,5},{4,2},{5,3},{6,0},{7,1},{8,14},{9,15},{10,... | collective-permute-start | bytes 196616 | tf_op jit(solution)/shard_map/ppermute | solution.py:298
  8.6 5.4 %collective-permute-start.2 = (bf16[256,128]{1,0:T(8,128)(2,1)S(1)}, bf16[256,128]{1,0:T(8,128)(2,1)S(1)}, u32[]{:S(2)}, u32[]{:S(2)}) collective-permute-start(bf16[256,128]{1,0:T(8,128)(2,1)S(1)} %get-tuple-element.33.refs_3_.refs_5_), channel_id=1, source_target_pairs={{0,4},{1,5},{2,6},{3,7},{4,0},{5,1},{6,2},{7,3},{8,12},{9,13},{10,... | collective-permute-start | bytes 196616 | tf_op jit(solution)/shard_map/ppermute | solution.py:298
  8.6 5.4 %collective-permute-start.1 = (bf16[256,128]{1,0:T(8,128)(2,1)S(1)}, bf16[256,128]{1,0:T(8,128)(2,1)S(1)}, u32[]{:S(2)}, u32[]{:S(2)}) collective-permute-start(bf16[256,128]{1,0:T(8,128)(2,1)S(1)} %get-tuple-element.33.refs_3_.refs_5_), channel_id=1, source_target_pairs={{0,2},{1,3},{2,0},{3,1},{4,6},{5,7},{6,4},{7,5},{8,10},{9,11},{10,... | collective-permute-start | bytes 196616 | tf_op jit(solution)/shard_map/ppermute | solution.py:298
  9.4 7.7 %collective-permute-start.5 = (bf16[32,4096]{1,0:T(8,128)(2,1)S(1)}, bf16[32,4096]{1,0:T(8,128)(2,1)S(1)}, u32[]{:S(2)}, u32[]{:S(2)}) collective-permute-start(bf16[32,4096]{1,0:T(8,128)(2,1)S(1)} %bitcast.11), channel_id=1, source_target_pairs={{0,1},{1,0},{2,3},{3,2},{4,5},{5,4},{6,7},{7,6},{8,9},{9,8},{10,11... | collective-permute-start | bytes 786440 | tf_op jit(solution)/shard_map/ppermute | solution.py:298
  14.4 3.8 %collective-permute-start.4 = (f32[16,256]{1,0:T(8,128)S(1)}, f32[16,256]{1,0:T(8,128)S(1)}, u32[]{:S(2)}, u32[]{:S(2)}) collective-permute-start(f32[16,256]{1,0:T(8,128)S(1)} %get-tuple-element.34.own_ref), channel_id=1, source_target_pairs={{0,1},{1,0},{2,3},{3,2},{4,5},{5,4},{6,7},{7,6},{8,9},{9,8},{10,11... | collective-permute-start | bytes 49160 | tf_op jit(solution)/shard_map/ppermute | solution.py:298
  18.4 5.8 %collective-permute-start.10 = (f32[32,128]{1,0:T(8,128)S(1)}, f32[32,128]{1,0:T(8,128)S(1)}, u32[]{:S(2)}, u32[]{:S(2)}) collective-permute-start(f32[32,128]{1,0:T(8,128)S(1)} %get-tuple-element.46.refs_0_), channel_id=1, source_target_pairs={{0,24},{8,16},{16,8},{24,0},{1,25},{9,17},{17,9},{25,1},{2,26},{10... | collective-permute-start | bytes 49160 | tf_op jit(solution)/shard_map/ppermute | solution.py:298
  18.5 5.7 %collective-permute-start.9 = (f32[32,128]{1,0:T(8,128)S(1)}, f32[32,128]{1,0:T(8,128)S(1)}, u32[]{:S(2)}, u32[]{:S(2)}) collective-permute-start(f32[32,128]{1,0:T(8,128)S(1)} %get-tuple-element.46.refs_0_), channel_id=1, source_target_pairs={{0,16},{8,24},{16,0},{24,8},{1,17},{9,25},{17,1},{25,9},{2,18},{10... | collective-permute-start | bytes 49160 | tf_op jit(solution)/shard_map/ppermute | solution.py:298
  20.1 4.1 %collective-permute-start.8 = (f32[32,128]{1,0:T(8,128)S(1)}, f32[32,128]{1,0:T(8,128)S(1)}, u32[]{:S(2)}, u32[]{:S(2)}) collective-permute-start(f32[32,128]{1,0:T(8,128)S(1)} %get-tuple-element.46.refs_0_), channel_id=1, source_target_pairs={{0,8},{8,0},{16,24},{24,16},{1,9},{9,1},{17,25},{25,17},{2,10},{10... | collective-permute-start | bytes 49160 | tf_op jit(solution)/shard_map/ppermute | solution.py:298
  20.8 7.9 %collective-permute-start.7 = (bf16[256,128]{1,0:T(8,128)(2,1)S(1)}, bf16[256,128]{1,0:T(8,128)(2,1)S(1)}, u32[]{:S(2)}, u32[]{:S(2)}) collective-permute-start(bf16[256,128]{1,0:T(8,128)(2,1)S(1)} %get-tuple-element.41), channel_id=1, source_target_pairs={{0,4},{1,5},{2,6},{3,7},{4,0},{5,1},{6,2},{7,3},{8,12},{9,13},{10,... | collective-permute-start | bytes 196616 | tf_op jit(solution)/shard_map/ppermute | solution.py:298
  22.7 6.0 %collective-permute-start.6 = (bf16[512,128]{1,0:T(8,128)(2,1)S(1)}, bf16[512,128]{1,0:T(8,128)(2,1)S(1)}, u32[]{:S(2)}, u32[]{:S(2)}) collective-permute-start(bf16[512,128]{1,0:T(8,128)(2,1)S(1)} %get-tuple-element.40), channel_id=1, source_target_pairs={{0,1},{1,0},{2,3},{3,2},{4,5},{5,4},{6,7},{7,6},{8,9},{9,8},{10,11... | collective-permute-start | bytes 393224 | tf_op jit(solution)/shard_map/ppermute | solution.py:298
  24.2 6.8 %collective-permute-start.12 = (bf16[288,128]{1,0:T(8,128)(2,1)S(1)}, bf16[288,128]{1,0:T(8,128)(2,1)S(1)}, u32[]{:S(2)}, u32[]{:S(2)}) collective-permute-start(bf16[288,128]{1,0:T(8,128)(2,1)S(1)} %get-tuple-element.51), channel_id=1, source_target_pairs={{0,6},{1,7},{2,4},{3,5},{4,2},{5,3},{6,0},{7,1},{8,14},{9,15},{10,... | collective-permute-start | bytes 221192 | tf_op jit(solution)/shard_map/ppermute | solution.py:298
  25.6 5.7 %collective-permute-start.13 = (bf16[288,128]{1,0:T(8,128)(2,1)S(1)}, bf16[288,128]{1,0:T(8,128)(2,1)S(1)}, u32[]{:S(2)}, u32[]{:S(2)}) collective-permute-start(bf16[288,128]{1,0:T(8,128)(2,1)S(1)} %get-tuple-element.52), channel_id=1, source_target_pairs={{0,2},{1,3},{2,0},{3,1},{4,6},{5,7},{6,4},{7,5},{8,10},{9,11},{10,... | collective-permute-start | bytes 221192 | tf_op jit(solution)/shard_map/ppermute | solution.py:298
  25.9 5.1 %collective-permute-start.11 = (bf16[32,128]{1,0:T(8,128)(2,1)S(1)}, bf16[32,128]{1,0:T(8,128)(2,1)S(1)}, u32[]{:S(2)}, u32[]{:S(2)}) collective-permute-start(bf16[32,128]{1,0:T(8,128)(2,1)S(1)} %get-tuple-element.50), channel_id=1, source_target_pairs={{0,4},{1,5},{2,6},{3,7},{4,0},{5,1},{6,2},{7,3},{8,12},{9,13},{10,... | collective-permute-start | bytes 24584 | tf_op jit(solution)/shard_map/ppermute | solution.py:298

commit v7 on v6

--- a/solution.py
+++ b/solution.py
@@ -48,9 +48,9 @@
 
 
 def prepare_kernel(*refs):
-    place_hbm, table_hbm, key_hbm, value_hbm, query_hbm, upstream_hbm = refs[:6]
-    pair_ref, query_out, trig_ref = refs[6:9]
-    place_ref, table_ref, key_ref, value_ref, query_ref, upstream_ref, semaphores = refs[9:]
+    place_hbm, table_hbm, key_hbm, value_hbm, query_hbm = refs[:5]
+    pair_ref, query_out, trig_ref = refs[5:8]
+    place_ref, table_ref, key_ref, value_ref, query_ref, semaphores = refs[8:]
     slots = key_ref.shape[0]
     copies = [
         pltpu.make_async_copy(source, target, semaphores.at[at])
@@ -61,7 +61,6 @@
                 (key_hbm, key_ref),
                 (value_hbm, value_ref),
                 (query_hbm, query_ref),
-                (upstream_hbm, upstream_ref),
             ]
         )
     ]
@@ -92,13 +91,15 @@
     for number in range(HQ):
         wide = query_ref[:, head(number)].astype(jnp.float32)
         query_out[rows_of(number, slots), :] = turn(wide, cosine, sine).astype(jnp.bfloat16)
-        query_out[rows_of(HQ + number, slots), :] = upstream_ref[:, head(number)]
-
-
-def gate_kernel(weight_hbm, input_hbm, gate_ref, input_ref, weight_ref, semaphores):
+
+
+def gate_kernel(arrived_ref, *refs):
+    weight_hbm, input_hbm, upstream_hbm, gate_ref, input_ref, upstream_ref = refs[:6]
+    weight_ref, semaphores = refs[6:]
     copies = [
         pltpu.make_async_copy(weight_hbm, weight_ref, semaphores.at[0]),
         pltpu.make_async_copy(input_hbm, input_ref, semaphores.at[1]),
+        pltpu.make_async_copy(upstream_hbm, upstream_ref, semaphores.at[2]),
     ]
     for copy in copies:
         copy.start()
@@ -116,22 +117,24 @@
     )
 
 
-def tiles(pair_refs, query_refs, number, slots):
+def tiles(pair_refs, query_refs, upstream_refs, number, slots):
     rows = GROUP * slots
     key_tile = jnp.concatenate([ref[rows_of(number, slots), :] for ref in pair_refs], axis=0)
     value_tile = jnp.concatenate(
         [ref[rows_of(KVH + number, slots), :] for ref in pair_refs], axis=0
     )
     query_tile = jnp.concatenate([ref[rows_of(number, rows), :] for ref in query_refs], axis=0)
+    members = range(number * GROUP, (number + 1) * GROUP)
     upstream_tile = jnp.concatenate(
-        [ref[rows_of(KVH + number, rows), :] for ref in query_refs], axis=0
+        [ref[:, head(at)] for ref in upstream_refs for at in members], axis=0
     )
     return key_tile, value_tile, query_tile, upstream_tile
 
 
 def scores_kernel(slots, *refs):
-    gate_ref, own_ref, other_ref = refs[:3]
-    pair_refs = refs[3:-3]
+    gate_ref = refs[0]
+    query_refs, upstream_refs = refs[1:3], refs[3:5]
+    pair_refs = refs[5:-3]
     grown_out, grad_out, stats_out = refs[-3:]
     rows = GROUP * slots
     keys_total = len(pair_refs) * slots
@@ -146,7 +149,7 @@
     across = (((1,), (1,)), ((), ()))
     for number in range(KVH):
         key_tile, value_tile, query_tile, upstream_tile = tiles(
-            pair_refs, (own_ref, other_ref), number, slots
+            pair_refs, query_refs, upstream_refs, number, slots
         )
         scores = lax.dot_general(
             key_tile, query_tile, across, preferred_element_type=jnp.float32
@@ -200,15 +203,16 @@
 
 
 def terms_kernel(slots, half, *refs):
-    coef_ref, grown_ref, grad_ref, own_ref, other_ref = refs[:5]
-    pair_refs = refs[5 : 5 + half]
-    query_out, query_send, term_own = refs[5 + half : 8 + half]
-    term_refs = refs[8 + half :]
+    coef_ref, grown_ref, grad_ref = refs[:3]
+    query_refs, upstream_refs = refs[3:5], refs[5:7]
+    pair_refs = refs[7 : 7 + half]
+    query_out, query_send, term_own = refs[7 + half : 10 + half]
+    term_refs = refs[10 + half :]
     rows = GROUP * slots
     scale = 1.0 / math.sqrt(HD)
     for number in range(KVH):
         key_tile, _, query_tile, upstream_tile = tiles(
-            pair_refs, (own_ref, other_ref), number, slots
+            pair_refs, query_refs, upstream_refs, number, slots
         )
         gated = grown_ref[number] * coef_ref[number : number + 1, :]
         inner = coef_ref[KVH + number : KVH + number + 1, :]
@@ -312,12 +316,13 @@
         return exchange(array, "ctx", 1, count)
 
     near = pltpu.VMEM
-    fetched = [positions, jnp.asarray(rope_table()), keys[0], values[0], queries[0], out_grad[0]]
+    upstream_other = swap(out_grad[0])
+    fetched = [positions, jnp.asarray(rope_table()), keys[0], values[0], queries[0]]
     pair, query, trig = call(
         prepare_kernel,
         [
             near((2 * KVH * slots, HD), bf16),
-            near((2 * HQ * slots, HD), bf16),
+            near((HQ * slots, HD), bf16),
             near((2 * slots, HD), f32),
         ],
         [],
@@ -328,11 +333,11 @@
     pairs = [pair] + [
         exchange(pair, "ctx", 2 * step, count) for step in range(1, half)
     ]
-    gate, inputs = call(
+    gate, inputs, upstream = call(
         gate_kernel,
-        [near((8, rows), f32), near((slots, width), bf16)],
-        [],
-        [router_weight.reshape(lines, HD), routed_inputs[0]],
+        [near((8, rows), f32), near((slots, width), bf16), near((slots, HQ * HD), bf16)],
+        [upstream_other],
+        [router_weight.reshape(lines, HD), routed_inputs[0], out_grad[0]],
         [near((lines, HD), f32)],
     )
     inputs_other = swap(routed_inputs[0])
@@ -343,7 +348,7 @@
             near((KVH, half * slots, 2 * rows), f32),
             near((4 * KVH, 2 * rows), f32),
         ],
-        [gate, query, query_other, *pairs],
+        [gate, query, query_other, upstream, upstream_other, *pairs],
         cost=SCORES_COST,
     )
     coef, router = call(
@@ -362,7 +367,7 @@
             near((2 * KVH * slots, HD), f32),
         ]
         + [near((2 * KVH * slots, HD), bf16)] * (half - 1),
-        [coef, grown, grad, query, query_other, *pairs],
+        [coef, grown, grad, query, query_other, upstream, upstream_other, *pairs],
         cost=TERMS_COST,
     )
     query_back = swap(query_send)

time: 32.3 us -> 32.3 us (level)
  starting transfers between devices: 18 us -> 21 us
  waiting for transfers between devices: 8.35 us -> 5.46 us
    ppermute x14 -> x15, starting transfers between devices: 18 us -> 21 us  [exchange(): return lax.ppermute(array, axis, [(at, at ^ step) for at in range(size)])]
    ppermute x14 -> x15, waiting for transfers between devices: 8.35 us -> 5.46 us  [exchange(): return lax.ppermute(array, axis, [(at, at ^ step) for at in range(size)])]
  transfers between devices with their start and end apart: 14 -> 15, of which waited for: 7 -> 3; matrix products, arithmetic and copies ran while one was open for 0% -> 0% of each run, Pallas kernels for 9% -> 12%
where the time goes in v7:
time: 32.3 us; the launch traced here: 32 us
  starting transfers between devices  21 us (65%)
  waiting for transfers between devices  5.46 us (17%)
  Pallas kernels  4.87 us (15%)
  between operations  0.71 us (2%)
    ppermute x15, starting transfers between devices, exchange(): return lax.ppermute(array, axis, [(at, at ^ step) for at in range(size)])  21 us
    ppermute x15, waiting for transfers between devices, exchange(): return lax.ppermute(array, axis, [(at, at ^ step) for at in range(size)])  5.46 us
    pallas_call x8, Pallas kernels, call(): pl.pallas_call(kernel, out_shape=outs, in_specs=[local] * len(args) + [di...  4.87 us
  transfers between devices with their start and end apart: 15, of which 3 were waited for; matrix products, arithmetic and copies ran while one was open for 0% of the time, Pallas kernels for 12%

profile of v7, /device:TPU:0, one launch (start us, length us, event | category | flops | bytes accessed | tf_op | source)
XLA Modules:
  0.0 32.0 jit_solution(17040709256973744767)
XLA Ops:
  0.6 3.0 %collective-permute-start = (bf16[32,2048]{1,0:T(8,128)(2,1)}, bf16[32,2048]{1,0:T(8,128)(2,1)S(1)}, u32[]{:S(2)}, u32[]{:S(2)}) collective-permute-start(bf16[32,2048]{1,0:T(8,128)(2,1)} %bitcast.13), channel_id=1, source_target_pairs={{0,1},{1,0},{2,3},{3,2},{4,5},{5,4},{6,7},{7,6},{8,9},{9,8},{10,11... | collective-permute-start | bytes 393224 | tf_op jit(solution)/shard_map/ppermute | solution.py:302
  3.7 1.1 %shard_map.111 = (bf16[256,128]{1,0:T(8,128)(2,1)S(1)}, bf16[512,128]{1,0:T(8,128)(2,1)S(1)}, f32[64,128]{1,0:T(8,128)S(1)}) custom-call(s32[1,32]{1,0:T(1,128)} %refs_0_.1, f32[2,128]{1,0:T(2,128)} %constant.2.clone.refs_1_, bf16[32,512]{1,0:T(8,128)(2,1)} %bitcast.15, bf16[32,512]{1,0:T(8,128)(2,1)} %bitcast.16, bf16[32,2048]{1,0:T(8,128)(2,1)} %bitcast.12), custom_call_target="tpu_custom_call" | custom-call | tf_op jit(solution)/shard_map/pallas_call | solution.py:290
  4.8 0.1 collective-permute-start.1
  4.9 4.1 %collective-permute-start.4 = (bf16[256,128]{1,0:T(8,128)(2,1)S(1)}, bf16[256,128]{1,0:T(8,128)(2,1)S(1)}, u32[]{:S(2)}, u32[]{:S(2)}) collective-permute-start(bf16[256,128]{1,0:T(8,128)(2,1)S(1)} %get-tuple-element.35.refs_5_.refs_7_), channel_id=1, source_target_pairs={{0,6},{1,7},{2,4},{3,5},{4,2},{5,3},{6,0},{7,1},{8,14},{9,15},{10,... | collective-permute-start | bytes 196616 | tf_op jit(solution)/shard_map/ppermute | solution.py:302
  9.0 0.0 collective-permute-start.3
  9.0 0.6 %collective-permute-start.2 = (bf16[256,128]{1,0:T(8,128)(2,1)S(1)}, bf16[256,128]{1,0:T(8,128)(2,1)S(1)}, u32[]{:S(2)}, u32[]{:S(2)}) collective-permute-start(bf16[256,128]{1,0:T(8,128)(2,1)S(1)} %get-tuple-element.35.refs_5_.refs_7_), channel_id=1, source_target_pairs={{0,2},{1,3},{2,0},{3,1},{4,6},{5,7},{6,4},{7,5},{8,10},{9,11},{10,... | collective-permute-start | bytes 196616 | tf_op jit(solution)/shard_map/ppermute | solution.py:302
  9.6 0.0 collective-permute-done.arrived_ref.refs_4_.refs_6_
  9.6 1.7 %collective-permute-start.6 = (bf16[32,4096]{1,0:T(8,128)(2,1)}, bf16[32,4096]{1,0:T(8,128)(2,1)S(1)}, u32[]{:S(2)}, u32[]{:S(2)}) collective-permute-start(bf16[32,4096]{1,0:T(8,128)(2,1)} %bitcast.10), channel_id=1, source_target_pairs={{0,1},{1,0},{2,3},{3,2},{4,5},{5,4},{6,7},{7,6},{8,9},{9,8},{10,11... | collective-permute-start | bytes 786440 | tf_op jit(solution)/shard_map/ppermute | solution.py:302
  11.3 1.2 %shard_map.112 = (f32[8,128]{1,0:T(8,128)S(1)}, bf16[32,4096]{1,0:T(8,128)(2,1)S(1)}, bf16[32,2048]{1,0:T(8,128)(2,1)S(1)}) custom-call(bf16[32,2048]{1,0:T(8,128)(2,1)S(1)} %collective-permute-done.arrived_ref.refs_4_.refs_6_, f32[32,128]{1,0:T(8,128)} %bitcast.17, bf16[32,4096]{1,0:T(8,128)(2,1)} %bitcast.11, bf16[32,2048]{1,0:T(8,128)(2,1)} %bitcast.14), custom_call_target="tpu_custom_call" | custom-call | tf_op jit(solution)/shard_map/pallas_call | solution.py:290
  12.5 0.0 collective-permute-done.4.refs_8_.refs_10_
  12.5 1.7 %collective-permute-done.3.refs_7_.refs_9_ = bf16[256,128]{1,0:T(8,128)(2,1)S(1)} collective-permute-done((bf16[256,128]{1,0:T(8,128)(2,1)S(1)}, bf16[256,128]{1,0:T(8,128)(2,1)S(1)}, u32[]{:S(2)}, u32[]{:S(2)}) %collective-permute-start.3) | collective-permute-done | bytes 65568 | tf_op jit(solution)/shard_map/ppermute | solution.py:302
  14.2 0.0 collective-permute-done.2.refs_6_.refs_8_
  14.2 0.0 collective-permute-done.1.refs_2_.refs_4_
  14.2 0.4 %shard_map.113 = (f32[4,128,256]{2,1,0:T(8,128)S(1)}, f32[4,128,256]{2,1,0:T(8,128)S(1)}, f32[16,256]{1,0:T(8,128)S(1)}) custom-call(f32[8,128]{1,0:T(8,128)S(1)} %get-tuple-element.32.refs_0_, bf16[512,128]{1,0:T(8,128)(2,1)S(1)} %get-tuple-element.33.refs_1_.refs_3_, bf16[512,128]{1,0:T(8,128)(2,1)S(1)} %collective-permute-done.1.refs_2_.refs_4_, ...), custom_call_target="tpu_custom_call" | custom-call | flops 20000000000 | tf_op jit(solution)/shard_map/pallas_call | solution.py:290
  14.6 1.6 %collective-permute-start.5 = (f32[16,256]{1,0:T(8,128)S(1)}, f32[16,256]{1,0:T(8,128)S(1)}, u32[]{:S(2)}, u32[]{:S(2)}) collective-permute-start(f32[16,256]{1,0:T(8,128)S(1)} %get-tuple-element.36.own_ref), channel_id=1, source_target_pairs={{0,1},{1,0},{2,3},{3,2},{4,5},{5,4},{6,7},{7,6},{8,9},{9,8},{10,11... | collective-permute-start | bytes 49160 | tf_op jit(solution)/shard_map/ppermute | solution.py:302
  16.2 2.2 %collective-permute-done.5.other_ref = f32[16,256]{1,0:T(8,128)S(1)} collective-permute-done((f32[16,256]{1,0:T(8,128)S(1)}, f32[16,256]{1,0:T(8,128)S(1)}, u32[]{:S(2)}, u32[]{:S(2)}) %collective-permute-start.5) | collective-permute-done | bytes 16416 | tf_op jit(solution)/shard_map/ppermute | solution.py:302
  18.4 0.0 collective-permute-done.6.input_other_ref
  18.4 0.2 shard_map.114
  18.7 0.1 collective-permute-start.11
  18.8 1.6 %collective-permute-start.10 = (f32[32,128]{1,0:T(8,128)S(1)}, f32[32,128]{1,0:T(8,128)S(1)}, u32[]{:S(2)}, u32[]{:S(2)}) collective-permute-start(f32[32,128]{1,0:T(8,128)S(1)} %get-tuple-element.48.refs_0_), channel_id=1, source_target_pairs={{0,16},{8,24},{16,0},{24,8},{1,17},{9,25},{17,1},{25,9},{2,18},{10... | collective-permute-start | bytes 49160 | tf_op jit(solution)/shard_map/ppermute | solution.py:302
  20.3 0.3 collective-permute-start.9
  20.6 0.4 %shard_map.115 = (f32[512,128]{1,0:T(8,128)S(1)}, bf16[512,128]{1,0:T(8,128)(2,1)S(1)}, f32[256,128]{1,0:T(8,128)S(1)}, bf16[256,128]{1,0:T(8,128)(2,1)S(1)}, bf...) custom-call(f32[8,256]{1,0:T(8,128)S(1)} %get-tuple-element.38.refs_0_, ...), custom_call_target="tpu_custom_call" | custom-call | flops 20000000000 | tf_op jit(solution)/shard_map/pallas_call | solution.py:290
  21.0 2.0 %collective-permute-start.8 = (bf16[256,128]{1,0:T(8,128)(2,1)S(1)}, bf16[256,128]{1,0:T(8,128)(2,1)S(1)}, u32[]{:S(2)}, u32[]{:S(2)}) collective-permute-start(bf16[256,128]{1,0:T(8,128)(2,1)S(1)} %get-tuple-element.43), channel_id=1, source_target_pairs={{0,4},{1,5},{2,6},{3,7},{4,0},{5,1},{6,2},{7,3},{8,12},{9,13},{10,... | collective-permute-start | bytes 196616 | tf_op jit(solution)/shard_map/ppermute | solution.py:302
  23.0 1.5 %collective-permute-start.7 = (bf16[512,128]{1,0:T(8,128)(2,1)S(1)}, bf16[512,128]{1,0:T(8,128)(2,1)S(1)}, u32[]{:S(2)}, u32[]{:S(2)}) collective-permute-start(bf16[512,128]{1,0:T(8,128)(2,1)S(1)} %get-tuple-element.42), channel_id=1, source_target_pairs={{0,1},{1,0},{2,3},{3,2},{4,5},{5,4},{6,7},{7,6},{8,9},{9,8},{10,11... | collective-permute-start | bytes 393224 | tf_op jit(solution)/shard_map/ppermute | solution.py:302
  24.5 0.0 collective-permute-done.11.refs_3_
  24.5 0.0 collective-permute-done.10.refs_2_
  24.5 0.0 collective-permute-done.9.refs_1_
  24.6 1.4 %collective-permute-start.13 = (bf16[288,128]{1,0:T(8,128)(2,1)S(1)}, bf16[288,128]{1,0:T(8,128)(2,1)S(1)}, u32[]{:S(2)}, u32[]{:S(2)}) collective-permute-start(bf16[288,128]{1,0:T(8,128)(2,1)S(1)} %get-tuple-element.53), channel_id=1, source_target_pairs={{0,6},{1,7},{2,4},{3,5},{4,2},{5,3},{6,0},{7,1},{8,14},{9,15},{10,... | collective-permute-start | bytes 221192 | tf_op jit(solution)/shard_map/ppermute | solution.py:302
  25.9 0.3 collective-permute-start.14
  26.2 2.8 %collective-permute-start.12 = (bf16[32,128]{1,0:T(8,128)(2,1)S(1)}, bf16[32,128]{1,0:T(8,128)(2,1)S(1)}, u32[]{:S(2)}, u32[]{:S(2)}) collective-permute-start(bf16[32,128]{1,0:T(8,128)(2,1)S(1)} %get-tuple-element.52), channel_id=1, source_target_pairs={{0,4},{1,5},{2,6},{3,7},{4,0},{5,1},{6,2},{7,3},{8,12},{9,13},{10,... | collective-permute-start | bytes 24584 | tf_op jit(solution)/shard_map/ppermute | solution.py:302
  29.0 0.0 collective-permute-done.8.far_ref
  29.0 0.0 collective-permute-done.7.other_ref
  29.0 0.8 %shard_map.116 = (bf16[32,2048]{1,0:T(8,128)(2,1)}, f32[64,128]{1,0:T(8,128)S(1)}, f32[256,128]{1,0:T(8,128)S(1)}) custom-call(f32[64,128]{1,0:T(8,128)S(1)} %get-tuple-element.31.trig_ref, f32[512,128]{1,0:T(8,128)S(1)} %get-tuple-element.41.own_ref, bf16[512,128]{1,0:T(8,128)(2,1)S(1)} %collective-permute-done.7.other_ref, ...), custom_call_target="tpu_custom_call" | custom-call | flops 500000000 | tf_op jit(solution)/shard_map/pallas_call | solution.py:290
  29.8 1.5 %collective-permute-done.12.refs_3_ = bf16[32,128]{1,0:T(8,128)(2,1)S(1)} collective-permute-done((bf16[32,128]{1,0:T(8,128)(2,1)S(1)}, bf16[32,128]{1,0:T(8,128)(2,1)S(1)}, u32[]{:S(2)}, u32[]{:S(2)}) %collective-permute-start.12) | collective-permute-done | bytes 8224 | tf_op jit(solution)/shard_map/ppermute | solution.py:302
  31.3 0.0 collective-permute-done.13.refs_4_
  31.3 0.0 collective-permute-done.14.refs_5_
  31.3 0.7 %shard_map.118 = (bf16[32,512]{1,0:T(8,128)(2,1)}, bf16[32,512]{1,0:T(8,128)(2,1)}, f32[32,128]{1,0:T(8,128)}) custom-call(f32[64,128]{1,0:T(8,128)S(1)} %get-tuple-element.46.refs_0_, f32[256,128]{1,0:T(8,128)S(1)} %get-tuple-element.47.refs_1_, f32[32,128]{1,0:T(8,128)S(1)} %get-tuple-element.51.refs_2_, ...), custom_call_target="tpu_custom_call" | custom-call | tf_op jit(solution)/shard_map/pallas_call | solution.py:290
  (1 shorter events, 0.0 us)
Async XLA Ops:
  0.6 8.9 %collective-permute-start = (bf16[32,2048]{1,0:T(8,128)(2,1)}, bf16[32,2048]{1,0:T(8,128)(2,1)S(1)}, u32[]{:S(2)}, u32[]{:S(2)}) collective-permute-start(bf16[32,2048]{1,0:T(8,128)(2,1)} %bitcast.13), channel_id=1, source_target_pairs={{0,1},{1,0},{2,3},{3,2},{4,5},{5,4},{6,7},{7,6},{8,9},{9,8},{10,11... | collective-permute-start | bytes 393224 | tf_op jit(solution)/shard_map/ppermute | solution.py:302
  4.8 9.4 %collective-permute-start.1 = (bf16[512,128]{1,0:T(8,128)(2,1)S(1)}, bf16[512,128]{1,0:T(8,128)(2,1)S(1)}, u32[]{:S(2)}, u32[]{:S(2)}) collective-permute-start(bf16[512,128]{1,0:T(8,128)(2,1)S(1)} %get-tuple-element.33.refs_1_.refs_3_), channel_id=1, source_target_pairs={{0,1},{1,0},{2,3},{3,2},{4,5},{5,4},{6,7},{7,6},{8,9},{9,8},{10,11... | collective-permute-start | bytes 393224 | tf_op jit(solution)/shard_map/ppermute | solution.py:302
  4.9 7.6 %collective-permute-start.4 = (bf16[256,128]{1,0:T(8,128)(2,1)S(1)}, bf16[256,128]{1,0:T(8,128)(2,1)S(1)}, u32[]{:S(2)}, u32[]{:S(2)}) collective-permute-start(bf16[256,128]{1,0:T(8,128)(2,1)S(1)} %get-tuple-element.35.refs_5_.refs_7_), channel_id=1, source_target_pairs={{0,6},{1,7},{2,4},{3,5},{4,2},{5,3},{6,0},{7,1},{8,14},{9,15},{10,... | collective-permute-start | bytes 196616 | tf_op jit(solution)/shard_map/ppermute | solution.py:302
  9.0 5.2 %collective-permute-start.3 = (bf16[256,128]{1,0:T(8,128)(2,1)S(1)}, bf16[256,128]{1,0:T(8,128)(2,1)S(1)}, u32[]{:S(2)}, u32[]{:S(2)}) collective-permute-start(bf16[256,128]{1,0:T(8,128)(2,1)S(1)} %get-tuple-element.35.refs_5_.refs_7_), channel_id=1, source_target_pairs={{0,4},{1,5},{2,6},{3,7},{4,0},{5,1},{6,2},{7,3},{8,12},{9,13},{10,... | collective-permute-start | bytes 196616 | tf_op jit(solution)/shard_map/ppermute | solution.py:302
  9.0 5.2 %collective-permute-start.2 = (bf16[256,128]{1,0:T(8,128)(2,1)S(1)}, bf16[256,128]{1,0:T(8,128)(2,1)S(1)}, u32[]{:S(2)}, u32[]{:S(2)}) collective-permute-start(bf16[256,128]{1,0:T(8,128)(2,1)S(1)} %get-tuple-element.35.refs_5_.refs_7_), channel_id=1, source_target_pairs={{0,2},{1,3},{2,0},{3,1},{4,6},{5,7},{6,4},{7,5},{8,10},{9,11},{10,... | collective-permute-start | bytes 196616 | tf_op jit(solution)/shard_map/ppermute | solution.py:302
  9.6 8.9 %collective-permute-start.6 = (bf16[32,4096]{1,0:T(8,128)(2,1)}, bf16[32,4096]{1,0:T(8,128)(2,1)S(1)}, u32[]{:S(2)}, u32[]{:S(2)}) collective-permute-start(bf16[32,4096]{1,0:T(8,128)(2,1)} %bitcast.10), channel_id=1, source_target_pairs={{0,1},{1,0},{2,3},{3,2},{4,5},{5,4},{6,7},{7,6},{8,9},{9,8},{10,11... | collective-permute-start | bytes 786440 | tf_op jit(solution)/shard_map/ppermute | solution.py:302
  14.6 3.8 %collective-permute-start.5 = (f32[16,256]{1,0:T(8,128)S(1)}, f32[16,256]{1,0:T(8,128)S(1)}, u32[]{:S(2)}, u32[]{:S(2)}) collective-permute-start(f32[16,256]{1,0:T(8,128)S(1)} %get-tuple-element.36.own_ref), channel_id=1, source_target_pairs={{0,1},{1,0},{2,3},{3,2},{4,5},{5,4},{6,7},{7,6},{8,9},{9,8},{10,11... | collective-permute-start | bytes 49160 | tf_op jit(solution)/shard_map/ppermute | solution.py:302
  18.7 5.8 %collective-permute-start.11 = (f32[32,128]{1,0:T(8,128)S(1)}, f32[32,128]{1,0:T(8,128)S(1)}, u32[]{:S(2)}, u32[]{:S(2)}) collective-permute-start(f32[32,128]{1,0:T(8,128)S(1)} %get-tuple-element.48.refs_0_), channel_id=1, source_target_pairs={{0,24},{8,16},{16,8},{24,0},{1,25},{9,17},{17,9},{25,1},{2,26},{10... | collective-permute-start | bytes 49160 | tf_op jit(solution)/shard_map/ppermute | solution.py:302
  18.8 5.8 %collective-permute-start.10 = (f32[32,128]{1,0:T(8,128)S(1)}, f32[32,128]{1,0:T(8,128)S(1)}, u32[]{:S(2)}, u32[]{:S(2)}) collective-permute-start(f32[32,128]{1,0:T(8,128)S(1)} %get-tuple-element.48.refs_0_), channel_id=1, source_target_pairs={{0,16},{8,24},{16,0},{24,8},{1,17},{9,25},{17,1},{25,9},{2,18},{10... | collective-permute-start | bytes 49160 | tf_op jit(solution)/shard_map/ppermute | solution.py:302
  20.3 4.2 %collective-permute-start.9 = (f32[32,128]{1,0:T(8,128)S(1)}, f32[32,128]{1,0:T(8,128)S(1)}, u32[]{:S(2)}, u32[]{:S(2)}) collective-permute-start(f32[32,128]{1,0:T(8,128)S(1)} %get-tuple-element.48.refs_0_), channel_id=1, source_target_pairs={{0,8},{8,0},{16,24},{24,16},{1,9},{9,1},{17,25},{25,17},{2,10},{10... | collective-permute-start | bytes 49160 | tf_op jit(solution)/shard_map/ppermute | solution.py:302
  21.0 8.0 %collective-permute-start.8 = (bf16[256,128]{1,0:T(8,128)(2,1)S(1)}, bf16[256,128]{1,0:T(8,128)(2,1)S(1)}, u32[]{:S(2)}, u32[]{:S(2)}) collective-permute-start(bf16[256,128]{1,0:T(8,128)(2,1)S(1)} %get-tuple-element.43), channel_id=1, source_target_pairs={{0,4},{1,5},{2,6},{3,7},{4,0},{5,1},{6,2},{7,3},{8,12},{9,13},{10,... | collective-permute-start | bytes 196616 | tf_op jit(solution)/shard_map/ppermute | solution.py:302
  23.0 6.0 %collective-permute-start.7 = (bf16[512,128]{1,0:T(8,128)(2,1)S(1)}, bf16[512,128]{1,0:T(8,128)(2,1)S(1)}, u32[]{:S(2)}, u32[]{:S(2)}) collective-permute-start(bf16[512,128]{1,0:T(8,128)(2,1)S(1)} %get-tuple-element.42), channel_id=1, source_target_pairs={{0,1},{1,0},{2,3},{3,2},{4,5},{5,4},{6,7},{7,6},{8,9},{9,8},{10,11... | collective-permute-start | bytes 393224 | tf_op jit(solution)/shard_map/ppermute | solution.py:302
  24.6 6.7 %collective-permute-start.13 = (bf16[288,128]{1,0:T(8,128)(2,1)S(1)}, bf16[288,128]{1,0:T(8,128)(2,1)S(1)}, u32[]{:S(2)}, u32[]{:S(2)}) collective-permute-start(bf16[288,128]{1,0:T(8,128)(2,1)S(1)} %get-tuple-element.53), channel_id=1, source_target_pairs={{0,6},{1,7},{2,4},{3,5},{4,2},{5,3},{6,0},{7,1},{8,14},{9,15},{10,... | collective-permute-start | bytes 221192 | tf_op jit(solution)/shard_map/ppermute | solution.py:302
  25.9 5.4 %collective-permute-start.14 = (bf16[288,128]{1,0:T(8,128)(2,1)S(1)}, bf16[288,128]{1,0:T(8,128)(2,1)S(1)}, u32[]{:S(2)}, u32[]{:S(2)}) collective-permute-start(bf16[288,128]{1,0:T(8,128)(2,1)S(1)} %get-tuple-element.54), channel_id=1, source_target_pairs={{0,2},{1,3},{2,0},{3,1},{4,6},{5,7},{6,4},{7,5},{8,10},{9,11},{10,... | collective-permute-start | bytes 221192 | tf_op jit(solution)/shard_map/ppermute | solution.py:302
  26.2 5.1 %collective-permute-start.12 = (bf16[32,128]{1,0:T(8,128)(2,1)S(1)}, bf16[32,128]{1,0:T(8,128)(2,1)S(1)}, u32[]{:S(2)}, u32[]{:S(2)}) collective-permute-start(bf16[32,128]{1,0:T(8,128)(2,1)S(1)} %get-tuple-element.52), channel_id=1, source_target_pairs={{0,4},{1,5},{2,6},{3,7},{4,0},{5,1},{6,2},{7,3},{8,12},{9,13},{10,... | collective-permute-start | bytes 24584 | tf_op jit(solution)/shard_map/ppermute | solution.py:302

commit v8 on v6

--- a/solution.py
+++ b/solution.py
@@ -368,7 +368,7 @@
     query_back = swap(query_send)
     early = half // 2
     far = exchange(terms[early - 1], "ctx", 2 * early, count)
-    others = [step for step in reversed(range(1, half)) if step != early]
+    others = [step for step in range(1, half) if step != early]
     router, router_send, *terms = call(
         functools.partial(ride_kernel, groups),
         [near((lines, HD), f32), near((lines, HD), bf16)]

time: 32.3 us -> 33 us (1.022)
  waiting for transfers between devices: 8.35 us -> 9.97 us
  starting transfers between devices: 18 us -> 17.1 us
    ppermute x14, waiting for transfers between devices: 8.35 us -> 9.97 us  [exchange(): return lax.ppermute(array, axis, [(at, at ^ step) for at in range(size)])]
    ppermute x14, starting transfers between devices: 18 us -> 17.1 us  [exchange(): return lax.ppermute(array, axis, [(at, at ^ step) for at in range(size)])]
  transfers between devices with their start and end apart: 14 -> 14, of which waited for: 7 -> 8; matrix products, arithmetic and copies ran while one was open for 0% -> 0% of each run, Pallas kernels for 9% -> 8%
where the time goes in v8:
time: 33 us; the launch traced here: 32.7 us
  starting transfers between devices  17.1 us (52%)
  waiting for transfers between devices  9.97 us (30%)
  Pallas kernels  4.96 us (15%)
  between operations  0.71 us (2%)
    ppermute x14, starting transfers between devices, exchange(): return lax.ppermute(array, axis, [(at, at ^ step) for at in range(size)])  17.1 us
    ppermute x14, waiting for transfers between devices, exchange(): return lax.ppermute(array, axis, [(at, at ^ step) for at in range(size)])  9.97 us
    pallas_call x8, Pallas kernels, call(): pl.pallas_call(kernel, out_shape=outs, in_specs=[local] * len(args) + [di...  4.96 us
  transfers between devices with their start and end apart: 14, of which 8 were waited for; matrix products, arithmetic and copies ran while one was open for 0% of the time, Pallas kernels for 8%

profile of v8, /device:TPU:0, one launch (start us, length us, event | category | flops | bytes accessed | tf_op | source)
XLA Modules:
  0.0 32.7 jit_solution(6017330407787036123)
XLA Ops:
  0.6 0.0 copy-start
  0.6 1.3 %shard_map.111 = (bf16[256,128]{1,0:T(8,128)(2,1)S(1)}, bf16[1024,128]{1,0:T(8,128)(2,1)S(1)}, f32[64,128]{1,0:T(8,128)S(1)}) custom-call(s32[1,32]{1,0:T(1,128)} %refs_0_.1, f32[2,128]{1,0:T(2,128)} %constant.2.clone.refs_1_, bf16[32,512]{1,0:T(8,128)(2,1)} %bitcast.14, bf16[32,512]{1,0:T(8,128)(2,1)} %bitcast.15, bf16[32,2048]{1,0:T(8,128)(2,1)} %bitcast.12, ...), custom_call_target="tpu_custom_call" | custom-call | tf_op jit(solution)/shard_map/pallas_call | solution.py:286
  1.9 3.0 %collective-permute-start = (bf16[1024,128]{1,0:T(8,128)(2,1)S(1)}, bf16[1024,128]{1,0:T(8,128)(2,1)S(1)}, u32[]{:S(2)}, u32[]{:S(2)}) collective-permute-start(bf16[1024,128]{1,0:T(8,128)(2,1)S(1)} %get-tuple-element.32.refs_1_.refs_3_), channel_id=1, source_target_pairs={{0,1},{1,0},{2,3},{3,2},{4,5},{5,4},{6,7},{7,6},{8,9},{9,8},{10,11... | collective-permute-start | bytes 786440 | tf_op jit(solution)/shard_map/ppermute | solution.py:298
  5.0 3.6 %collective-permute-start.3 = (bf16[256,128]{1,0:T(8,128)(2,1)S(1)}, bf16[256,128]{1,0:T(8,128)(2,1)S(1)}, u32[]{:S(2)}, u32[]{:S(2)}) collective-permute-start(bf16[256,128]{1,0:T(8,128)(2,1)S(1)} %get-tuple-element.33.refs_3_.refs_5_), channel_id=1, source_target_pairs={{0,6},{1,7},{2,4},{3,5},{4,2},{5,3},{6,0},{7,1},{8,14},{9,15},{10,... | collective-permute-start | bytes 196616 | tf_op jit(solution)/shard_map/ppermute | solution.py:298
  8.6 0.0 collective-permute-start.2
  8.6 0.8 %collective-permute-start.1 = (bf16[256,128]{1,0:T(8,128)(2,1)S(1)}, bf16[256,128]{1,0:T(8,128)(2,1)S(1)}, u32[]{:S(2)}, u32[]{:S(2)}) collective-permute-start(bf16[256,128]{1,0:T(8,128)(2,1)S(1)} %get-tuple-element.33.refs_3_.refs_5_), channel_id=1, source_target_pairs={{0,2},{1,3},{2,0},{3,1},{4,6},{5,7},{6,4},{7,5},{8,10},{9,11},{10,... | collective-permute-start | bytes 196616 | tf_op jit(solution)/shard_map/ppermute | solution.py:298
  9.4 0.0 copy-done
  9.4 0.3 collective-permute-start.5
  9.6 1.1 %shard_map.112 = (f32[8,128]{1,0:T(8,128)S(1)}, bf16[32,4096]{1,0:T(8,128)(2,1)S(1)}) custom-call(f32[32,128]{1,0:T(8,128)} %bitcast.16, bf16[32,4096]{1,0:T(8,128)(2,1)} %bitcast.10), custom_call_target="tpu_custom_call" | custom-call | tf_op jit(solution)/shard_map/pallas_call | solution.py:286
  10.8 1.0 %collective-permute-done.3.refs_6_.refs_8_ = bf16[256,128]{1,0:T(8,128)(2,1)S(1)} collective-permute-done((bf16[256,128]{1,0:T(8,128)(2,1)S(1)}, bf16[256,128]{1,0:T(8,128)(2,1)S(1)}, u32[]{:S(2)}, u32[]{:S(2)}) %collective-permute-start.3) | collective-permute-done | bytes 65568 | tf_op jit(solution)/shard_map/ppermute | solution.py:298
  11.8 2.1 %collective-permute-done.2.refs_5_.refs_7_ = bf16[256,128]{1,0:T(8,128)(2,1)S(1)} collective-permute-done((bf16[256,128]{1,0:T(8,128)(2,1)S(1)}, bf16[256,128]{1,0:T(8,128)(2,1)S(1)}, u32[]{:S(2)}, u32[]{:S(2)}) %collective-permute-start.2) | collective-permute-done | bytes 65568 | tf_op jit(solution)/shard_map/ppermute | solution.py:298
  13.9 0.1 collective-permute-done.1.refs_4_.refs_6_
  14.0 0.0 collective-permute-done.refs_2_.refs_4_
  14.0 0.4 %shard_map.113 = (f32[4,128,256]{2,1,0:T(8,128)S(1)}, f32[4,128,256]{2,1,0:T(8,128)S(1)}, f32[16,256]{1,0:T(8,128)S(1)}) custom-call(f32[8,128]{1,0:T(8,128)S(1)} %get-tuple-element.31.refs_0_, bf16[1024,128]{1,0:T(8,128)(2,1)S(1)} %get-tuple-element.32.refs_1_.refs_3_, bf16[1024,128]{1,0:T(8,128)(2,1)S(1)} %collective-permute-done.refs_2_.refs_4_, ...), custom_call_target="tpu_custom_call" | custom-call | flops 20000000000 | tf_op jit(solution)/shard_map/pallas_call | solution.py:286
  14.4 0.5 %collective-permute-start.4 = (f32[16,256]{1,0:T(8,128)S(1)}, f32[16,256]{1,0:T(8,128)S(1)}, u32[]{:S(2)}, u32[]{:S(2)}) collective-permute-start(f32[16,256]{1,0:T(8,128)S(1)} %get-tuple-element.34.own_ref), channel_id=1, source_target_pairs={{0,1},{1,0},{2,3},{3,2},{4,5},{5,4},{6,7},{7,6},{8,9},{9,8},{10,11... | collective-permute-start | bytes 49160 | tf_op jit(solution)/shard_map/ppermute | solution.py:298
  14.9 2.2 %collective-permute-done.5.input_other_ref = bf16[32,4096]{1,0:T(8,128)(2,1)S(1)} collective-permute-done((bf16[32,4096]{1,0:T(8,128)(2,1)S(1)}, bf16[32,4096]{1,0:T(8,128)(2,1)S(1)}, u32[]{:S(2)}, u32[]{:S(2)}) %collective-permute-start.5) | collective-permute-done | bytes 262176 | tf_op jit(solution)/shard_map/ppermute | solution.py:298
  17.1 1.1 %collective-permute-done.4.other_ref = f32[16,256]{1,0:T(8,128)S(1)} collective-permute-done((f32[16,256]{1,0:T(8,128)S(1)}, f32[16,256]{1,0:T(8,128)S(1)}, u32[]{:S(2)}, u32[]{:S(2)}) %collective-permute-start.4) | collective-permute-done | bytes 16416 | tf_op jit(solution)/shard_map/ppermute | solution.py:298
  18.2 0.2 shard_map.114
  18.4 0.1 collective-permute-start.10
  18.5 1.6 %collective-permute-start.9 = (f32[32,128]{1,0:T(8,128)S(1)}, f32[32,128]{1,0:T(8,128)S(1)}, u32[]{:S(2)}, u32[]{:S(2)}) collective-permute-start(f32[32,128]{1,0:T(8,128)S(1)} %get-tuple-element.46.refs_0_), channel_id=1, source_target_pairs={{0,16},{8,24},{16,0},{24,8},{1,17},{9,25},{17,1},{25,9},{2,18},{10... | collective-permute-start | bytes 49160 | tf_op jit(solution)/shard_map/ppermute | solution.py:298
  20.1 0.3 collective-permute-start.8
  20.4 0.4 %shard_map.115 = (f32[512,128]{1,0:T(8,128)S(1)}, bf16[512,128]{1,0:T(8,128)(2,1)S(1)}, f32[256,128]{1,0:T(8,128)S(1)}, bf16[256,128]{1,0:T(8,128)(2,1)S(1)}, bf...) custom-call(f32[8,256]{1,0:T(8,128)S(1)} %get-tuple-element.36.refs_0_, ...), custom_call_target="tpu_custom_call" | custom-call | flops 20000000000 | tf_op jit(solution)/shard_map/pallas_call | solution.py:286
  20.8 1.9 %collective-permute-start.7 = (bf16[256,128]{1,0:T(8,128)(2,1)S(1)}, bf16[256,128]{1,0:T(8,128)(2,1)S(1)}, u32[]{:S(2)}, u32[]{:S(2)}) collective-permute-start(bf16[256,128]{1,0:T(8,128)(2,1)S(1)} %get-tuple-element.41), channel_id=1, source_target_pairs={{0,4},{1,5},{2,6},{3,7},{4,0},{5,1},{6,2},{7,3},{8,12},{9,13},{10,... | collective-permute-start | bytes 196616 | tf_op jit(solution)/shard_map/ppermute | solution.py:298
  22.7 1.5 %collective-permute-start.6 = (bf16[512,128]{1,0:T(8,128)(2,1)S(1)}, bf16[512,128]{1,0:T(8,128)(2,1)S(1)}, u32[]{:S(2)}, u32[]{:S(2)}) collective-permute-start(bf16[512,128]{1,0:T(8,128)(2,1)S(1)} %get-tuple-element.40), channel_id=1, source_target_pairs={{0,1},{1,0},{2,3},{3,2},{4,5},{5,4},{6,7},{7,6},{8,9},{9,8},{10,11... | collective-permute-start | bytes 393224 | tf_op jit(solution)/shard_map/ppermute | solution.py:298
  24.2 0.0 collective-permute-done.10.refs_3_
  24.2 0.0 collective-permute-done.9.refs_2_
  24.2 0.0 collective-permute-done.8.refs_1_
  24.2 1.6 %collective-permute-start.12 = (bf16[288,128]{1,0:T(8,128)(2,1)S(1)}, bf16[288,128]{1,0:T(8,128)(2,1)S(1)}, u32[]{:S(2)}, u32[]{:S(2)}) collective-permute-start(bf16[288,128]{1,0:T(8,128)(2,1)S(1)} %get-tuple-element.51), channel_id=1, source_target_pairs={{0,2},{1,3},{2,0},{3,1},{4,6},{5,7},{6,4},{7,5},{8,10},{9,11},{10,... | collective-permute-start | bytes 221192 | tf_op jit(solution)/shard_map/ppermute | solution.py:298
  25.9 0.2 collective-permute-start.13
  26.1 1.7 %collective-permute-start.11 = (bf16[32,128]{1,0:T(8,128)(2,1)S(1)}, bf16[32,128]{1,0:T(8,128)(2,1)S(1)}, u32[]{:S(2)}, u32[]{:S(2)}) collective-permute-start(bf16[32,128]{1,0:T(8,128)(2,1)S(1)} %get-tuple-element.50), channel_id=1, source_target_pairs={{0,4},{1,5},{2,6},{3,7},{4,0},{5,1},{6,2},{7,3},{8,12},{9,13},{10,... | collective-permute-start | bytes 24584 | tf_op jit(solution)/shard_map/ppermute | solution.py:298
  27.8 0.0 collective-permute-done.7.far_ref
  27.8 0.2 collective-permute-done.6.other_ref
  28.0 0.8 %shard_map.116 = (bf16[32,2048]{1,0:T(8,128)(2,1)}, f32[64,128]{1,0:T(8,128)S(1)}, f32[256,128]{1,0:T(8,128)S(1)}) custom-call(f32[64,128]{1,0:T(8,128)S(1)} %get-tuple-element.30.trig_ref, f32[512,128]{1,0:T(8,128)S(1)} %get-tuple-element.39.own_ref, bf16[512,128]{1,0:T(8,128)(2,1)S(1)} %collective-permute-done.6.other_ref, ...), custom_call_target="tpu_custom_call" | custom-call | flops 500000000 | tf_op jit(solution)/shard_map/pallas_call | solution.py:286
  28.8 2.3 %collective-permute-done.11.refs_3_ = bf16[32,128]{1,0:T(8,128)(2,1)S(1)} collective-permute-done((bf16[32,128]{1,0:T(8,128)(2,1)S(1)}, bf16[32,128]{1,0:T(8,128)(2,1)S(1)}, u32[]{:S(2)}, u32[]{:S(2)}) %collective-permute-start.11) | collective-permute-done | bytes 8224 | tf_op jit(solution)/shard_map/ppermute | solution.py:298
  31.1 0.0 collective-permute-done.12.refs_4_
  31.1 0.9 %collective-permute-done.13.refs_5_ = bf16[288,128]{1,0:T(8,128)(2,1)S(1)} collective-permute-done((bf16[288,128]{1,0:T(8,128)(2,1)S(1)}, bf16[288,128]{1,0:T(8,128)(2,1)S(1)}, u32[]{:S(2)}, u32[]{:S(2)}) %collective-permute-start.13) | collective-permute-done | bytes 73760 | tf_op jit(solution)/shard_map/ppermute | solution.py:298
  32.0 0.7 %shard_map.118 = (bf16[32,512]{1,0:T(8,128)(2,1)}, bf16[32,512]{1,0:T(8,128)(2,1)}, f32[32,128]{1,0:T(8,128)}) custom-call(f32[64,128]{1,0:T(8,128)S(1)} %get-tuple-element.44.refs_0_, f32[256,128]{1,0:T(8,128)S(1)} %get-tuple-element.45.refs_1_, f32[32,128]{1,0:T(8,128)S(1)} %get-tuple-element.49.refs_2_, ...), custom_call_target="tpu_custom_call" | custom-call | tf_op jit(solution)/shard_map/pallas_call | solution.py:286
  (1 shorter events, 0.0 us)
Async XLA Ops:
  0.6 8.7 %copy-start = (bf16[1,32,4096]{2,1,0:T(8,128)(2,1)S(1)}, bf16[1,32,4096]{2,1,0:T(8,128)(2,1)}, u32[]{:S(2)}) copy-start(bf16[1,32,4096]{2,1,0:T(8,128)(2,1)} %param.12) | copy-start | bytes 786436
  1.9 12.1 %collective-permute-start = (bf16[1024,128]{1,0:T(8,128)(2,1)S(1)}, bf16[1024,128]{1,0:T(8,128)(2,1)S(1)}, u32[]{:S(2)}, u32[]{:S(2)}) collective-permute-start(bf16[1024,128]{1,0:T(8,128)(2,1)S(1)} %get-tuple-element.32.refs_1_.refs_3_), channel_id=1, source_target_pairs={{0,1},{1,0},{2,3},{3,2},{4,5},{5,4},{6,7},{7,6},{8,9},{9,8},{10,11... | collective-permute-start | bytes 786440 | tf_op jit(solution)/shard_map/ppermute | solution.py:298
  5.0 6.9 %collective-permute-start.3 = (bf16[256,128]{1,0:T(8,128)(2,1)S(1)}, bf16[256,128]{1,0:T(8,128)(2,1)S(1)}, u32[]{:S(2)}, u32[]{:S(2)}) collective-permute-start(bf16[256,128]{1,0:T(8,128)(2,1)S(1)} %get-tuple-element.33.refs_3_.refs_5_), channel_id=1, source_target_pairs={{0,6},{1,7},{2,4},{3,5},{4,2},{5,3},{6,0},{7,1},{8,14},{9,15},{10,... | collective-permute-start | bytes 196616 | tf_op jit(solution)/shard_map/ppermute | solution.py:298
  8.6 5.4 %collective-permute-start.2 = (bf16[256,128]{1,0:T(8,128)(2,1)S(1)}, bf16[256,128]{1,0:T(8,128)(2,1)S(1)}, u32[]{:S(2)}, u32[]{:S(2)}) collective-permute-start(bf16[256,128]{1,0:T(8,128)(2,1)S(1)} %get-tuple-element.33.refs_3_.refs_5_), channel_id=1, source_target_pairs={{0,4},{1,5},{2,6},{3,7},{4,0},{5,1},{6,2},{7,3},{8,12},{9,13},{10,... | collective-permute-start | bytes 196616 | tf_op jit(solution)/shard_map/ppermute | solution.py:298
  8.6 5.4 %collective-permute-start.1 = (bf16[256,128]{1,0:T(8,128)(2,1)S(1)}, bf16[256,128]{1,0:T(8,128)(2,1)S(1)}, u32[]{:S(2)}, u32[]{:S(2)}) collective-permute-start(bf16[256,128]{1,0:T(8,128)(2,1)S(1)} %get-tuple-element.33.refs_3_.refs_5_), channel_id=1, source_target_pairs={{0,2},{1,3},{2,0},{3,1},{4,6},{5,7},{6,4},{7,5},{8,10},{9,11},{10,... | collective-permute-start | bytes 196616 | tf_op jit(solution)/shard_map/ppermute | solution.py:298
  9.4 7.7 %collective-permute-start.5 = (bf16[32,4096]{1,0:T(8,128)(2,1)S(1)}, bf16[32,4096]{1,0:T(8,128)(2,1)S(1)}, u32[]{:S(2)}, u32[]{:S(2)}) collective-permute-start(bf16[32,4096]{1,0:T(8,128)(2,1)S(1)} %bitcast.11), channel_id=1, source_target_pairs={{0,1},{1,0},{2,3},{3,2},{4,5},{5,4},{6,7},{7,6},{8,9},{9,8},{10,11... | collective-permute-start | bytes 786440 | tf_op jit(solution)/shard_map/ppermute | solution.py:298
  14.4 3.8 %collective-permute-start.4 = (f32[16,256]{1,0:T(8,128)S(1)}, f32[16,256]{1,0:T(8,128)S(1)}, u32[]{:S(2)}, u32[]{:S(2)}) collective-permute-start(f32[16,256]{1,0:T(8,128)S(1)} %get-tuple-element.34.own_ref), channel_id=1, source_target_pairs={{0,1},{1,0},{2,3},{3,2},{4,5},{5,4},{6,7},{7,6},{8,9},{9,8},{10,11... | collective-permute-start | bytes 49160 | tf_op jit(solution)/shard_map/ppermute | solution.py:298
  18.4 5.8 %collective-permute-start.10 = (f32[32,128]{1,0:T(8,128)S(1)}, f32[32,128]{1,0:T(8,128)S(1)}, u32[]{:S(2)}, u32[]{:S(2)}) collective-permute-start(f32[32,128]{1,0:T(8,128)S(1)} %get-tuple-element.46.refs_0_), channel_id=1, source_target_pairs={{0,24},{8,16},{16,8},{24,0},{1,25},{9,17},{17,9},{25,1},{2,26},{10... | collective-permute-start | bytes 49160 | tf_op jit(solution)/shard_map/ppermute | solution.py:298
  18.5 5.7 %collective-permute-start.9 = (f32[32,128]{1,0:T(8,128)S(1)}, f32[32,128]{1,0:T(8,128)S(1)}, u32[]{:S(2)}, u32[]{:S(2)}) collective-permute-start(f32[32,128]{1,0:T(8,128)S(1)} %get-tuple-element.46.refs_0_), channel_id=1, source_target_pairs={{0,16},{8,24},{16,0},{24,8},{1,17},{9,25},{17,1},{25,9},{2,18},{10... | collective-permute-start | bytes 49160 | tf_op jit(solution)/shard_map/ppermute | solution.py:298
  20.1 4.1 %collective-permute-start.8 = (f32[32,128]{1,0:T(8,128)S(1)}, f32[32,128]{1,0:T(8,128)S(1)}, u32[]{:S(2)}, u32[]{:S(2)}) collective-permute-start(f32[32,128]{1,0:T(8,128)S(1)} %get-tuple-element.46.refs_0_), channel_id=1, source_target_pairs={{0,8},{8,0},{16,24},{24,16},{1,9},{9,1},{17,25},{25,17},{2,10},{10... | collective-permute-start | bytes 49160 | tf_op jit(solution)/shard_map/ppermute | solution.py:298
  20.8 7.0 %collective-permute-start.7 = (bf16[256,128]{1,0:T(8,128)(2,1)S(1)}, bf16[256,128]{1,0:T(8,128)(2,1)S(1)}, u32[]{:S(2)}, u32[]{:S(2)}) collective-permute-start(bf16[256,128]{1,0:T(8,128)(2,1)S(1)} %get-tuple-element.41), channel_id=1, source_target_pairs={{0,4},{1,5},{2,6},{3,7},{4,0},{5,1},{6,2},{7,3},{8,12},{9,13},{10,... | collective-permute-start | bytes 196616 | tf_op jit(solution)/shard_map/ppermute | solution.py:298
  22.7 5.3 %collective-permute-start.6 = (bf16[512,128]{1,0:T(8,128)(2,1)S(1)}, bf16[512,128]{1,0:T(8,128)(2,1)S(1)}, u32[]{:S(2)}, u32[]{:S(2)}) collective-permute-start(bf16[512,128]{1,0:T(8,128)(2,1)S(1)} %get-tuple-element.40), channel_id=1, source_target_pairs={{0,1},{1,0},{2,3},{3,2},{4,5},{5,4},{6,7},{7,6},{8,9},{9,8},{10,11... | collective-permute-start | bytes 393224 | tf_op jit(solution)/shard_map/ppermute | solution.py:298
  24.2 6.8 %collective-permute-start.12 = (bf16[288,128]{1,0:T(8,128)(2,1)S(1)}, bf16[288,128]{1,0:T(8,128)(2,1)S(1)}, u32[]{:S(2)}, u32[]{:S(2)}) collective-permute-start(bf16[288,128]{1,0:T(8,128)(2,1)S(1)} %get-tuple-element.51), channel_id=1, source_target_pairs={{0,2},{1,3},{2,0},{3,1},{4,6},{5,7},{6,4},{7,5},{8,10},{9,11},{10,... | collective-permute-start | bytes 221192 | tf_op jit(solution)/shard_map/ppermute | solution.py:298
  25.9 6.2 %collective-permute-start.13 = (bf16[288,128]{1,0:T(8,128)(2,1)S(1)}, bf16[288,128]{1,0:T(8,128)(2,1)S(1)}, u32[]{:S(2)}, u32[]{:S(2)}) collective-permute-start(bf16[288,128]{1,0:T(8,128)(2,1)S(1)} %get-tuple-element.52), channel_id=1, source_target_pairs={{0,6},{1,7},{2,4},{3,5},{4,2},{5,3},{6,0},{7,1},{8,14},{9,15},{10,... | collective-permute-start | bytes 221192 | tf_op jit(solution)/shard_map/ppermute | solution.py:298
  26.1 5.0 %collective-permute-start.11 = (bf16[32,128]{1,0:T(8,128)(2,1)S(1)}, bf16[32,128]{1,0:T(8,128)(2,1)S(1)}, u32[]{:S(2)}, u32[]{:S(2)}) collective-permute-start(bf16[32,128]{1,0:T(8,128)(2,1)S(1)} %get-tuple-element.50), channel_id=1, source_target_pairs={{0,4},{1,5},{2,6},{3,7},{4,0},{5,1},{6,2},{7,3},{8,12},{9,13},{10,... | collective-permute-start | bytes 24584 | tf_op jit(solution)/shard_map/ppermute | solution.py:298

commit v9 on v6

--- a/solution.py
+++ b/solution.py
@@ -95,16 +95,26 @@
         query_out[rows_of(HQ + number, slots), :] = upstream_ref[:, head(number)]
 
 
-def gate_kernel(weight_hbm, input_hbm, gate_ref, input_ref, weight_ref, semaphores):
+def gate_kernel(weight_hbm, input_hbm, gate_ref, input_ref, bias_ref, weight_ref, semaphores):
     copies = [
         pltpu.make_async_copy(weight_hbm, weight_ref, semaphores.at[0]),
         pltpu.make_async_copy(input_hbm, input_ref, semaphores.at[1]),
     ]
     for copy in copies:
         copy.start()
+    slots = input_ref.shape[0]
+    rows = GROUP * slots
+    keys_total = bias_ref.shape[0]
+    own = lax.axis_index("ctx")
+    other = own + 1 - 2 * lax.rem(own, 2)
+    row = lax.broadcasted_iota(jnp.int32, (keys_total, 2 * rows), 0)
+    lane = lax.broadcasted_iota(jnp.int32, (keys_total, 2 * rows), 1)
+    owner = 2 * jnp.bitwise_xor(own // 2, row // slots) + lax.rem(own, 2)
+    key_at = owner * slots + lax.rem(row, slots)
+    query_at = lax.rem(lane, slots) + jnp.where(lane < rows, own, other) * slots
+    bias_ref[...] = jnp.where(key_at <= query_at, 0.0, NEG_LARGE)
     for copy in copies:
         copy.wait()
-    slots = input_ref.shape[0]
     blocks = weight_ref.shape[0]
     total = jnp.zeros((slots, HD), jnp.float32)
     for number in range(blocks):
@@ -130,19 +140,10 @@
 
 
 def scores_kernel(slots, *refs):
-    gate_ref, own_ref, other_ref = refs[:3]
-    pair_refs = refs[3:-3]
-    grown_out, grad_out, stats_out = refs[-3:]
-    rows = GROUP * slots
-    keys_total = len(pair_refs) * slots
-    own = lax.axis_index("ctx")
-    other = own + 1 - 2 * lax.rem(own, 2)
-    row = lax.broadcasted_iota(jnp.int32, (keys_total, 2 * rows), 0)
-    lane = lax.broadcasted_iota(jnp.int32, (keys_total, 2 * rows), 1)
-    owner = 2 * jnp.bitwise_xor(own // 2, row // slots) + lax.rem(own, 2)
-    key_at = owner * slots + lax.rem(row, slots)
-    query_at = lax.rem(lane, slots) + jnp.where(lane < rows, own, other) * slots
-    bias = jnp.where(key_at <= query_at, 0.0, NEG_LARGE)
+    gate_ref, bias_ref, own_ref, other_ref = refs[:4]
+    pair_refs = refs[4:-2]
+    grown_out, stats_out = refs[-2:]
+    rows = GROUP * slots
     across = (((1,), (1,)), ((), ()))
     for number in range(KVH):
         key_tile, value_tile, query_tile, upstream_tile = tiles(
@@ -151,14 +152,13 @@
         scores = lax.dot_general(
             key_tile, query_tile, across, preferred_element_type=jnp.float32
         )
-        scores = scores * (1.0 / math.sqrt(HD)) + bias
+        scores = scores * (1.0 / math.sqrt(HD)) + bias_ref[...]
         top = jnp.max(scores, axis=0, keepdims=True)
         grown = jnp.exp(scores - top)
         prob_grad = lax.dot_general(
             value_tile, upstream_tile, across, preferred_element_type=jnp.float32
         )
         grown_out[number] = grown
-        grad_out[number] = prob_grad
         stats_out[number : number + 1, :] = top
         stats_out[KVH + number : KVH + number + 1, :] = jnp.sum(grown, axis=0, keepdims=True)
         stats_out[2 * KVH + number : 2 * KVH + number + 1, :] = jnp.sum(
@@ -169,7 +169,9 @@
     )
 
 
-def combine_kernel(own_ref, other_ref, input_ref, input_other_ref, coef_out, router_out):
+def combine_kernel(
+    own_ref, other_ref, input_ref, input_other_ref, coef_out, router_out, send_out
+):
     slots = input_ref.shape[0]
     rows = GROUP * slots
     mine = own_ref[...]
@@ -197,22 +199,29 @@
             axis=0,
             keepdims=True,
         )
+    send_out[...] = router_out[...].astype(jnp.bfloat16)
 
 
 def terms_kernel(slots, half, *refs):
-    coef_ref, grown_ref, grad_ref, own_ref, other_ref = refs[:5]
-    pair_refs = refs[5 : 5 + half]
-    query_out, query_send, term_own = refs[5 + half : 8 + half]
-    term_refs = refs[8 + half :]
+    coef_ref, grown_ref, own_ref, other_ref = refs[:4]
+    pair_refs = refs[4 : 4 + half]
+    query_out, query_send, term_own = refs[4 + half : 7 + half]
+    term_refs = refs[7 + half :]
     rows = GROUP * slots
     scale = 1.0 / math.sqrt(HD)
     for number in range(KVH):
-        key_tile, _, query_tile, upstream_tile = tiles(
+        key_tile, value_tile, query_tile, upstream_tile = tiles(
             pair_refs, (own_ref, other_ref), number, slots
+        )
+        prob_grad = lax.dot_general(
+            value_tile,
+            upstream_tile,
+            (((1,), (1,)), ((), ())),
+            preferred_element_type=jnp.float32,
         )
         gated = grown_ref[number] * coef_ref[number : number + 1, :]
         inner = coef_ref[KVH + number : KVH + number + 1, :]
-        score_grad = (gated * (grad_ref[number] - inner) * scale).astype(jnp.bfloat16)
+        score_grad = (gated * (prob_grad - inner) * scale).astype(jnp.bfloat16)
         key_term = jnp.dot(score_grad, query_tile, preferred_element_type=jnp.float32)
         value_term = jnp.dot(
             gated.astype(jnp.bfloat16), upstream_tile, preferred_element_type=jnp.float32
@@ -236,7 +245,7 @@
     router_out, send_out = refs[groups + count : groups + count + 2]
     router = refs[0][...]
     for ref in refs[1:groups]:
-        router += ref[...]
+        router += ref[...].astype(jnp.float32)
     router_out[...] = router
     narrow = router.astype(jnp.bfloat16)
     send_out[...] = narrow
@@ -328,32 +337,33 @@
     pairs = [pair] + [
         exchange(pair, "ctx", 2 * step, count) for step in range(1, half)
     ]
-    gate, inputs = call(
+    gate, inputs, bias = call(
         gate_kernel,
-        [near((8, rows), f32), near((slots, width), bf16)],
+        [
+            near((8, rows), f32),
+            near((slots, width), bf16),
+            near((half * slots, 2 * rows), f32),
+        ],
         [],
         [router_weight.reshape(lines, HD), routed_inputs[0]],
         [near((lines, HD), f32)],
     )
     inputs_other = swap(routed_inputs[0])
-    grown, grad, stats = call(
+    grown, stats = call(
         functools.partial(scores_kernel, slots),
         [
             near((KVH, half * slots, 2 * rows), f32),
-            near((KVH, half * slots, 2 * rows), f32),
             near((4 * KVH, 2 * rows), f32),
         ],
-        [gate, query, query_other, *pairs],
+        [gate, bias, query, query_other, *pairs],
         cost=SCORES_COST,
     )
-    coef, router = call(
+    coef, router, router_send = call(
         combine_kernel,
-        [near((2 * KVH, 2 * rows), f32), near((lines, HD), f32)],
+        [near((2 * KVH, 2 * rows), f32), near((lines, HD), f32), near((lines, HD), bf16)],
         [stats, swap(stats), inputs, inputs_other],
     )
-    routers = [router] + [
-        exchange(router, "dp", step, groups) for step in range(1, groups)
-    ]
+    routers = [router] + [exchange(router_send, "dp", step, groups) for step in range(1, groups)]
     query_own, query_send, term_own, *terms = call(
         functools.partial(terms_kernel, slots, half),
         [
@@ -362,7 +372,7 @@
             near((2 * KVH * slots, HD), f32),
         ]
         + [near((2 * KVH * slots, HD), bf16)] * (half - 1),
-        [coef, grown, grad, query, query_other, *pairs],
+        [coef, grown, query, query_other, *pairs],
         cost=TERMS_COST,
     )
     query_back = swap(query_send)

time: 32.3 us -> 32.3 us (level)
  transfers between devices with their start and end apart: 14 -> 14, of which waited for: 7 -> 6; matrix products, arithmetic and copies ran while one was open for 0% -> 0% of each run, Pallas kernels for 9% -> 10%
where the time goes in v9:
time: 32.3 us; the launch traced here: 32 us
  starting transfers between devices  18 us (56%)
  waiting for transfers between devices  8.03 us (25%)
  Pallas kernels  5.28 us (16%)
  between operations  0.7 us (2%)
    ppermute x14, starting transfers between devices, exchange(): return lax.ppermute(array, axis, [(at, at ^ step) for at in range(size)])  18 us
    ppermute x14, waiting for transfers between devices, exchange(): return lax.ppermute(array, axis, [(at, at ^ step) for at in range(size)])  8.03 us
    pallas_call x8, Pallas kernels, call(): pl.pallas_call(kernel, out_shape=outs, in_specs=[local] * len(args) + [di...  5.28 us
  transfers between devices with their start and end apart: 14, of which 6 were waited for; matrix products, arithmetic and copies ran while one was open for 0% of the time, Pallas kernels for 10%

profile of v9, /device:TPU:0, one launch (start us, length us, event | category | flops | bytes accessed | tf_op | source)
XLA Modules:
  0.0 32.0 jit_solution(16631628672720738800)
XLA Ops:
  0.6 0.0 copy-start
  0.6 1.3 %shard_map.111 = (bf16[256,128]{1,0:T(8,128)(2,1)S(1)}, bf16[1024,128]{1,0:T(8,128)(2,1)S(1)}, f32[64,128]{1,0:T(8,128)S(1)}) custom-call(s32[1,32]{1,0:T(1,128)} %refs_0_.1, f32[2,128]{1,0:T(2,128)} %constant.2.clone.refs_1_, bf16[32,512]{1,0:T(8,128)(2,1)} %bitcast.14, bf16[32,512]{1,0:T(8,128)(2,1)} %bitcast.15, bf16[32,2048]{1,0:T(8,128)(2,1)} %bitcast.12, ...), custom_call_target="tpu_custom_call" | custom-call | tf_op jit(solution)/shard_map/pallas_call | solution.py:295
  1.9 3.0 %collective-permute-start = (bf16[1024,128]{1,0:T(8,128)(2,1)S(1)}, bf16[1024,128]{1,0:T(8,128)(2,1)S(1)}, u32[]{:S(2)}, u32[]{:S(2)}) collective-permute-start(bf16[1024,128]{1,0:T(8,128)(2,1)S(1)} %get-tuple-element.34.refs_2_), channel_id=1, source_target_pairs={{0,1},{1,0},{2,3},{3,2},{4,5},{5,4},{6,7},{7,6},{8,9},{9,8},{10,11... | collective-permute-start | bytes 786440 | tf_op jit(solution)/shard_map/ppermute | solution.py:307
  5.0 3.6 %collective-permute-start.3 = (bf16[256,128]{1,0:T(8,128)(2,1)S(1)}, bf16[256,128]{1,0:T(8,128)(2,1)S(1)}, u32[]{:S(2)}, u32[]{:S(2)}) collective-permute-start(bf16[256,128]{1,0:T(8,128)(2,1)S(1)} %get-tuple-element.35.refs_4_), channel_id=1, source_target_pairs={{0,6},{1,7},{2,4},{3,5},{4,2},{5,3},{6,0},{7,1},{8,14},{9,15},{10,... | collective-permute-start | bytes 196616 | tf_op jit(solution)/shard_map/ppermute | solution.py:307
  8.6 0.0 collective-permute-start.2
  8.6 0.8 %collective-permute-start.1 = (bf16[256,128]{1,0:T(8,128)(2,1)S(1)}, bf16[256,128]{1,0:T(8,128)(2,1)S(1)}, u32[]{:S(2)}, u32[]{:S(2)}) collective-permute-start(bf16[256,128]{1,0:T(8,128)(2,1)S(1)} %get-tuple-element.35.refs_4_), channel_id=1, source_target_pairs={{0,2},{1,3},{2,0},{3,1},{4,6},{5,7},{6,4},{7,5},{8,10},{9,11},{10,... | collective-permute-start | bytes 196616 | tf_op jit(solution)/shard_map/ppermute | solution.py:307
  9.4 0.0 copy-done
  9.4 0.3 collective-permute-start.5
  9.6 1.1 %shard_map.112 = (f32[8,128]{1,0:T(8,128)S(1)}, bf16[32,4096]{1,0:T(8,128)(2,1)S(1)}, f32[128,256]{1,0:T(8,128)S(1)}) custom-call(f32[32,128]{1,0:T(8,128)} %bitcast.16, bf16[32,4096]{1,0:T(8,128)(2,1)} %bitcast.10), custom_call_target="tpu_custom_call" | custom-call | tf_op jit(solution)/shard_map/pallas_call | solution.py:295
  10.8 1.0 %collective-permute-done.3.refs_7_ = bf16[256,128]{1,0:T(8,128)(2,1)S(1)} collective-permute-done((bf16[256,128]{1,0:T(8,128)(2,1)S(1)}, bf16[256,128]{1,0:T(8,128)(2,1)S(1)}, u32[]{:S(2)}, u32[]{:S(2)}) %collective-permute-start.3) | collective-permute-done | bytes 65568 | tf_op jit(solution)/shard_map/ppermute | solution.py:307
  11.8 2.1 %collective-permute-done.2.refs_6_ = bf16[256,128]{1,0:T(8,128)(2,1)S(1)} collective-permute-done((bf16[256,128]{1,0:T(8,128)(2,1)S(1)}, bf16[256,128]{1,0:T(8,128)(2,1)S(1)}, u32[]{:S(2)}, u32[]{:S(2)}) %collective-permute-start.2) | collective-permute-done | bytes 65568 | tf_op jit(solution)/shard_map/ppermute | solution.py:307
  13.9 0.1 collective-permute-done.1.refs_5_
  14.0 0.0 collective-permute-done.refs_3_
  14.0 0.4 %shard_map.113 = (f32[4,128,256]{2,1,0:T(8,128)S(1)}, f32[16,256]{1,0:T(8,128)S(1)}) custom-call(f32[8,128]{1,0:T(8,128)S(1)} %get-tuple-element.32.refs_0_, f32[128,256]{1,0:T(8,128)S(1)} %get-tuple-element.33.refs_1_, bf16[1024,128]{1,0:T(8,128)(2,1)S(1)} %get-tuple-element.34.refs_2_, bf16[1024,128]{1,0:T(8,128)(2,1)S(1)} %collective-permute-done.refs_3_, ...), custom_call_target="tpu_custom_call" | custom-call | flops 20000000000 | tf_op jit(solution)/shard_map/pallas_call | solution.py:295
  14.4 0.5 %collective-permute-start.4 = (f32[16,256]{1,0:T(8,128)S(1)}, f32[16,256]{1,0:T(8,128)S(1)}, u32[]{:S(2)}, u32[]{:S(2)}) collective-permute-start(f32[16,256]{1,0:T(8,128)S(1)} %get-tuple-element.36.own_ref), channel_id=1, source_target_pairs={{0,1},{1,0},{2,3},{3,2},{4,5},{5,4},{6,7},{7,6},{8,9},{9,8},{10,11... | collective-permute-start | bytes 49160 | tf_op jit(solution)/shard_map/ppermute | solution.py:307
  14.9 2.2 %collective-permute-done.5.input_other_ref = bf16[32,4096]{1,0:T(8,128)(2,1)S(1)} collective-permute-done((bf16[32,4096]{1,0:T(8,128)(2,1)S(1)}, bf16[32,4096]{1,0:T(8,128)(2,1)S(1)}, u32[]{:S(2)}, u32[]{:S(2)}) %collective-permute-start.5) | collective-permute-done | bytes 262176 | tf_op jit(solution)/shard_map/ppermute | solution.py:307
  17.1 1.1 %collective-permute-done.4.other_ref = f32[16,256]{1,0:T(8,128)S(1)} collective-permute-done((f32[16,256]{1,0:T(8,128)S(1)}, f32[16,256]{1,0:T(8,128)S(1)}, u32[]{:S(2)}, u32[]{:S(2)}) %collective-permute-start.4) | collective-permute-done | bytes 16416 | tf_op jit(solution)/shard_map/ppermute | solution.py:307
  18.2 0.2 shard_map.114
  18.4 0.1 collective-permute-start.10
  18.5 1.6 %collective-permute-start.9 = (bf16[32,128]{1,0:T(8,128)(2,1)S(1)}, bf16[32,128]{1,0:T(8,128)(2,1)S(1)}, u32[]{:S(2)}, u32[]{:S(2)}) collective-permute-start(bf16[32,128]{1,0:T(8,128)(2,1)S(1)} %get-tuple-element.48), channel_id=1, source_target_pairs={{0,16},{8,24},{16,0},{24,8},{1,17},{9,25},{17,1},{25,9},{2,18},{10... | collective-permute-start | bytes 24584 | tf_op jit(solution)/shard_map/ppermute | solution.py:307
  20.1 0.3 collective-permute-start.8
  20.4 0.7 %shard_map.115 = (f32[512,128]{1,0:T(8,128)S(1)}, bf16[512,128]{1,0:T(8,128)(2,1)S(1)}, f32[256,128]{1,0:T(8,128)S(1)}, bf16[256,128]{1,0:T(8,128)(2,1)S(1)}, bf...) custom-call(f32[8,256]{1,0:T(8,128)S(1)} %get-tuple-element.38.refs_0_, ...), custom_call_target="tpu_custom_call" | custom-call | flops 20000000000 | tf_op jit(solution)/shard_map/pallas_call | solution.py:295
  21.1 1.9 %collective-permute-start.7 = (bf16[256,128]{1,0:T(8,128)(2,1)S(1)}, bf16[256,128]{1,0:T(8,128)(2,1)S(1)}, u32[]{:S(2)}, u32[]{:S(2)}) collective-permute-start(bf16[256,128]{1,0:T(8,128)(2,1)S(1)} %get-tuple-element.42), channel_id=1, source_target_pairs={{0,4},{1,5},{2,6},{3,7},{4,0},{5,1},{6,2},{7,3},{8,12},{9,13},{10,... | collective-permute-start | bytes 196616 | tf_op jit(solution)/shard_map/ppermute | solution.py:307
  23.0 1.5 %collective-permute-start.6 = (bf16[512,128]{1,0:T(8,128)(2,1)S(1)}, bf16[512,128]{1,0:T(8,128)(2,1)S(1)}, u32[]{:S(2)}, u32[]{:S(2)}) collective-permute-start(bf16[512,128]{1,0:T(8,128)(2,1)S(1)} %get-tuple-element.41), channel_id=1, source_target_pairs={{0,1},{1,0},{2,3},{3,2},{4,5},{5,4},{6,7},{7,6},{8,9},{9,8},{10,11... | collective-permute-start | bytes 393224 | tf_op jit(solution)/shard_map/ppermute | solution.py:307
  24.5 0.0 collective-permute-done.10.refs_3_
  24.5 0.0 collective-permute-done.9.refs_2_
  24.5 0.0 collective-permute-done.8.refs_1_
  24.5 1.4 %collective-permute-start.12 = (bf16[288,128]{1,0:T(8,128)(2,1)S(1)}, bf16[288,128]{1,0:T(8,128)(2,1)S(1)}, u32[]{:S(2)}, u32[]{:S(2)}) collective-permute-start(bf16[288,128]{1,0:T(8,128)(2,1)S(1)} %get-tuple-element.53), channel_id=1, source_target_pairs={{0,6},{1,7},{2,4},{3,5},{4,2},{5,3},{6,0},{7,1},{8,14},{9,15},{10,... | collective-permute-start | bytes 221192 | tf_op jit(solution)/shard_map/ppermute | solution.py:307
  26.0 0.3 collective-permute-start.13
  26.3 2.7 %collective-permute-start.11 = (bf16[32,128]{1,0:T(8,128)(2,1)S(1)}, bf16[32,128]{1,0:T(8,128)(2,1)S(1)}, u32[]{:S(2)}, u32[]{:S(2)}) collective-permute-start(bf16[32,128]{1,0:T(8,128)(2,1)S(1)} %get-tuple-element.52), channel_id=1, source_target_pairs={{0,4},{1,5},{2,6},{3,7},{4,0},{5,1},{6,2},{7,3},{8,12},{9,13},{10,... | collective-permute-start | bytes 24584 | tf_op jit(solution)/shard_map/ppermute | solution.py:307
  29.0 0.0 collective-permute-done.7.far_ref
  29.0 0.0 collective-permute-done.6.other_ref
  29.0 0.8 %shard_map.116 = (bf16[32,2048]{1,0:T(8,128)(2,1)}, f32[64,128]{1,0:T(8,128)S(1)}, f32[256,128]{1,0:T(8,128)S(1)}) custom-call(f32[64,128]{1,0:T(8,128)S(1)} %get-tuple-element.31.trig_ref, f32[512,128]{1,0:T(8,128)S(1)} %get-tuple-element.40.own_ref, bf16[512,128]{1,0:T(8,128)(2,1)S(1)} %collective-permute-done.6.other_ref, ...), custom_call_target="tpu_custom_call" | custom-call | flops 500000000 | tf_op jit(solution)/shard_map/pallas_call | solution.py:295
  29.8 1.5 %collective-permute-done.11.refs_3_ = bf16[32,128]{1,0:T(8,128)(2,1)S(1)} collective-permute-done((bf16[32,128]{1,0:T(8,128)(2,1)S(1)}, bf16[32,128]{1,0:T(8,128)(2,1)S(1)}, u32[]{:S(2)}, u32[]{:S(2)}) %collective-permute-start.11) | collective-permute-done | bytes 8224 | tf_op jit(solution)/shard_map/ppermute | solution.py:307
  31.3 0.0 collective-permute-done.12.refs_4_
  31.3 0.0 collective-permute-done.13.refs_5_
  31.3 0.7 %shard_map.118 = (bf16[32,512]{1,0:T(8,128)(2,1)}, bf16[32,512]{1,0:T(8,128)(2,1)}, f32[32,128]{1,0:T(8,128)}) custom-call(f32[64,128]{1,0:T(8,128)S(1)} %get-tuple-element.45.refs_0_, f32[256,128]{1,0:T(8,128)S(1)} %get-tuple-element.46.refs_1_, f32[32,128]{1,0:T(8,128)S(1)} %get-tuple-element.51.refs_2_, ...), custom_call_target="tpu_custom_call" | custom-call | tf_op jit(solution)/shard_map/pallas_call | solution.py:295
  (1 shorter events, 0.0 us)
Async XLA Ops:
  0.6 8.7 %copy-start = (bf16[1,32,4096]{2,1,0:T(8,128)(2,1)S(1)}, bf16[1,32,4096]{2,1,0:T(8,128)(2,1)}, u32[]{:S(2)}) copy-start(bf16[1,32,4096]{2,1,0:T(8,128)(2,1)} %param.12) | copy-start | bytes 786436
  1.9 12.1 %collective-permute-start = (bf16[1024,128]{1,0:T(8,128)(2,1)S(1)}, bf16[1024,128]{1,0:T(8,128)(2,1)S(1)}, u32[]{:S(2)}, u32[]{:S(2)}) collective-permute-start(bf16[1024,128]{1,0:T(8,128)(2,1)S(1)} %get-tuple-element.34.refs_2_), channel_id=1, source_target_pairs={{0,1},{1,0},{2,3},{3,2},{4,5},{5,4},{6,7},{7,6},{8,9},{9,8},{10,11... | collective-permute-start | bytes 786440 | tf_op jit(solution)/shard_map/ppermute | solution.py:307
  5.0 6.9 %collective-permute-start.3 = (bf16[256,128]{1,0:T(8,128)(2,1)S(1)}, bf16[256,128]{1,0:T(8,128)(2,1)S(1)}, u32[]{:S(2)}, u32[]{:S(2)}) collective-permute-start(bf16[256,128]{1,0:T(8,128)(2,1)S(1)} %get-tuple-element.35.refs_4_), channel_id=1, source_target_pairs={{0,6},{1,7},{2,4},{3,5},{4,2},{5,3},{6,0},{7,1},{8,14},{9,15},{10,... | collective-permute-start | bytes 196616 | tf_op jit(solution)/shard_map/ppermute | solution.py:307
  8.6 5.4 %collective-permute-start.2 = (bf16[256,128]{1,0:T(8,128)(2,1)S(1)}, bf16[256,128]{1,0:T(8,128)(2,1)S(1)}, u32[]{:S(2)}, u32[]{:S(2)}) collective-permute-start(bf16[256,128]{1,0:T(8,128)(2,1)S(1)} %get-tuple-element.35.refs_4_), channel_id=1, source_target_pairs={{0,4},{1,5},{2,6},{3,7},{4,0},{5,1},{6,2},{7,3},{8,12},{9,13},{10,... | collective-permute-start | bytes 196616 | tf_op jit(solution)/shard_map/ppermute | solution.py:307
  8.6 5.4 %collective-permute-start.1 = (bf16[256,128]{1,0:T(8,128)(2,1)S(1)}, bf16[256,128]{1,0:T(8,128)(2,1)S(1)}, u32[]{:S(2)}, u32[]{:S(2)}) collective-permute-start(bf16[256,128]{1,0:T(8,128)(2,1)S(1)} %get-tuple-element.35.refs_4_), channel_id=1, source_target_pairs={{0,2},{1,3},{2,0},{3,1},{4,6},{5,7},{6,4},{7,5},{8,10},{9,11},{10,... | collective-permute-start | bytes 196616 | tf_op jit(solution)/shard_map/ppermute | solution.py:307
  9.4 7.7 %collective-permute-start.5 = (bf16[32,4096]{1,0:T(8,128)(2,1)S(1)}, bf16[32,4096]{1,0:T(8,128)(2,1)S(1)}, u32[]{:S(2)}, u32[]{:S(2)}) collective-permute-start(bf16[32,4096]{1,0:T(8,128)(2,1)S(1)} %bitcast.11), channel_id=1, source_target_pairs={{0,1},{1,0},{2,3},{3,2},{4,5},{5,4},{6,7},{7,6},{8,9},{9,8},{10,11... | collective-permute-start | bytes 786440 | tf_op jit(solution)/shard_map/ppermute | solution.py:307
  14.4 3.8 %collective-permute-start.4 = (f32[16,256]{1,0:T(8,128)S(1)}, f32[16,256]{1,0:T(8,128)S(1)}, u32[]{:S(2)}, u32[]{:S(2)}) collective-permute-start(f32[16,256]{1,0:T(8,128)S(1)} %get-tuple-element.36.own_ref), channel_id=1, source_target_pairs={{0,1},{1,0},{2,3},{3,2},{4,5},{5,4},{6,7},{7,6},{8,9},{9,8},{10,11... | collective-permute-start | bytes 49160 | tf_op jit(solution)/shard_map/ppermute | solution.py:307
  18.4 6.1 %collective-permute-start.10 = (bf16[32,128]{1,0:T(8,128)(2,1)S(1)}, bf16[32,128]{1,0:T(8,128)(2,1)S(1)}, u32[]{:S(2)}, u32[]{:S(2)}) collective-permute-start(bf16[32,128]{1,0:T(8,128)(2,1)S(1)} %get-tuple-element.48), channel_id=1, source_target_pairs={{0,24},{8,16},{16,8},{24,0},{1,25},{9,17},{17,9},{25,1},{2,26},{10... | collective-permute-start | bytes 24584 | tf_op jit(solution)/shard_map/ppermute | solution.py:307
  18.5 6.0 %collective-permute-start.9 = (bf16[32,128]{1,0:T(8,128)(2,1)S(1)}, bf16[32,128]{1,0:T(8,128)(2,1)S(1)}, u32[]{:S(2)}, u32[]{:S(2)}) collective-permute-start(bf16[32,128]{1,0:T(8,128)(2,1)S(1)} %get-tuple-element.48), channel_id=1, source_target_pairs={{0,16},{8,24},{16,0},{24,8},{1,17},{9,25},{17,1},{25,9},{2,18},{10... | collective-permute-start | bytes 24584 | tf_op jit(solution)/shard_map/ppermute | solution.py:307
  20.1 4.4 %collective-permute-start.8 = (bf16[32,128]{1,0:T(8,128)(2,1)S(1)}, bf16[32,128]{1,0:T(8,128)(2,1)S(1)}, u32[]{:S(2)}, u32[]{:S(2)}) collective-permute-start(bf16[32,128]{1,0:T(8,128)(2,1)S(1)} %get-tuple-element.48), channel_id=1, source_target_pairs={{0,8},{8,0},{16,24},{24,16},{1,9},{9,1},{17,25},{25,17},{2,10},{10... | collective-permute-start | bytes 24584 | tf_op jit(solution)/shard_map/ppermute | solution.py:307
  21.1 7.9 %collective-permute-start.7 = (bf16[256,128]{1,0:T(8,128)(2,1)S(1)}, bf16[256,128]{1,0:T(8,128)(2,1)S(1)}, u32[]{:S(2)}, u32[]{:S(2)}) collective-permute-start(bf16[256,128]{1,0:T(8,128)(2,1)S(1)} %get-tuple-element.42), channel_id=1, source_target_pairs={{0,4},{1,5},{2,6},{3,7},{4,0},{5,1},{6,2},{7,3},{8,12},{9,13},{10,... | collective-permute-start | bytes 196616 | tf_op jit(solution)/shard_map/ppermute | solution.py:307
  23.0 6.0 %collective-permute-start.6 = (bf16[512,128]{1,0:T(8,128)(2,1)S(1)}, bf16[512,128]{1,0:T(8,128)(2,1)S(1)}, u32[]{:S(2)}, u32[]{:S(2)}) collective-permute-start(bf16[512,128]{1,0:T(8,128)(2,1)S(1)} %get-tuple-element.41), channel_id=1, source_target_pairs={{0,1},{1,0},{2,3},{3,2},{4,5},{5,4},{6,7},{7,6},{8,9},{9,8},{10,11... | collective-permute-start | bytes 393224 | tf_op jit(solution)/shard_map/ppermute | solution.py:307
  24.5 6.8 %collective-permute-start.12 = (bf16[288,128]{1,0:T(8,128)(2,1)S(1)}, bf16[288,128]{1,0:T(8,128)(2,1)S(1)}, u32[]{:S(2)}, u32[]{:S(2)}) collective-permute-start(bf16[288,128]{1,0:T(8,128)(2,1)S(1)} %get-tuple-element.53), channel_id=1, source_target_pairs={{0,6},{1,7},{2,4},{3,5},{4,2},{5,3},{6,0},{7,1},{8,14},{9,15},{10,... | collective-permute-start | bytes 221192 | tf_op jit(solution)/shard_map/ppermute | solution.py:307
  26.0 5.3 %collective-permute-start.13 = (bf16[288,128]{1,0:T(8,128)(2,1)S(1)}, bf16[288,128]{1,0:T(8,128)(2,1)S(1)}, u32[]{:S(2)}, u32[]{:S(2)}) collective-permute-start(bf16[288,128]{1,0:T(8,128)(2,1)S(1)} %get-tuple-element.54), channel_id=1, source_target_pairs={{0,2},{1,3},{2,0},{3,1},{4,6},{5,7},{6,4},{7,5},{8,10},{9,11},{10,... | collective-permute-start | bytes 221192 | tf_op jit(solution)/shard_map/ppermute | solution.py:307
  26.3 5.0 %collective-permute-start.11 = (bf16[32,128]{1,0:T(8,128)(2,1)S(1)}, bf16[32,128]{1,0:T(8,128)(2,1)S(1)}, u32[]{:S(2)}, u32[]{:S(2)}) collective-permute-start(bf16[32,128]{1,0:T(8,128)(2,1)S(1)} %get-tuple-element.52), channel_id=1, source_target_pairs={{0,4},{1,5},{2,6},{3,7},{4,0},{5,1},{6,2},{7,3},{8,12},{9,13},{10,... | collective-permute-start | bytes 24584 | tf_op jit(solution)/shard_map/ppermute | solution.py:307

commit v10 on v6

--- a/solution.py
+++ b/solution.py
@@ -20,6 +20,7 @@
 TERMS_COST = 20 * 10**9
 RIDE_COST = 20 * 10**9
 QUERY_COST = 5 * 10**8
+QUERY_TERMS_COST = 1
 
 
 def rope_table():
@@ -202,8 +203,8 @@
 def terms_kernel(slots, half, *refs):
     coef_ref, grown_ref, grad_ref, own_ref, other_ref = refs[:5]
     pair_refs = refs[5 : 5 + half]
-    query_out, query_send, term_own = refs[5 + half : 8 + half]
-    term_refs = refs[8 + half :]
+    score_out, term_own = refs[5 + half : 7 + half]
+    term_refs = refs[7 + half :]
     rows = GROUP * slots
     scale = 1.0 / math.sqrt(HD)
     for number in range(KVH):
@@ -213,6 +214,7 @@
         gated = grown_ref[number] * coef_ref[number : number + 1, :]
         inner = coef_ref[KVH + number : KVH + number + 1, :]
         score_grad = (gated * (grad_ref[number] - inner) * scale).astype(jnp.bfloat16)
+        score_out[number] = score_grad
         key_term = jnp.dot(score_grad, query_tile, preferred_element_type=jnp.float32)
         value_term = jnp.dot(
             gated.astype(jnp.bfloat16), upstream_tile, preferred_element_type=jnp.float32
@@ -223,8 +225,20 @@
         for at, ref in enumerate(term_refs, 1):
             ref[key_rows, :] = key_term[rows_of(at, slots)].astype(jnp.bfloat16)
             ref[value_rows, :] = value_term[rows_of(at, slots)].astype(jnp.bfloat16)
+
+
+def query_terms_kernel(score_ref, *refs):
+    pair_refs = refs[:-2]
+    query_out, query_send = refs[-2:]
+    slots = pair_refs[0].shape[0] // (2 * KVH)
+    rows = GROUP * slots
+    for number in range(KVH):
+        key_tile = jnp.concatenate([ref[rows_of(number, slots), :] for ref in pair_refs], axis=0)
         query_term = lax.dot_general(
-            score_grad, key_tile, (((0,), (0,)), ((), ())), preferred_element_type=jnp.float32
+            score_ref[number],
+            key_tile,
+            (((0,), (0,)), ((), ())),
+            preferred_element_type=jnp.float32,
         )
         query_out[rows_of(number, rows), :] = query_term[0:rows]
         query_send[rows_of(number, rows), :] = query_term[rows:].astype(jnp.bfloat16)
@@ -354,16 +368,18 @@
     routers = [router] + [
         exchange(router, "dp", step, groups) for step in range(1, groups)
     ]
-    query_own, query_send, term_own, *terms = call(
+    score_grad, term_own, *terms = call(
         functools.partial(terms_kernel, slots, half),
-        [
-            near((HQ * slots, HD), f32),
-            near((HQ * slots, HD), bf16),
-            near((2 * KVH * slots, HD), f32),
-        ]
+        [near((KVH, half * slots, 2 * rows), bf16), near((2 * KVH * slots, HD), f32)]
         + [near((2 * KVH * slots, HD), bf16)] * (half - 1),
         [coef, grown, grad, query, query_other, *pairs],
         cost=TERMS_COST,
+    )
+    query_own, query_send = call(
+        query_terms_kernel,
+        [near((HQ * slots, HD), f32), near((HQ * slots, HD), bf16)],
+        [score_grad, *pairs],
+        cost=QUERY_TERMS_COST,
     )
     query_back = swap(query_send)
     early = half // 2

time: 32.3 us -> 32.3 us (level)
    pallas_call x8 -> x9, Pallas kernels: 4.96 us -> 5.12 us  [call(): pl.pallas_call(kernel, out_shape=outs, in_specs=[local] * len(args) + [di...]
  transfers between devices with their start and end apart: 14 -> 14, of which waited for: 7 -> 6; matrix products, arithmetic and copies ran while one was open for 0% -> 0% of each run, Pallas kernels for 9% -> 9%
where the time goes in v10:
time: 32.3 us; the launch traced here: 32 us
  starting transfers between devices  18.1 us (56%)
  waiting for transfers between devices  8.11 us (25%)
  Pallas kernels  5.12 us (16%)
  between operations  0.71 us (2%)
    ppermute x14, starting transfers between devices, exchange(): return lax.ppermute(array, axis, [(at, at ^ step) for at in range(size)])  18.1 us
    ppermute x14, waiting for transfers between devices, exchange(): return lax.ppermute(array, axis, [(at, at ^ step) for at in range(size)])  8.11 us
    pallas_call x9, Pallas kernels, call(): pl.pallas_call(kernel, out_shape=outs, in_specs=[local] * len(args) + [di...  5.12 us
  transfers between devices with their start and end apart: 14, of which 6 were waited for; matrix products, arithmetic and copies ran while one was open for 0% of the time, Pallas kernels for 9%

profile of v10, /device:TPU:0, one launch (start us, length us, event | category | flops | bytes accessed | tf_op | source)
XLA Modules:
  0.0 32.0 jit_solution(10896257549413082380)
XLA Ops:
  0.6 0.0 copy-start
  0.6 1.3 %shard_map.111 = (bf16[256,128]{1,0:T(8,128)(2,1)S(1)}, bf16[1024,128]{1,0:T(8,128)(2,1)S(1)}, f32[64,128]{1,0:T(8,128)S(1)}) custom-call(s32[1,32]{1,0:T(1,128)} %refs_0_.1, f32[2,128]{1,0:T(2,128)} %constant.2.clone.refs_1_, bf16[32,512]{1,0:T(8,128)(2,1)} %bitcast.14, bf16[32,512]{1,0:T(8,128)(2,1)} %bitcast.15, bf16[32,2048]{1,0:T(8,128)(2,1)} %bitcast.12, ...), custom_call_target="tpu_custom_call" | custom-call | tf_op jit(solution)/shard_map/pallas_call | solution.py:300
  1.9 3.0 %collective-permute-start = (bf16[1024,128]{1,0:T(8,128)(2,1)S(1)}, bf16[1024,128]{1,0:T(8,128)(2,1)S(1)}, u32[]{:S(2)}, u32[]{:S(2)}) collective-permute-start(bf16[1024,128]{1,0:T(8,128)(2,1)S(1)} %get-tuple-element.33.refs_1_.refs_3_), channel_id=1, source_target_pairs={{0,1},{1,0},{2,3},{3,2},{4,5},{5,4},{6,7},{7,6},{8,9},{9,8},{10,11... | collective-permute-start | bytes 786440 | tf_op jit(solution)/shard_map/ppermute | solution.py:312
  5.0 3.6 %collective-permute-start.3 = (bf16[256,128]{1,0:T(8,128)(2,1)S(1)}, bf16[256,128]{1,0:T(8,128)(2,1)S(1)}, u32[]{:S(2)}, u32[]{:S(2)}) collective-permute-start(bf16[256,128]{1,0:T(8,128)(2,1)S(1)} %get-tuple-element.34.refs_3_.refs_5_.refs_0_), channel_id=1, source_target_pairs={{0,6},{1,7},{2,4},{3,5},{4,2},{5,3},{6,0},{7,1},{8,14},{9,15},{10,... | collective-permute-start | bytes 196616 | tf_op jit(solution)/shard_map/ppermute | solution.py:312
  8.6 0.0 collective-permute-start.2
  8.6 0.8 %collective-permute-start.1 = (bf16[256,128]{1,0:T(8,128)(2,1)S(1)}, bf16[256,128]{1,0:T(8,128)(2,1)S(1)}, u32[]{:S(2)}, u32[]{:S(2)}) collective-permute-start(bf16[256,128]{1,0:T(8,128)(2,1)S(1)} %get-tuple-element.34.refs_3_.refs_5_.refs_0_), channel_id=1, source_target_pairs={{0,2},{1,3},{2,0},{3,1},{4,6},{5,7},{6,4},{7,5},{8,10},{9,11},{10,... | collective-permute-start | bytes 196616 | tf_op jit(solution)/shard_map/ppermute | solution.py:312
  9.4 0.0 copy-done
  9.4 0.3 collective-permute-start.5
  9.6 1.1 %shard_map.112 = (f32[8,128]{1,0:T(8,128)S(1)}, bf16[32,4096]{1,0:T(8,128)(2,1)S(1)}) custom-call(f32[32,128]{1,0:T(8,128)} %bitcast.16, bf16[32,4096]{1,0:T(8,128)(2,1)} %bitcast.10), custom_call_target="tpu_custom_call" | custom-call | tf_op jit(solution)/shard_map/pallas_call | solution.py:300
  10.8 1.0 %collective-permute-done.3.refs_6_.refs_8_.refs_3_ = bf16[256,128]{1,0:T(8,128)(2,1)S(1)} collective-permute-done((bf16[256,128]{1,0:T(8,128)(2,1)S(1)}, bf16[256,128]{1,0:T(8,128)(2,1)S(1)}, u32[]{:S(2)}, u32[]{:S(2)}) %collective-permute-start.3) | collective-permute-done | bytes 65568 | tf_op jit(solution)/shard_map/ppermute | solution.py:312
  11.8 2.1 %collective-permute-done.2.refs_5_.refs_7_.refs_2_ = bf16[256,128]{1,0:T(8,128)(2,1)S(1)} collective-permute-done((bf16[256,128]{1,0:T(8,128)(2,1)S(1)}, bf16[256,128]{1,0:T(8,128)(2,1)S(1)}, u32[]{:S(2)}, u32[]{:S(2)}) %collective-permute-start.2) | collective-permute-done | bytes 65568 | tf_op jit(solution)/shard_map/ppermute | solution.py:312
  13.9 0.1 collective-permute-done.1.refs_4_.refs_6_.refs_1_
  14.0 0.0 collective-permute-done.refs_2_.refs_4_
  14.0 0.4 %shard_map.113 = (f32[4,128,256]{2,1,0:T(8,128)S(1)}, f32[4,128,256]{2,1,0:T(8,128)S(1)}, f32[16,256]{1,0:T(8,128)S(1)}) custom-call(f32[8,128]{1,0:T(8,128)S(1)} %get-tuple-element.32.refs_0_, bf16[1024,128]{1,0:T(8,128)(2,1)S(1)} %get-tuple-element.33.refs_1_.refs_3_, bf16[1024,128]{1,0:T(8,128)(2,1)S(1)} %collective-permute-done.refs_2_.refs_4_, ...), custom_call_target="tpu_custom_call" | custom-call | flops 20000000000 | tf_op jit(solution)/shard_map/pallas_call | solution.py:300
  14.4 0.5 %collective-permute-start.4 = (f32[16,256]{1,0:T(8,128)S(1)}, f32[16,256]{1,0:T(8,128)S(1)}, u32[]{:S(2)}, u32[]{:S(2)}) collective-permute-start(f32[16,256]{1,0:T(8,128)S(1)} %get-tuple-element.35.own_ref), channel_id=1, source_target_pairs={{0,1},{1,0},{2,3},{3,2},{4,5},{5,4},{6,7},{7,6},{8,9},{9,8},{10,11... | collective-permute-start | bytes 49160 | tf_op jit(solution)/shard_map/ppermute | solution.py:312
  14.9 2.2 %collective-permute-done.5.input_other_ref = bf16[32,4096]{1,0:T(8,128)(2,1)S(1)} collective-permute-done((bf16[32,4096]{1,0:T(8,128)(2,1)S(1)}, bf16[32,4096]{1,0:T(8,128)(2,1)S(1)}, u32[]{:S(2)}, u32[]{:S(2)}) %collective-permute-start.5) | collective-permute-done | bytes 262176 | tf_op jit(solution)/shard_map/ppermute | solution.py:312
  17.1 1.1 %collective-permute-done.4.other_ref = f32[16,256]{1,0:T(8,128)S(1)} collective-permute-done((f32[16,256]{1,0:T(8,128)S(1)}, f32[16,256]{1,0:T(8,128)S(1)}, u32[]{:S(2)}, u32[]{:S(2)}) %collective-permute-start.4) | collective-permute-done | bytes 16416 | tf_op jit(solution)/shard_map/ppermute | solution.py:312
  18.2 0.2 shard_map.114
  18.4 0.1 collective-permute-start.10
  18.5 1.6 %collective-permute-start.9 = (f32[32,128]{1,0:T(8,128)S(1)}, f32[32,128]{1,0:T(8,128)S(1)}, u32[]{:S(2)}, u32[]{:S(2)}) collective-permute-start(f32[32,128]{1,0:T(8,128)S(1)} %get-tuple-element.48.refs_0_), channel_id=1, source_target_pairs={{0,16},{8,24},{16,0},{24,8},{1,17},{9,25},{17,1},{25,9},{2,18},{10... | collective-permute-start | bytes 49160 | tf_op jit(solution)/shard_map/ppermute | solution.py:312
  20.1 0.3 collective-permute-start.8
  20.4 0.3 shard_map.115
  20.7 1.9 %collective-permute-start.7 = (bf16[256,128]{1,0:T(8,128)(2,1)S(1)}, bf16[256,128]{1,0:T(8,128)(2,1)S(1)}, u32[]{:S(2)}, u32[]{:S(2)}) collective-permute-start(bf16[256,128]{1,0:T(8,128)(2,1)S(1)} %get-tuple-element.43), channel_id=1, source_target_pairs={{0,4},{1,5},{2,6},{3,7},{4,0},{5,1},{6,2},{7,3},{8,12},{9,13},{10,... | collective-permute-start | bytes 196616 | tf_op jit(solution)/shard_map/ppermute | solution.py:312
  22.6 0.3 shard_map.116
  22.8 1.6 %collective-permute-start.6 = (bf16[512,128]{1,0:T(8,128)(2,1)S(1)}, bf16[512,128]{1,0:T(8,128)(2,1)S(1)}, u32[]{:S(2)}, u32[]{:S(2)}) collective-permute-start(bf16[512,128]{1,0:T(8,128)(2,1)S(1)} %get-tuple-element.42), channel_id=1, source_target_pairs={{0,1},{1,0},{2,3},{3,2},{4,5},{5,4},{6,7},{7,6},{8,9},{9,8},{10,11... | collective-permute-start | bytes 393224 | tf_op jit(solution)/shard_map/ppermute | solution.py:312
  24.4 0.0 collective-permute-done.10.refs_3_
  24.4 0.0 collective-permute-done.9.refs_2_
  24.4 0.0 collective-permute-done.8.refs_1_
  24.5 1.4 %collective-permute-start.12 = (bf16[288,128]{1,0:T(8,128)(2,1)S(1)}, bf16[288,128]{1,0:T(8,128)(2,1)S(1)}, u32[]{:S(2)}, u32[]{:S(2)}) collective-permute-start(bf16[288,128]{1,0:T(8,128)(2,1)S(1)} %get-tuple-element.53), channel_id=1, source_target_pairs={{0,6},{1,7},{2,4},{3,5},{4,2},{5,3},{6,0},{7,1},{8,14},{9,15},{10,... | collective-permute-start | bytes 221192 | tf_op jit(solution)/shard_map/ppermute | solution.py:312
  25.9 0.3 collective-permute-start.13
  26.2 2.7 %collective-permute-start.11 = (bf16[32,128]{1,0:T(8,128)(2,1)S(1)}, bf16[32,128]{1,0:T(8,128)(2,1)S(1)}, u32[]{:S(2)}, u32[]{:S(2)}) collective-permute-start(bf16[32,128]{1,0:T(8,128)(2,1)S(1)} %get-tuple-element.52), channel_id=1, source_target_pairs={{0,4},{1,5},{2,6},{3,7},{4,0},{5,1},{6,2},{7,3},{8,12},{9,13},{10,... | collective-permute-start | bytes 24584 | tf_op jit(solution)/shard_map/ppermute | solution.py:312
  28.9 0.0 collective-permute-done.7.far_ref
  28.9 0.0 collective-permute-done.6.other_ref
  28.9 0.8 %shard_map.117 = (bf16[32,2048]{1,0:T(8,128)(2,1)}, f32[64,128]{1,0:T(8,128)S(1)}, f32[256,128]{1,0:T(8,128)S(1)}) custom-call(f32[64,128]{1,0:T(8,128)S(1)} %get-tuple-element.31.trig_ref, f32[512,128]{1,0:T(8,128)S(1)} %get-tuple-element.41.own_ref, bf16[512,128]{1,0:T(8,128)(2,1)S(1)} %collective-permute-done.6.other_ref, ...), custom_call_target="tpu_custom_call" | custom-call | flops 500000000 | tf_op jit(solution)/shard_map/pallas_call | solution.py:300
  29.7 1.6 %collective-permute-done.11.refs_3_ = bf16[32,128]{1,0:T(8,128)(2,1)S(1)} collective-permute-done((bf16[32,128]{1,0:T(8,128)(2,1)S(1)}, bf16[32,128]{1,0:T(8,128)(2,1)S(1)}, u32[]{:S(2)}, u32[]{:S(2)}) %collective-permute-start.11) | collective-permute-done | bytes 8224 | tf_op jit(solution)/shard_map/ppermute | solution.py:312
  31.3 0.0 collective-permute-done.12.refs_4_
  31.3 0.0 collective-permute-done.13.refs_5_
  31.3 0.7 %shard_map.119 = (bf16[32,512]{1,0:T(8,128)(2,1)}, bf16[32,512]{1,0:T(8,128)(2,1)}, f32[32,128]{1,0:T(8,128)}) custom-call(f32[64,128]{1,0:T(8,128)S(1)} %get-tuple-element.46.refs_0_, f32[256,128]{1,0:T(8,128)S(1)} %get-tuple-element.47.refs_1_, f32[32,128]{1,0:T(8,128)S(1)} %get-tuple-element.51.refs_2_, ...), custom_call_target="tpu_custom_call" | custom-call | tf_op jit(solution)/shard_map/pallas_call | solution.py:300
  (1 shorter events, 0.0 us)
Async XLA Ops:
  0.6 8.7 %copy-start = (bf16[1,32,4096]{2,1,0:T(8,128)(2,1)S(1)}, bf16[1,32,4096]{2,1,0:T(8,128)(2,1)}, u32[]{:S(2)}) copy-start(bf16[1,32,4096]{2,1,0:T(8,128)(2,1)} %param.12) | copy-start | bytes 786436
  1.9 12.1 %collective-permute-start = (bf16[1024,128]{1,0:T(8,128)(2,1)S(1)}, bf16[1024,128]{1,0:T(8,128)(2,1)S(1)}, u32[]{:S(2)}, u32[]{:S(2)}) collective-permute-start(bf16[1024,128]{1,0:T(8,128)(2,1)S(1)} %get-tuple-element.33.refs_1_.refs_3_), channel_id=1, source_target_pairs={{0,1},{1,0},{2,3},{3,2},{4,5},{5,4},{6,7},{7,6},{8,9},{9,8},{10,11... | collective-permute-start | bytes 786440 | tf_op jit(solution)/shard_map/ppermute | solution.py:312
  5.0 6.9 %collective-permute-start.3 = (bf16[256,128]{1,0:T(8,128)(2,1)S(1)}, bf16[256,128]{1,0:T(8,128)(2,1)S(1)}, u32[]{:S(2)}, u32[]{:S(2)}) collective-permute-start(bf16[256,128]{1,0:T(8,128)(2,1)S(1)} %get-tuple-element.34.refs_3_.refs_5_.refs_0_), channel_id=1, source_target_pairs={{0,6},{1,7},{2,4},{3,5},{4,2},{5,3},{6,0},{7,1},{8,14},{9,15},{10,... | collective-permute-start | bytes 196616 | tf_op jit(solution)/shard_map/ppermute | solution.py:312
  8.6 5.4 %collective-permute-start.2 = (bf16[256,128]{1,0:T(8,128)(2,1)S(1)}, bf16[256,128]{1,0:T(8,128)(2,1)S(1)}, u32[]{:S(2)}, u32[]{:S(2)}) collective-permute-start(bf16[256,128]{1,0:T(8,128)(2,1)S(1)} %get-tuple-element.34.refs_3_.refs_5_.refs_0_), channel_id=1, source_target_pairs={{0,4},{1,5},{2,6},{3,7},{4,0},{5,1},{6,2},{7,3},{8,12},{9,13},{10,... | collective-permute-start | bytes 196616 | tf_op jit(solution)/shard_map/ppermute | solution.py:312
  8.6 5.4 %collective-permute-start.1 = (bf16[256,128]{1,0:T(8,128)(2,1)S(1)}, bf16[256,128]{1,0:T(8,128)(2,1)S(1)}, u32[]{:S(2)}, u32[]{:S(2)}) collective-permute-start(bf16[256,128]{1,0:T(8,128)(2,1)S(1)} %get-tuple-element.34.refs_3_.refs_5_.refs_0_), channel_id=1, source_target_pairs={{0,2},{1,3},{2,0},{3,1},{4,6},{5,7},{6,4},{7,5},{8,10},{9,11},{10,... | collective-permute-start | bytes 196616 | tf_op jit(solution)/shard_map/ppermute | solution.py:312
  9.4 7.7 %collective-permute-start.5 = (bf16[32,4096]{1,0:T(8,128)(2,1)S(1)}, bf16[32,4096]{1,0:T(8,128)(2,1)S(1)}, u32[]{:S(2)}, u32[]{:S(2)}) collective-permute-start(bf16[32,4096]{1,0:T(8,128)(2,1)S(1)} %bitcast.11), channel_id=1, source_target_pairs={{0,1},{1,0},{2,3},{3,2},{4,5},{5,4},{6,7},{7,6},{8,9},{9,8},{10,11... | collective-permute-start | bytes 786440 | tf_op jit(solution)/shard_map/ppermute | solution.py:312
  14.4 3.8 %collective-permute-start.4 = (f32[16,256]{1,0:T(8,128)S(1)}, f32[16,256]{1,0:T(8,128)S(1)}, u32[]{:S(2)}, u32[]{:S(2)}) collective-permute-start(f32[16,256]{1,0:T(8,128)S(1)} %get-tuple-element.35.own_ref), channel_id=1, source_target_pairs={{0,1},{1,0},{2,3},{3,2},{4,5},{5,4},{6,7},{7,6},{8,9},{9,8},{10,11... | collective-permute-start | bytes 49160 | tf_op jit(solution)/shard_map/ppermute | solution.py:312
  18.4 6.0 %collective-permute-start.10 = (f32[32,128]{1,0:T(8,128)S(1)}, f32[32,128]{1,0:T(8,128)S(1)}, u32[]{:S(2)}, u32[]{:S(2)}) collective-permute-start(f32[32,128]{1,0:T(8,128)S(1)} %get-tuple-element.48.refs_0_), channel_id=1, source_target_pairs={{0,24},{8,16},{16,8},{24,0},{1,25},{9,17},{17,9},{25,1},{2,26},{10... | collective-permute-start | bytes 49160 | tf_op jit(solution)/shard_map/ppermute | solution.py:312
  18.5 5.9 %collective-permute-start.9 = (f32[32,128]{1,0:T(8,128)S(1)}, f32[32,128]{1,0:T(8,128)S(1)}, u32[]{:S(2)}, u32[]{:S(2)}) collective-permute-start(f32[32,128]{1,0:T(8,128)S(1)} %get-tuple-element.48.refs_0_), channel_id=1, source_target_pairs={{0,16},{8,24},{16,0},{24,8},{1,17},{9,25},{17,1},{25,9},{2,18},{10... | collective-permute-start | bytes 49160 | tf_op jit(solution)/shard_map/ppermute | solution.py:312
  20.1 4.4 %collective-permute-start.8 = (f32[32,128]{1,0:T(8,128)S(1)}, f32[32,128]{1,0:T(8,128)S(1)}, u32[]{:S(2)}, u32[]{:S(2)}) collective-permute-start(f32[32,128]{1,0:T(8,128)S(1)} %get-tuple-element.48.refs_0_), channel_id=1, source_target_pairs={{0,8},{8,0},{16,24},{24,16},{1,9},{9,1},{17,25},{25,17},{2,10},{10... | collective-permute-start | bytes 49160 | tf_op jit(solution)/shard_map/ppermute | solution.py:312
  20.7 8.3 %collective-permute-start.7 = (bf16[256,128]{1,0:T(8,128)(2,1)S(1)}, bf16[256,128]{1,0:T(8,128)(2,1)S(1)}, u32[]{:S(2)}, u32[]{:S(2)}) collective-permute-start(bf16[256,128]{1,0:T(8,128)(2,1)S(1)} %get-tuple-element.43), channel_id=1, source_target_pairs={{0,4},{1,5},{2,6},{3,7},{4,0},{5,1},{6,2},{7,3},{8,12},{9,13},{10,... | collective-permute-start | bytes 196616 | tf_op jit(solution)/shard_map/ppermute | solution.py:312
  22.8 6.1 %collective-permute-start.6 = (bf16[512,128]{1,0:T(8,128)(2,1)S(1)}, bf16[512,128]{1,0:T(8,128)(2,1)S(1)}, u32[]{:S(2)}, u32[]{:S(2)}) collective-permute-start(bf16[512,128]{1,0:T(8,128)(2,1)S(1)} %get-tuple-element.42), channel_id=1, source_target_pairs={{0,1},{1,0},{2,3},{3,2},{4,5},{5,4},{6,7},{7,6},{8,9},{9,8},{10,11... | collective-permute-start | bytes 393224 | tf_op jit(solution)/shard_map/ppermute | solution.py:312
  24.5 6.8 %collective-permute-start.12 = (bf16[288,128]{1,0:T(8,128)(2,1)S(1)}, bf16[288,128]{1,0:T(8,128)(2,1)S(1)}, u32[]{:S(2)}, u32[]{:S(2)}) collective-permute-start(bf16[288,128]{1,0:T(8,128)(2,1)S(1)} %get-tuple-element.53), channel_id=1, source_target_pairs={{0,6},{1,7},{2,4},{3,5},{4,2},{5,3},{6,0},{7,1},{8,14},{9,15},{10,... | collective-permute-start | bytes 221192 | tf_op jit(solution)/shard_map/ppermute | solution.py:312
  25.9 5.4 %collective-permute-start.13 = (bf16[288,128]{1,0:T(8,128)(2,1)S(1)}, bf16[288,128]{1,0:T(8,128)(2,1)S(1)}, u32[]{:S(2)}, u32[]{:S(2)}) collective-permute-start(bf16[288,128]{1,0:T(8,128)(2,1)S(1)} %get-tuple-element.54), channel_id=1, source_target_pairs={{0,2},{1,3},{2,0},{3,1},{4,6},{5,7},{6,4},{7,5},{8,10},{9,11},{10,... | collective-permute-start | bytes 221192 | tf_op jit(solution)/shard_map/ppermute | solution.py:312
  26.2 5.1 %collective-permute-start.11 = (bf16[32,128]{1,0:T(8,128)(2,1)S(1)}, bf16[32,128]{1,0:T(8,128)(2,1)S(1)}, u32[]{:S(2)}, u32[]{:S(2)}) collective-permute-start(bf16[32,128]{1,0:T(8,128)(2,1)S(1)} %get-tuple-element.52), channel_id=1, source_target_pairs={{0,4},{1,5},{2,6},{3,7},{4,0},{5,1},{6,2},{7,3},{8,12},{9,13},{10,... | collective-permute-start | bytes 24584 | tf_op jit(solution)/shard_map/ppermute | solution.py:312

commit v11 on v10

--- a/solution.py
+++ b/solution.py
@@ -170,7 +170,9 @@
     )
 
 
-def combine_kernel(own_ref, other_ref, input_ref, input_other_ref, coef_out, router_out):
+def combine_kernel(
+    own_ref, other_ref, input_ref, input_other_ref, coef_out, router_out, send_out
+):
     slots = input_ref.shape[0]
     rows = GROUP * slots
     mine = own_ref[...]
@@ -198,6 +200,7 @@
             axis=0,
             keepdims=True,
         )
+    send_out[...] = router_out[...].astype(jnp.bfloat16)
 
 
 def terms_kernel(slots, half, *refs):
@@ -250,7 +253,7 @@
     router_out, send_out = refs[groups + count : groups + count + 2]
     router = refs[0][...]
     for ref in refs[1:groups]:
-        router += ref[...]
+        router += ref[...].astype(jnp.float32)
     router_out[...] = router
     narrow = router.astype(jnp.bfloat16)
     send_out[...] = narrow
@@ -360,14 +363,12 @@
         [gate, query, query_other, *pairs],
         cost=SCORES_COST,
     )
-    coef, router = call(
+    coef, router, router_send = call(
         combine_kernel,
-        [near((2 * KVH, 2 * rows), f32), near((lines, HD), f32)],
+        [near((2 * KVH, 2 * rows), f32), near((lines, HD), f32), near((lines, HD), bf16)],
         [stats, swap(stats), inputs, inputs_other],
     )
-    routers = [router] + [
-        exchange(router, "dp", step, groups) for step in range(1, groups)
-    ]
+    routers = [router] + [exchange(router_send, "dp", step, groups) for step in range(1, groups)]
     score_grad, term_own, *terms = call(
         functools.partial(terms_kernel, slots, half),
         [near((KVH, half * slots, 2 * rows), bf16), near((2 * KVH * slots, HD), f32)]

time: 32.3 us -> 32.2 us (level)
  no operation moved by 1% of the time
where the time goes in v11:
time: 32.2 us; the launch traced here: 31.9 us
  starting transfers between devices  18.1 us (56%)
  waiting for transfers between devices  8.04 us (25%)
  Pallas kernels  5.13 us (16%)
  between operations  0.71 us (2%)
    ppermute x14, starting transfers between devices, exchange(): return lax.ppermute(array, axis, [(at, at ^ step) for at in range(size)])  18.1 us
    ppermute x14, waiting for transfers between devices, exchange(): return lax.ppermute(array, axis, [(at, at ^ step) for at in range(size)])  8.04 us
    pallas_call x9, Pallas kernels, call(): pl.pallas_call(kernel, out_shape=outs, in_specs=[local] * len(args) + [di...  5.13 us
  transfers between devices with their start and end apart: 14, of which 6 were waited for; matrix products, arithmetic and copies ran while one was open for 0% of the time, Pallas kernels for 9%

profile of v11, /device:TPU:0, one launch (start us, length us, event | category | flops | bytes accessed | tf_op | source)
XLA Modules:
  0.0 31.9 jit_solution(8372904570674445667)
XLA Ops:
  0.6 0.0 copy-start
  0.6 1.3 %shard_map.111 = (bf16[256,128]{1,0:T(8,128)(2,1)S(1)}, bf16[1024,128]{1,0:T(8,128)(2,1)S(1)}, f32[64,128]{1,0:T(8,128)S(1)}) custom-call(s32[1,32]{1,0:T(1,128)} %refs_0_.1, f32[2,128]{1,0:T(2,128)} %constant.2.clone.refs_1_, bf16[32,512]{1,0:T(8,128)(2,1)} %bitcast.14, bf16[32,512]{1,0:T(8,128)(2,1)} %bitcast.15, bf16[32,2048]{1,0:T(8,128)(2,1)} %bitcast.12, ...), custom_call_target="tpu_custom_call" | custom-call | tf_op jit(solution)/shard_map/pallas_call | solution.py:303
  1.9 3.0 %collective-permute-start = (bf16[1024,128]{1,0:T(8,128)(2,1)S(1)}, bf16[1024,128]{1,0:T(8,128)(2,1)S(1)}, u32[]{:S(2)}, u32[]{:S(2)}) collective-permute-start(bf16[1024,128]{1,0:T(8,128)(2,1)S(1)} %get-tuple-element.34.refs_1_.refs_3_), channel_id=1, source_target_pairs={{0,1},{1,0},{2,3},{3,2},{4,5},{5,4},{6,7},{7,6},{8,9},{9,8},{10,11... | collective-permute-start | bytes 786440 | tf_op jit(solution)/shard_map/ppermute | solution.py:315
  5.0 3.6 %collective-permute-start.3 = (bf16[256,128]{1,0:T(8,128)(2,1)S(1)}, bf16[256,128]{1,0:T(8,128)(2,1)S(1)}, u32[]{:S(2)}, u32[]{:S(2)}) collective-permute-start(bf16[256,128]{1,0:T(8,128)(2,1)S(1)} %get-tuple-element.35.refs_3_.refs_5_.refs_0_), channel_id=1, source_target_pairs={{0,6},{1,7},{2,4},{3,5},{4,2},{5,3},{6,0},{7,1},{8,14},{9,15},{10,... | collective-permute-start | bytes 196616 | tf_op jit(solution)/shard_map/ppermute | solution.py:315
  8.6 0.0 collective-permute-start.2
  8.6 0.8 %collective-permute-start.1 = (bf16[256,128]{1,0:T(8,128)(2,1)S(1)}, bf16[256,128]{1,0:T(8,128)(2,1)S(1)}, u32[]{:S(2)}, u32[]{:S(2)}) collective-permute-start(bf16[256,128]{1,0:T(8,128)(2,1)S(1)} %get-tuple-element.35.refs_3_.refs_5_.refs_0_), channel_id=1, source_target_pairs={{0,2},{1,3},{2,0},{3,1},{4,6},{5,7},{6,4},{7,5},{8,10},{9,11},{10,... | collective-permute-start | bytes 196616 | tf_op jit(solution)/shard_map/ppermute | solution.py:315
  9.4 0.0 copy-done
  9.4 0.3 collective-permute-start.5
  9.6 1.1 %shard_map.112 = (f32[8,128]{1,0:T(8,128)S(1)}, bf16[32,4096]{1,0:T(8,128)(2,1)S(1)}) custom-call(f32[32,128]{1,0:T(8,128)} %bitcast.16, bf16[32,4096]{1,0:T(8,128)(2,1)} %bitcast.10), custom_call_target="tpu_custom_call" | custom-call | tf_op jit(solution)/shard_map/pallas_call | solution.py:303
  10.8 1.0 %collective-permute-done.3.refs_6_.refs_8_.refs_3_ = bf16[256,128]{1,0:T(8,128)(2,1)S(1)} collective-permute-done((bf16[256,128]{1,0:T(8,128)(2,1)S(1)}, bf16[256,128]{1,0:T(8,128)(2,1)S(1)}, u32[]{:S(2)}, u32[]{:S(2)}) %collective-permute-start.3) | collective-permute-done | bytes 65568 | tf_op jit(solution)/shard_map/ppermute | solution.py:315
  11.8 2.1 %collective-permute-done.2.refs_5_.refs_7_.refs_2_ = bf16[256,128]{1,0:T(8,128)(2,1)S(1)} collective-permute-done((bf16[256,128]{1,0:T(8,128)(2,1)S(1)}, bf16[256,128]{1,0:T(8,128)(2,1)S(1)}, u32[]{:S(2)}, u32[]{:S(2)}) %collective-permute-start.2) | collective-permute-done | bytes 65568 | tf_op jit(solution)/shard_map/ppermute | solution.py:315
  13.9 0.1 collective-permute-done.1.refs_4_.refs_6_.refs_1_
  14.0 0.0 collective-permute-done.refs_2_.refs_4_
  14.0 0.4 %shard_map.113 = (f32[4,128,256]{2,1,0:T(8,128)S(1)}, f32[4,128,256]{2,1,0:T(8,128)S(1)}, f32[16,256]{1,0:T(8,128)S(1)}) custom-call(f32[8,128]{1,0:T(8,128)S(1)} %get-tuple-element.33.refs_0_, bf16[1024,128]{1,0:T(8,128)(2,1)S(1)} %get-tuple-element.34.refs_1_.refs_3_, bf16[1024,128]{1,0:T(8,128)(2,1)S(1)} %collective-permute-done.refs_2_.refs_4_, ...), custom_call_target="tpu_custom_call" | custom-call | flops 20000000000 | tf_op jit(solution)/shard_map/pallas_call | solution.py:303
  14.4 0.5 %collective-permute-start.4 = (f32[16,256]{1,0:T(8,128)S(1)}, f32[16,256]{1,0:T(8,128)S(1)}, u32[]{:S(2)}, u32[]{:S(2)}) collective-permute-start(f32[16,256]{1,0:T(8,128)S(1)} %get-tuple-element.36.own_ref), channel_id=1, source_target_pairs={{0,1},{1,0},{2,3},{3,2},{4,5},{5,4},{6,7},{7,6},{8,9},{9,8},{10,11... | collective-permute-start | bytes 49160 | tf_op jit(solution)/shard_map/ppermute | solution.py:315
  14.9 2.2 %collective-permute-done.5.input_other_ref = bf16[32,4096]{1,0:T(8,128)(2,1)S(1)} collective-permute-done((bf16[32,4096]{1,0:T(8,128)(2,1)S(1)}, bf16[32,4096]{1,0:T(8,128)(2,1)S(1)}, u32[]{:S(2)}, u32[]{:S(2)}) %collective-permute-start.5) | collective-permute-done | bytes 262176 | tf_op jit(solution)/shard_map/ppermute | solution.py:315
  17.1 1.1 %collective-permute-done.4.other_ref = f32[16,256]{1,0:T(8,128)S(1)} collective-permute-done((f32[16,256]{1,0:T(8,128)S(1)}, f32[16,256]{1,0:T(8,128)S(1)}, u32[]{:S(2)}, u32[]{:S(2)}) %collective-permute-start.4) | collective-permute-done | bytes 16416 | tf_op jit(solution)/shard_map/ppermute | solution.py:315
  18.2 0.2 shard_map.114
  18.4 0.1 collective-permute-start.10
  18.5 1.6 %collective-permute-start.9 = (bf16[32,128]{1,0:T(8,128)(2,1)S(1)}, bf16[32,128]{1,0:T(8,128)(2,1)S(1)}, u32[]{:S(2)}, u32[]{:S(2)}) collective-permute-start(bf16[32,128]{1,0:T(8,128)(2,1)S(1)} %get-tuple-element.50), channel_id=1, source_target_pairs={{0,16},{8,24},{16,0},{24,8},{1,17},{9,25},{17,1},{25,9},{2,18},{10... | collective-permute-start | bytes 24584 | tf_op jit(solution)/shard_map/ppermute | solution.py:315
  20.1 0.3 collective-permute-start.8
  20.4 0.3 shard_map.115
  20.7 1.9 %collective-permute-start.7 = (bf16[256,128]{1,0:T(8,128)(2,1)S(1)}, bf16[256,128]{1,0:T(8,128)(2,1)S(1)}, u32[]{:S(2)}, u32[]{:S(2)}) collective-permute-start(bf16[256,128]{1,0:T(8,128)(2,1)S(1)} %get-tuple-element.44), channel_id=1, source_target_pairs={{0,4},{1,5},{2,6},{3,7},{4,0},{5,1},{6,2},{7,3},{8,12},{9,13},{10,... | collective-permute-start | bytes 196616 | tf_op jit(solution)/shard_map/ppermute | solution.py:315
  22.6 0.3 shard_map.116
  22.8 1.6 %collective-permute-start.6 = (bf16[512,128]{1,0:T(8,128)(2,1)S(1)}, bf16[512,128]{1,0:T(8,128)(2,1)S(1)}, u32[]{:S(2)}, u32[]{:S(2)}) collective-permute-start(bf16[512,128]{1,0:T(8,128)(2,1)S(1)} %get-tuple-element.43), channel_id=1, source_target_pairs={{0,1},{1,0},{2,3},{3,2},{4,5},{5,4},{6,7},{7,6},{8,9},{9,8},{10,11... | collective-permute-start | bytes 393224 | tf_op jit(solution)/shard_map/ppermute | solution.py:315
  24.4 0.0 collective-permute-done.10.refs_3_
  24.4 0.0 collective-permute-done.9.refs_2_
  24.4 0.0 collective-permute-done.8.refs_1_
  24.5 1.4 %collective-permute-start.12 = (bf16[288,128]{1,0:T(8,128)(2,1)S(1)}, bf16[288,128]{1,0:T(8,128)(2,1)S(1)}, u32[]{:S(2)}, u32[]{:S(2)}) collective-permute-start(bf16[288,128]{1,0:T(8,128)(2,1)S(1)} %get-tuple-element.55), channel_id=1, source_target_pairs={{0,6},{1,7},{2,4},{3,5},{4,2},{5,3},{6,0},{7,1},{8,14},{9,15},{10,... | collective-permute-start | bytes 221192 | tf_op jit(solution)/shard_map/ppermute | solution.py:315
  25.9 0.3 collective-permute-start.13
  26.2 2.7 %collective-permute-start.11 = (bf16[32,128]{1,0:T(8,128)(2,1)S(1)}, bf16[32,128]{1,0:T(8,128)(2,1)S(1)}, u32[]{:S(2)}, u32[]{:S(2)}) collective-permute-start(bf16[32,128]{1,0:T(8,128)(2,1)S(1)} %get-tuple-element.54), channel_id=1, source_target_pairs={{0,4},{1,5},{2,6},{3,7},{4,0},{5,1},{6,2},{7,3},{8,12},{9,13},{10,... | collective-permute-start | bytes 24584 | tf_op jit(solution)/shard_map/ppermute | solution.py:315
  28.9 0.0 collective-permute-done.7.far_ref
  28.9 0.0 collective-permute-done.6.other_ref
  28.9 0.8 %shard_map.117 = (bf16[32,2048]{1,0:T(8,128)(2,1)}, f32[64,128]{1,0:T(8,128)S(1)}, f32[256,128]{1,0:T(8,128)S(1)}) custom-call(f32[64,128]{1,0:T(8,128)S(1)} %get-tuple-element.32.trig_ref, f32[512,128]{1,0:T(8,128)S(1)} %get-tuple-element.42.own_ref, bf16[512,128]{1,0:T(8,128)(2,1)S(1)} %collective-permute-done.6.other_ref, ...), custom_call_target="tpu_custom_call" | custom-call | flops 500000000 | tf_op jit(solution)/shard_map/pallas_call | solution.py:303
  29.7 1.5 %collective-permute-done.11.refs_3_ = bf16[32,128]{1,0:T(8,128)(2,1)S(1)} collective-permute-done((bf16[32,128]{1,0:T(8,128)(2,1)S(1)}, bf16[32,128]{1,0:T(8,128)(2,1)S(1)}, u32[]{:S(2)}, u32[]{:S(2)}) %collective-permute-start.11) | collective-permute-done | bytes 8224 | tf_op jit(solution)/shard_map/ppermute | solution.py:315
  31.2 0.0 collective-permute-done.12.refs_4_
  31.2 0.0 collective-permute-done.13.refs_5_
  31.2 0.7 %shard_map.119 = (bf16[32,512]{1,0:T(8,128)(2,1)}, bf16[32,512]{1,0:T(8,128)(2,1)}, f32[32,128]{1,0:T(8,128)}) custom-call(f32[64,128]{1,0:T(8,128)S(1)} %get-tuple-element.47.refs_0_, f32[256,128]{1,0:T(8,128)S(1)} %get-tuple-element.48.refs_1_, f32[32,128]{1,0:T(8,128)S(1)} %get-tuple-element.53.refs_2_, ...), custom_call_target="tpu_custom_call" | custom-call | tf_op jit(solution)/shard_map/pallas_call | solution.py:303
  (1 shorter events, 0.0 us)
Async XLA Ops:
  0.6 8.7 %copy-start = (bf16[1,32,4096]{2,1,0:T(8,128)(2,1)S(1)}, bf16[1,32,4096]{2,1,0:T(8,128)(2,1)}, u32[]{:S(2)}) copy-start(bf16[1,32,4096]{2,1,0:T(8,128)(2,1)} %param.12) | copy-start | bytes 786436
  1.9 12.1 %collective-permute-start = (bf16[1024,128]{1,0:T(8,128)(2,1)S(1)}, bf16[1024,128]{1,0:T(8,128)(2,1)S(1)}, u32[]{:S(2)}, u32[]{:S(2)}) collective-permute-start(bf16[1024,128]{1,0:T(8,128)(2,1)S(1)} %get-tuple-element.34.refs_1_.refs_3_), channel_id=1, source_target_pairs={{0,1},{1,0},{2,3},{3,2},{4,5},{5,4},{6,7},{7,6},{8,9},{9,8},{10,11... | collective-permute-start | bytes 786440 | tf_op jit(solution)/shard_map/ppermute | solution.py:315
  5.0 6.9 %collective-permute-start.3 = (bf16[256,128]{1,0:T(8,128)(2,1)S(1)}, bf16[256,128]{1,0:T(8,128)(2,1)S(1)}, u32[]{:S(2)}, u32[]{:S(2)}) collective-permute-start(bf16[256,128]{1,0:T(8,128)(2,1)S(1)} %get-tuple-element.35.refs_3_.refs_5_.refs_0_), channel_id=1, source_target_pairs={{0,6},{1,7},{2,4},{3,5},{4,2},{5,3},{6,0},{7,1},{8,14},{9,15},{10,... | collective-permute-start | bytes 196616 | tf_op jit(solution)/shard_map/ppermute | solution.py:315
  8.6 5.4 %collective-permute-start.2 = (bf16[256,128]{1,0:T(8,128)(2,1)S(1)}, bf16[256,128]{1,0:T(8,128)(2,1)S(1)}, u32[]{:S(2)}, u32[]{:S(2)}) collective-permute-start(bf16[256,128]{1,0:T(8,128)(2,1)S(1)} %get-tuple-element.35.refs_3_.refs_5_.refs_0_), channel_id=1, source_target_pairs={{0,4},{1,5},{2,6},{3,7},{4,0},{5,1},{6,2},{7,3},{8,12},{9,13},{10,... | collective-permute-start | bytes 196616 | tf_op jit(solution)/shard_map/ppermute | solution.py:315
  8.6 5.4 %collective-permute-start.1 = (bf16[256,128]{1,0:T(8,128)(2,1)S(1)}, bf16[256,128]{1,0:T(8,128)(2,1)S(1)}, u32[]{:S(2)}, u32[]{:S(2)}) collective-permute-start(bf16[256,128]{1,0:T(8,128)(2,1)S(1)} %get-tuple-element.35.refs_3_.refs_5_.refs_0_), channel_id=1, source_target_pairs={{0,2},{1,3},{2,0},{3,1},{4,6},{5,7},{6,4},{7,5},{8,10},{9,11},{10,... | collective-permute-start | bytes 196616 | tf_op jit(solution)/shard_map/ppermute | solution.py:315
  9.4 7.7 %collective-permute-start.5 = (bf16[32,4096]{1,0:T(8,128)(2,1)S(1)}, bf16[32,4096]{1,0:T(8,128)(2,1)S(1)}, u32[]{:S(2)}, u32[]{:S(2)}) collective-permute-start(bf16[32,4096]{1,0:T(8,128)(2,1)S(1)} %bitcast.11), channel_id=1, source_target_pairs={{0,1},{1,0},{2,3},{3,2},{4,5},{5,4},{6,7},{7,6},{8,9},{9,8},{10,11... | collective-permute-start | bytes 786440 | tf_op jit(solution)/shard_map/ppermute | solution.py:315
  14.4 3.8 %collective-permute-start.4 = (f32[16,256]{1,0:T(8,128)S(1)}, f32[16,256]{1,0:T(8,128)S(1)}, u32[]{:S(2)}, u32[]{:S(2)}) collective-permute-start(f32[16,256]{1,0:T(8,128)S(1)} %get-tuple-element.36.own_ref), channel_id=1, source_target_pairs={{0,1},{1,0},{2,3},{3,2},{4,5},{5,4},{6,7},{7,6},{8,9},{9,8},{10,11... | collective-permute-start | bytes 49160 | tf_op jit(solution)/shard_map/ppermute | solution.py:315
  18.4 6.0 %collective-permute-start.10 = (bf16[32,128]{1,0:T(8,128)(2,1)S(1)}, bf16[32,128]{1,0:T(8,128)(2,1)S(1)}, u32[]{:S(2)}, u32[]{:S(2)}) collective-permute-start(bf16[32,128]{1,0:T(8,128)(2,1)S(1)} %get-tuple-element.50), channel_id=1, source_target_pairs={{0,24},{8,16},{16,8},{24,0},{1,25},{9,17},{17,9},{25,1},{2,26},{10... | collective-permute-start | bytes 24584 | tf_op jit(solution)/shard_map/ppermute | solution.py:315
  18.5 5.9 %collective-permute-start.9 = (bf16[32,128]{1,0:T(8,128)(2,1)S(1)}, bf16[32,128]{1,0:T(8,128)(2,1)S(1)}, u32[]{:S(2)}, u32[]{:S(2)}) collective-permute-start(bf16[32,128]{1,0:T(8,128)(2,1)S(1)} %get-tuple-element.50), channel_id=1, source_target_pairs={{0,16},{8,24},{16,0},{24,8},{1,17},{9,25},{17,1},{25,9},{2,18},{10... | collective-permute-start | bytes 24584 | tf_op jit(solution)/shard_map/ppermute | solution.py:315
  20.1 4.4 %collective-permute-start.8 = (bf16[32,128]{1,0:T(8,128)(2,1)S(1)}, bf16[32,128]{1,0:T(8,128)(2,1)S(1)}, u32[]{:S(2)}, u32[]{:S(2)}) collective-permute-start(bf16[32,128]{1,0:T(8,128)(2,1)S(1)} %get-tuple-element.50), channel_id=1, source_target_pairs={{0,8},{8,0},{16,24},{24,16},{1,9},{9,1},{17,25},{25,17},{2,10},{10... | collective-permute-start | bytes 24584 | tf_op jit(solution)/shard_map/ppermute | solution.py:315
  20.7 8.3 %collective-permute-start.7 = (bf16[256,128]{1,0:T(8,128)(2,1)S(1)}, bf16[256,128]{1,0:T(8,128)(2,1)S(1)}, u32[]{:S(2)}, u32[]{:S(2)}) collective-permute-start(bf16[256,128]{1,0:T(8,128)(2,1)S(1)} %get-tuple-element.44), channel_id=1, source_target_pairs={{0,4},{1,5},{2,6},{3,7},{4,0},{5,1},{6,2},{7,3},{8,12},{9,13},{10,... | collective-permute-start | bytes 196616 | tf_op jit(solution)/shard_map/ppermute | solution.py:315
  22.8 6.1 %collective-permute-start.6 = (bf16[512,128]{1,0:T(8,128)(2,1)S(1)}, bf16[512,128]{1,0:T(8,128)(2,1)S(1)}, u32[]{:S(2)}, u32[]{:S(2)}) collective-permute-start(bf16[512,128]{1,0:T(8,128)(2,1)S(1)} %get-tuple-element.43), channel_id=1, source_target_pairs={{0,1},{1,0},{2,3},{3,2},{4,5},{5,4},{6,7},{7,6},{8,9},{9,8},{10,11... | collective-permute-start | bytes 393224 | tf_op jit(solution)/shard_map/ppermute | solution.py:315
  24.5 6.8 %collective-permute-start.12 = (bf16[288,128]{1,0:T(8,128)(2,1)S(1)}, bf16[288,128]{1,0:T(8,128)(2,1)S(1)}, u32[]{:S(2)}, u32[]{:S(2)}) collective-permute-start(bf16[288,128]{1,0:T(8,128)(2,1)S(1)} %get-tuple-element.55), channel_id=1, source_target_pairs={{0,6},{1,7},{2,4},{3,5},{4,2},{5,3},{6,0},{7,1},{8,14},{9,15},{10,... | collective-permute-start | bytes 221192 | tf_op jit(solution)/shard_map/ppermute | solution.py:315
  25.9 5.3 %collective-permute-start.13 = (bf16[288,128]{1,0:T(8,128)(2,1)S(1)}, bf16[288,128]{1,0:T(8,128)(2,1)S(1)}, u32[]{:S(2)}, u32[]{:S(2)}) collective-permute-start(bf16[288,128]{1,0:T(8,128)(2,1)S(1)} %get-tuple-element.56), channel_id=1, source_target_pairs={{0,2},{1,3},{2,0},{3,1},{4,6},{5,7},{6,4},{7,5},{8,10},{9,11},{10,... | collective-permute-start | bytes 221192 | tf_op jit(solution)/shard_map/ppermute | solution.py:315
  26.2 5.0 %collective-permute-start.11 = (bf16[32,128]{1,0:T(8,128)(2,1)S(1)}, bf16[32,128]{1,0:T(8,128)(2,1)S(1)}, u32[]{:S(2)}, u32[]{:S(2)}) collective-permute-start(bf16[32,128]{1,0:T(8,128)(2,1)S(1)} %get-tuple-element.54), channel_id=1, source_target_pairs={{0,4},{1,5},{2,6},{3,7},{4,0},{5,1},{6,2},{7,3},{8,12},{9,13},{10,... | collective-permute-start | bytes 24584 | tf_op jit(solution)/shard_map/ppermute | solution.py:315
